TPU v7x, 32 devices: a whole 2x2x4 slice. The times are simulated.
32 devices in a mesh: dp: 2 (over x), ctx: 4 (over y, core), tensor: 4 (over z).
Axes of the slice: x: 2, y: 2, z: 4, core: 2. Of those that a mesh axis runs over, the one named last changes fastest.
Arguments:
- tokens: bfloat16 [32, 1024, 1024], P('dp', 'ctx'), may hold values from -6 to 6
- segment_ids: int32 [32, 1024], P('dp', 'ctx'), may hold values from 0 to 3, as said below
- norm1_gain: bfloat16 [1024], P(('dp', 'ctx')), may hold values from 0.5 to 1.5
- norm1_shift: bfloat16 [1024], P(('dp', 'ctx')), may hold values from -1.75 to 1.75
- w_query: bfloat16 [1024, 1024], P(('dp', 'ctx'), 'tensor'), may hold values from -0.1875 to 0.1875
- w_key: bfloat16 [1024, 1024], P(('dp', 'ctx'), 'tensor'), may hold values from -0.1875 to 0.1875
- w_value: bfloat16 [1024, 1024], P(('dp', 'ctx'), 'tensor'), may hold values from -0.1875 to 0.1875
- query_bias: bfloat16 [16, 64], P('tensor', ('dp', 'ctx')), may hold values from -1.75 to 1.75
- value_bias: bfloat16 [16, 64], P('tensor', ('dp', 'ctx')), may hold values from -1.75 to 1.75
- w_out: bfloat16 [1024, 1024], P('tensor', ('dp', 'ctx')), may hold values from -0.75 to 0.75
- out_bias: bfloat16 [1024], P(('dp', 'ctx')), may hold values from -1.75 to 1.75
- norm2_gain: bfloat16 [1024], P(('dp', 'ctx')), may hold values from 0.5 to 1.5
- norm2_shift: bfloat16 [1024], P(('dp', 'ctx')), may hold values from -1.75 to 1.75
- w_up: bfloat16 [1024, 4096], P(('dp', 'ctx'), 'tensor'), may hold values from -0.1875 to 0.1875
- up_bias: bfloat16 [16, 256], P('tensor', ('dp', 'ctx')), may hold values from -1.75 to 1.75
- w_down: bfloat16 [4096, 1024], P('tensor', ('dp', 'ctx')), may hold values from -0.1875 to 0.1875
- down_bias: bfloat16 [1024], P(('dp', 'ctx')), may hold values from -1.75 to 1.75
- out_grad: bfloat16 [32, 1024, 1024], P('dp', 'ctx'), may hold values from -6 to 6
Outputs:
- outputs: bfloat16 [32, 1024, 1024], P('dp', 'ctx')
- tokens_grad: bfloat16 [32, 1024, 1024], P('dp', 'ctx')
- norm1_gain_grad: float32 [1024], P(('dp', 'ctx'))
- norm1_shift_grad: float32 [1024], P(('dp', 'ctx'))
- w_query_grad: float32 [1024, 1024], P(('dp', 'ctx'), 'tensor')
- w_key_grad: float32 [1024, 1024], P(('dp', 'ctx'), 'tensor')
- w_value_grad: float32 [1024, 1024], P(('dp', 'ctx'), 'tensor')
- query_bias_grad: float32 [16, 64], P('tensor', ('dp', 'ctx'))
- value_bias_grad: float32 [16, 64], P('tensor', ('dp', 'ctx'))
- w_out_grad: float32 [1024, 1024], P('tensor', ('dp', 'ctx'))
- out_bias_grad: float32 [1024], P(('dp', 'ctx'))
- norm2_gain_grad: float32 [1024], P(('dp', 'ctx'))
- norm2_shift_grad: float32 [1024], P(('dp', 'ctx'))
- w_up_grad: float32 [1024, 4096], P(('dp', 'ctx'), 'tensor')
- up_bias_grad: float32 [16, 256], P('tensor', ('dp', 'ctx'))
- w_down_grad: float32 [4096, 1024], P('tensor', ('dp', 'ctx'))
- down_bias_grad: float32 [1024], P(('dp', 'ctx'))
Inputs may be any that keep to these rules, and one draw needn't show every extreme that they name: `segment_ids`: ids start at 0 and never fall along a sequence. In each group of 16 sequences one (drawn) is a single document; every other sequence holds exactly four documents of 200 tokens or more each.
All inputs are finite; a program needn't handle non-finite values.
Results may differ from a plain program's by a relative error of at most 0.017.
Values may be sent and summed in bfloat16 or wider, within the bound.
A program may use at most 384 MiB of HBM per device.

v0:
```python
import functools
import math

import jax
import jax.numpy as jnp
from jax import lax
from jax.experimental import pallas as pl
from jax.experimental.pallas import tpu as pltpu
from jax.sharding import PartitionSpec as P

HEADS = 16
MICRO = 2
HEAD_DIM = 64


EPSILON = 1e-05


def layer_norm(values, gain, shift):
    centre = values - jnp.mean(values, axis=-1, keepdims=True)
    spread = jnp.mean(centre * centre, axis=-1, keepdims=True)
    return centre * lax.rsqrt(spread + EPSILON) * gain + shift


def gelu_tanh(values):
    return (
        0.5
        * values
        * (1.0 + jnp.tanh(0.7978845608028654 * (values + 0.044715 * values * values * values)))
    )


def matmul(left, right):
    return jnp.dot(left, right, preferred_element_type=jnp.float32)


def matmul_left(left, right):
    return lax.dot_general(
        left, right, (((0,), (0,)), ((), ())), preferred_element_type=jnp.float32
    )


def matmul_right(left, right):
    return lax.dot_general(
        left, right, (((1,), (1,)), ((), ())), preferred_element_type=jnp.float32
    )


def full_total(partial_value):
    return lax.psum(partial_value, "tensor")


def scores_of(query_heads, key_heads, query_seg, key_seg, slopes, query_first):
    query_count = query_heads.shape[1]
    key_count = key_heads.shape[1]
    head_width = query_heads.shape[3]
    raw_scores = jnp.einsum(
        "bqhd,bkhd->bhqk", query_heads, key_heads, preferred_element_type=jnp.float32
    )
    query_place = query_first + jnp.arange(query_count)
    key_place = jnp.arange(key_count)
    offsets = (key_place[None, :] - query_place[:, None]).astype(jnp.float32)
    scores = (
        raw_scores * (1.0 / math.sqrt(head_width))
        + slopes[None, :, None, None] * offsets[None, None]
    )
    causal = (key_place[None, :] <= query_place[:, None])[None, None]
    same_doc = query_seg[:, None, :, None] == key_seg[:, None, None, :]
    return jnp.where(causal & same_doc, scores, -1e30)


def shards(
    tokens,
    segment_ids,
    norm1_gain,
    norm1_shift,
    w_query,
    w_key,
    w_value,
    query_bias,
    value_bias,
    w_out,
    out_bias,
    norm2_gain,
    norm2_shift,
    w_up,
    up_bias,
    w_down,
    down_bias,
    out_grad,
):
    seqs_local, span_len, model_width = tokens.shape
    micro_seqs = seqs_local // MICRO
    row_count = micro_seqs * span_len
    heads_local = query_bias.shape[0]
    cols_local = heads_local * HEAD_DIM
    ff_local = w_up.shape[1]
    length_all = span_len * lax.axis_size("ctx")
    span_first = lax.axis_index("ctx") * span_len
    head_global = lax.axis_index("tensor") * heads_local + jnp.arange(heads_local)
    slopes = jnp.exp2(-8.0 * (head_global + 1).astype(jnp.float32) / HEADS)
    scale = 1.0 / math.sqrt(HEAD_DIM)
    grad_query = jnp.zeros((model_width, cols_local), jnp.float32)
    grad_key = jnp.zeros((model_width, cols_local), jnp.float32)
    grad_value = jnp.zeros((model_width, cols_local), jnp.float32)
    grad_qbias = jnp.zeros((heads_local, HEAD_DIM), jnp.float32)
    grad_vbias = jnp.zeros((heads_local, HEAD_DIM), jnp.float32)
    grad_wout = jnp.zeros((cols_local, model_width), jnp.float32)
    grad_small = jnp.zeros((6, model_width), jnp.float32)
    grad_up = jnp.zeros((model_width, ff_local), jnp.float32)
    grad_ubias = jnp.zeros((heads_local, ff_local // heads_local), jnp.float32)
    grad_down = jnp.zeros((ff_local, model_width), jnp.float32)
    outputs_list = []
    inputs_grad_list = []
    for micro_index in range(MICRO):
        first = micro_index * micro_seqs
        inputs = (
            tokens[first : first + micro_seqs].reshape(row_count, model_width).astype(jnp.float32)
        )
        query_seg = segment_ids[first : first + micro_seqs]
        cotangent = out_grad[first : first + micro_seqs].reshape(row_count, model_width)
        weights = (
            lax.all_gather(norm1_gain, ("dp", "ctx"), axis=0, tiled=True),
            lax.all_gather(norm1_shift, ("dp", "ctx"), axis=0, tiled=True),
            lax.all_gather(w_query, ("dp", "ctx"), axis=0, tiled=True),
            lax.all_gather(w_key, ("dp", "ctx"), axis=0, tiled=True),
            lax.all_gather(w_value, ("dp", "ctx"), axis=0, tiled=True),
            lax.all_gather(query_bias, ("dp", "ctx"), axis=1, tiled=True),
            lax.all_gather(value_bias, ("dp", "ctx"), axis=1, tiled=True),
            lax.all_gather(w_out, ("dp", "ctx"), axis=1, tiled=True),
            lax.all_gather(out_bias, ("dp", "ctx"), axis=0, tiled=True),
            lax.all_gather(norm2_gain, ("dp", "ctx"), axis=0, tiled=True),
            lax.all_gather(norm2_shift, ("dp", "ctx"), axis=0, tiled=True),
            lax.all_gather(w_up, ("dp", "ctx"), axis=0, tiled=True),
            lax.all_gather(up_bias, ("dp", "ctx"), axis=1, tiled=True),
            lax.all_gather(w_down, ("dp", "ctx"), axis=1, tiled=True),
            lax.all_gather(down_bias, ("dp", "ctx"), axis=0, tiled=True),
        )
        (
            gain_one,
            shift_one,
            full_query,
            full_key,
            full_value,
            bias_query,
            bias_value,
            full_out,
            bias_out,
            gain_two,
            shift_two,
            full_up,
            bias_up,
            full_down,
            bias_down,
        ) = weights
        gain_one = gain_one.astype(jnp.float32)
        shift_one = shift_one.astype(jnp.float32)
        gain_two = gain_two.astype(jnp.float32)
        shift_two = shift_two.astype(jnp.float32)
        bias_out = bias_out.astype(jnp.float32)
        bias_down = bias_down.astype(jnp.float32)
        normed_one = layer_norm(inputs, gain_one, shift_one).astype(jnp.bfloat16)
        queries = (
            matmul(normed_one, full_query) + bias_query.reshape(-1).astype(jnp.float32)
        ).astype(jnp.bfloat16)
        key_rows = matmul(normed_one, full_key).astype(jnp.bfloat16)
        value_rows = (
            matmul(normed_one, full_value) + bias_value.reshape(-1).astype(jnp.float32)
        ).astype(jnp.bfloat16)
        local_pairs = jnp.concatenate([key_rows, value_rows], axis=1).reshape(
            micro_seqs, span_len, 2 * cols_local
        )
        pairs_all, key_seg = (
            lax.all_gather(local_pairs, "ctx", axis=1, tiled=True),
            lax.all_gather(query_seg.astype(jnp.bfloat16), "ctx", axis=1, tiled=True),
        )
        key_seg = key_seg.astype(jnp.float32)
        query_segf = query_seg.astype(jnp.float32)
        key_heads = pairs_all[:, :, :cols_local].reshape(
            micro_seqs, length_all, heads_local, HEAD_DIM
        )
        value_heads = pairs_all[:, :, cols_local:].reshape(
            micro_seqs, length_all, heads_local, HEAD_DIM
        )
        query_heads = queries.reshape(micro_seqs, span_len, heads_local, HEAD_DIM)
        scores = scores_of(query_heads, key_heads, query_segf, key_seg, slopes, span_first)
        highest = jnp.max(scores, axis=-1, keepdims=True)
        exponent = jnp.exp(scores - highest)
        totals = jnp.sum(exponent, axis=-1, keepdims=True)
        softmaxed = exponent / totals
        log_total = highest + jnp.log(totals)
        mixed_heads = jnp.einsum(
            "bhqk,bkhd->bqhd",
            softmaxed.astype(jnp.bfloat16),
            value_heads,
            preferred_element_type=jnp.float32,
        )
        mixed_low = mixed_heads.reshape(row_count, cols_local).astype(jnp.bfloat16)
        attn_part = matmul(mixed_low, full_out)
        residual = inputs + full_total(attn_part) + bias_out
        normed_two = layer_norm(residual, gain_two, shift_two).astype(jnp.bfloat16)
        pre_act = matmul(normed_two, full_up) + bias_up.reshape(-1).astype(jnp.float32)
        activated = gelu_tanh(pre_act).astype(jnp.bfloat16)
        mlp_part = matmul(activated, full_down)
        result_rows = (residual + full_total(mlp_part) + bias_down).astype(jnp.bfloat16)
        outputs_list.append(result_rows.reshape(micro_seqs, span_len, model_width))
        weights_back = (
            lax.all_gather(norm1_gain, ("dp", "ctx"), axis=0, tiled=True),
            lax.all_gather(norm1_shift, ("dp", "ctx"), axis=0, tiled=True),
            lax.all_gather(w_query, ("dp", "ctx"), axis=0, tiled=True),
            lax.all_gather(w_key, ("dp", "ctx"), axis=0, tiled=True),
            lax.all_gather(w_value, ("dp", "ctx"), axis=0, tiled=True),
            lax.all_gather(query_bias, ("dp", "ctx"), axis=1, tiled=True),
            lax.all_gather(value_bias, ("dp", "ctx"), axis=1, tiled=True),
            lax.all_gather(w_out, ("dp", "ctx"), axis=1, tiled=True),
            lax.all_gather(out_bias, ("dp", "ctx"), axis=0, tiled=True),
            lax.all_gather(norm2_gain, ("dp", "ctx"), axis=0, tiled=True),
            lax.all_gather(norm2_shift, ("dp", "ctx"), axis=0, tiled=True),
            lax.all_gather(w_up, ("dp", "ctx"), axis=0, tiled=True),
            lax.all_gather(up_bias, ("dp", "ctx"), axis=1, tiled=True),
            lax.all_gather(w_down, ("dp", "ctx"), axis=1, tiled=True),
            lax.all_gather(down_bias, ("dp", "ctx"), axis=0, tiled=True),
        )
        back_query = weights_back[2]
        back_key = weights_back[3]
        back_value = weights_back[4]
        back_out = weights_back[7]
        back_up = weights_back[11]
        back_down = weights_back[13]
        gain_one = weights_back[0].astype(jnp.float32)
        shift_one = weights_back[1].astype(jnp.float32)
        gain_two = weights_back[9].astype(jnp.float32)
        shift_two = weights_back[10].astype(jnp.float32)
        act_grad = matmul_right(cotangent, back_down)
        unused, gelu_pull = jax.vjp(gelu_tanh, pre_act)
        pre_grad = gelu_pull(act_grad)[0].astype(jnp.bfloat16)
        grad_down = grad_down + matmul_left(activated, cotangent)
        grad_ubias = grad_ubias + jnp.sum(pre_grad.astype(jnp.float32), axis=0).reshape(
            heads_local, -1
        )
        grad_up = grad_up + matmul_left(normed_two, pre_grad)
        normed_two_back = matmul_right(pre_grad, back_up)
        unused, norm_pull = jax.vjp(layer_norm, residual, gain_two, shift_two)
        resid_grad, gain_two_grad, shift_two_grad = norm_pull(full_total(normed_two_back))
        cot_rows = cotangent.astype(jnp.float32)
        resid_grad = resid_grad + cot_rows
        attn_grad = resid_grad.astype(jnp.bfloat16)
        grad_wout = grad_wout + matmul_left(mixed_low, attn_grad)
        mixed_grad = matmul_right(attn_grad, back_out).astype(jnp.bfloat16)
        mixed_grad_heads = mixed_grad.reshape(micro_seqs, span_len, heads_local, HEAD_DIM)
        scores = scores_of(query_heads, key_heads, query_segf, key_seg, slopes, span_first)
        softmaxed = jnp.exp(scores - log_total)
        prob_grad = jnp.einsum(
            "bqhd,bkhd->bhqk", mixed_grad_heads, value_heads, preferred_element_type=jnp.float32
        )
        delta = jnp.sum(softmaxed * prob_grad, axis=-1, keepdims=True)
        score_grad = (softmaxed * (prob_grad - delta)).astype(jnp.bfloat16)
        query_grad = (
            jnp.einsum("bhqk,bkhd->bqhd", score_grad, key_heads, preferred_element_type=jnp.float32)
            * scale
        )
        query_low = query_grad.reshape(row_count, cols_local).astype(jnp.bfloat16)
        key_grad = (
            jnp.einsum(
                "bhqk,bqhd->bkhd", score_grad, query_heads, preferred_element_type=jnp.float32
            )
            * scale
        )
        value_grad = jnp.einsum(
            "bhqk,bqhd->bkhd",
            softmaxed.astype(jnp.bfloat16),
            mixed_grad_heads,
            preferred_element_type=jnp.float32,
        )
        pair_grad = jnp.concatenate(
            [
                key_grad.reshape(micro_seqs, length_all, cols_local),
                value_grad.reshape(micro_seqs, length_all, cols_local),
            ],
            axis=2,
        )
        pair_own = lax.psum_scatter(
            pair_grad.astype(jnp.bfloat16), "ctx", scatter_dimension=1, tiled=True
        ).astype(jnp.float32)
        key_low = pair_own[:, :, :cols_local].reshape(row_count, cols_local).astype(jnp.bfloat16)
        value_low = pair_own[:, :, cols_local:].reshape(row_count, cols_local).astype(jnp.bfloat16)
        grad_query = grad_query + matmul_left(normed_one, query_low)
        grad_key = grad_key + matmul_left(normed_one, key_low)
        grad_value = grad_value + matmul_left(normed_one, value_low)
        grad_qbias = grad_qbias + jnp.sum(query_low.astype(jnp.float32), axis=0).reshape(
            heads_local, HEAD_DIM
        )
        grad_vbias = grad_vbias + jnp.sum(value_low.astype(jnp.float32), axis=0).reshape(
            heads_local, HEAD_DIM
        )
        normed_one_back = (
            matmul_right(query_low, back_query)
            + matmul_right(key_low, back_key)
            + matmul_right(value_low, back_value)
        )
        unused, first_pull = jax.vjp(layer_norm, inputs, gain_one, shift_one)
        input_grad, gain_one_grad, shift_one_grad = first_pull(full_total(normed_one_back))
        input_grad = (input_grad + resid_grad).astype(jnp.bfloat16)
        inputs_grad_list.append(input_grad.reshape(micro_seqs, span_len, model_width))
        grad_small = grad_small + jnp.stack(
            [
                gain_one_grad,
                shift_one_grad,
                jnp.sum(resid_grad, axis=0),
                gain_two_grad,
                shift_two_grad,
                jnp.sum(cot_rows, axis=0),
            ],
            axis=0,
        )
    summed = (
        lax.psum_scatter(
            grad_query.astype(jnp.bfloat16), ("dp", "ctx"), scatter_dimension=0, tiled=True
        ).astype(jnp.float32),
        lax.psum_scatter(
            grad_key.astype(jnp.bfloat16), ("dp", "ctx"), scatter_dimension=0, tiled=True
        ).astype(jnp.float32),
        lax.psum_scatter(
            grad_value.astype(jnp.bfloat16), ("dp", "ctx"), scatter_dimension=0, tiled=True
        ).astype(jnp.float32),
        lax.psum_scatter(
            grad_qbias.astype(jnp.bfloat16), ("dp", "ctx"), scatter_dimension=1, tiled=True
        ).astype(jnp.float32),
        lax.psum_scatter(
            grad_vbias.astype(jnp.bfloat16), ("dp", "ctx"), scatter_dimension=1, tiled=True
        ).astype(jnp.float32),
        lax.psum_scatter(
            grad_wout.astype(jnp.bfloat16), ("dp", "ctx"), scatter_dimension=1, tiled=True
        ).astype(jnp.float32),
        lax.psum_scatter(
            grad_small.astype(jnp.bfloat16), ("dp", "ctx"), scatter_dimension=1, tiled=True
        ).astype(jnp.float32),
        lax.psum_scatter(
            grad_up.astype(jnp.bfloat16), ("dp", "ctx"), scatter_dimension=0, tiled=True
        ).astype(jnp.float32),
        lax.psum_scatter(
            grad_ubias.astype(jnp.bfloat16), ("dp", "ctx"), scatter_dimension=1, tiled=True
        ).astype(jnp.float32),
        lax.psum_scatter(
            grad_down.astype(jnp.bfloat16), ("dp", "ctx"), scatter_dimension=1, tiled=True
        ).astype(jnp.float32),
    )
    (
        sum_query,
        sum_key,
        sum_value,
        sum_qbias,
        sum_vbias,
        sum_wout,
        sum_small,
        sum_up,
        sum_ubias,
        sum_down,
    ) = summed
    return (
        jnp.concatenate(outputs_list, axis=0),
        jnp.concatenate(inputs_grad_list, axis=0),
        sum_small[0],
        sum_small[1],
        sum_query,
        sum_key,
        sum_value,
        sum_qbias,
        sum_vbias,
        sum_wout,
        sum_small[2],
        sum_small[3],
        sum_small[4],
        sum_up,
        sum_ubias,
        sum_down,
        sum_small[5],
    )


ALL = ("dp", "ctx", "tensor")
NORMAL = (((1,), (0,)), ((), ()))
ROWS = (((1,), (1,)), ((), ()))
COLS = (((0,), (0,)), ((), ()))
QUERY_BLOCK = 256


def dot(left, right, dims):
    return lax.dot_general(left, right, dims, preferred_element_type=jnp.float32)


def scores_turned(query, key, slope, first, seg_query, seg_key, causal_from):
    count, block = key.shape[0], query.shape[0]
    raw = dot(key, query, ROWS) * (1.0 / math.sqrt(HEAD_DIM))
    key_place = lax.broadcasted_iota(jnp.int32, (count, 1), 0)
    query_place = first + lax.broadcasted_iota(jnp.int32, (1, block), 1)
    scores = raw + slope * (key_place - query_place).astype(jnp.float32)
    allowed = (key_place <= query_place) & (seg_key == seg_query)
    return jnp.where(allowed, scores, -1e30)


def attend_kernel(heads, block, slope_ref, row_ref, col_ref, qkv_ref, o_ref, lse_ref):
    step = pl.program_id(1)
    length = qkv_ref.shape[0]
    width = heads * HEAD_DIM
    for head in range(heads):
        lo = head * HEAD_DIM
        slope = slope_ref[step * heads + head]
        for first in range(0, length, block):
            last = first + block
            query = qkv_ref[first:last, lo : lo + HEAD_DIM]
            key = qkv_ref[0:last, width + lo : width + lo + HEAD_DIM]
            value = qkv_ref[0:last, 2 * width + lo : 2 * width + lo + HEAD_DIM]
            scores = scores_turned(
                query, key, slope, first, row_ref[:, first:last], col_ref[0:last, :], first
            )
            highest = jnp.max(scores, axis=0, keepdims=True)
            exponent = jnp.exp(scores - highest)
            totals = jnp.sum(exponent, axis=0, keepdims=True)
            softmaxed = (exponent * (1.0 / totals)).astype(jnp.bfloat16)
            mixed = dot(softmaxed, value, COLS)
            o_ref[first:last, lo : lo + HEAD_DIM] = mixed.astype(jnp.bfloat16)
            lse_ref[head : head + 1, first:last] = highest + jnp.log(totals)


def attend_back_kernel(
    heads, block, slope_ref, row_ref, col_ref, qkv_ref, do_ref, lse_ref, grad_ref, dk_ref, dv_ref
):
    step = pl.program_id(1)
    length = qkv_ref.shape[0]
    width = heads * HEAD_DIM
    scale = 1.0 / math.sqrt(HEAD_DIM)
    for head in range(heads):
        lo = head * HEAD_DIM
        slope = slope_ref[step * heads + head]
        for first in reversed(range(0, length, block)):
            last = first + block
            query = qkv_ref[first:last, lo : lo + HEAD_DIM]
            key = qkv_ref[0:last, width + lo : width + lo + HEAD_DIM]
            value = qkv_ref[0:last, 2 * width + lo : 2 * width + lo + HEAD_DIM]
            mixed_grad = do_ref[first:last, lo : lo + HEAD_DIM]
            scores = scores_turned(
                query, key, slope, first, row_ref[:, first:last], col_ref[0:last, :], first
            )
            softmaxed = jnp.exp(scores - lse_ref[head : head + 1, first:last])
            prob_grad = dot(value, mixed_grad, ROWS)
            delta = jnp.sum(softmaxed * prob_grad, axis=0, keepdims=True)
            score_grad = (softmaxed * (prob_grad - delta)).astype(jnp.bfloat16)
            prob_low = softmaxed.astype(jnp.bfloat16)
            query_grad = dot(score_grad, key, COLS) * scale
            grad_ref[first:last, lo : lo + HEAD_DIM] = query_grad.astype(jnp.bfloat16)
            key_grad = dot(score_grad, query, NORMAL)
            value_grad = dot(prob_low, mixed_grad, NORMAL)
            if last == length:
                dk_ref[...] = key_grad
                dv_ref[...] = value_grad
            else:
                dk_ref[0:last, :] += key_grad
                dv_ref[0:last, :] += value_grad
        grad_ref[:, width + lo : width + lo + HEAD_DIM] = (dk_ref[...] * scale).astype(jnp.bfloat16)
        grad_ref[:, 2 * width + lo : 2 * width + lo + HEAD_DIM] = dv_ref[...].astype(jnp.bfloat16)


def attention_specs(seqs, length, groups, heads):
    width = heads * HEAD_DIM
    return (
        pl.BlockSpec(memory_space=pltpu.SMEM),
        pl.BlockSpec((None, 1, length), lambda s, t: (s, 0, 0)),
        pl.BlockSpec((None, length, 1), lambda s, t: (s, 0, 0)),
        pl.BlockSpec((None, length, 3 * width), lambda s, t: (s, 0, t)),
        pl.BlockSpec((None, length, width), lambda s, t: (s, 0, t)),
        pl.BlockSpec((None, None, heads, length), lambda s, t: (s, t, 0, 0)),
    )


def attend(slopes, seg_row, seg_col, qkv, groups, heads):
    seqs, length, _ = qkv.shape
    specs = attention_specs(seqs, length, groups, heads)
    block = math.gcd(length, QUERY_BLOCK)
    return pl.pallas_call(
        functools.partial(attend_kernel, heads, block),
        grid=(seqs, groups),
        in_specs=list(specs[:4]),
        out_specs=[specs[4], specs[5]],
        out_shape=[
            jax.ShapeDtypeStruct((seqs, length, groups * heads * HEAD_DIM), jnp.bfloat16),
            jax.ShapeDtypeStruct((seqs, groups, heads, length), jnp.float32),
        ],
        compiler_params=pltpu.CompilerParams(vmem_limit_bytes=40 * 2**20),
        name="attend",
    )(slopes, seg_row, seg_col, qkv)


def attend_back(slopes, seg_row, seg_col, qkv, mixed_grad, log_total, groups, heads):
    seqs, length, _ = qkv.shape
    specs = attention_specs(seqs, length, groups, heads)
    block = math.gcd(length, QUERY_BLOCK)
    return pl.pallas_call(
        functools.partial(attend_back_kernel, heads, block),
        grid=(seqs, groups),
        in_specs=list(specs),
        out_specs=specs[3],
        out_shape=jax.ShapeDtypeStruct(qkv.shape, jnp.bfloat16),
        scratch_shapes=[
            pltpu.VMEM((length, HEAD_DIM), jnp.float32),
            pltpu.VMEM((length, HEAD_DIM), jnp.float32),
        ],
        compiler_params=pltpu.CompilerParams(vmem_limit_bytes=40 * 2**20),
        name="attend_back",
    )(slopes, seg_row, seg_col, qkv, mixed_grad, log_total)


def whole_sequences(
    tokens,
    segment_ids,
    norm1_gain,
    norm1_shift,
    w_query,
    w_key,
    w_value,
    query_bias,
    value_bias,
    w_out,
    out_bias,
    norm2_gain,
    norm2_shift,
    w_up,
    up_bias,
    w_down,
    down_bias,
    out_grad,
):
    dps, ctxs, groups = (lax.axis_size(name) for name in ALL)
    owners = dps * ctxs
    place = lax.axis_index("tensor")
    seqs_local, span, model = tokens.shape
    per_group = seqs_local // groups
    seqs = per_group // ctxs
    length = span * ctxs
    rows = seqs * length
    heads = query_bias.shape[0]
    width = heads * HEAD_DIM
    shard = w_query.shape[0]
    hidden = w_up.shape[1]
    shared = query_bias.shape[1]
    shared_up = up_bias.shape[1]

    def gather(value):
        whole = lax.all_gather(value, ALL, axis=0, tiled=False)
        return whole.reshape((owners, groups) + value.shape)

    def to_sequences(value):
        mine = lax.dynamic_slice_in_dim(value, place * per_group, per_group, axis=0)
        mine = mine.reshape((ctxs, seqs) + value.shape[1:])
        mine = lax.all_to_all(mine, "ctx", split_axis=0, concat_axis=0, tiled=True)
        return jnp.swapaxes(mine, 0, 1)

    def to_spans(value):
        mine = jnp.swapaxes(value.reshape(seqs, ctxs, span, model), 0, 1)
        mine = lax.all_to_all(mine, "ctx", split_axis=0, concat_axis=0, tiled=True)
        mine = mine.reshape(per_group, span, model)
        return lax.all_gather(mine, "tensor", axis=0, tiled=True)

    def by_owner(value, columns):
        return value.reshape(owners, shard, groups, columns).transpose(0, 2, 1, 3)

    def scatter(value):
        return lax.psum_scatter(value, ALL, scatter_dimension=0, tiled=True)

    small = jnp.concatenate(
        [
            norm1_gain,
            norm1_shift,
            out_bias,
            norm2_gain,
            norm2_shift,
            down_bias,
            query_bias.reshape(-1),
            value_bias.reshape(-1),
            up_bias.reshape(-1),
        ]
    )
    first_pack = jnp.concatenate([w_query, w_key, w_value, w_out.T], axis=1)
    pack_width = first_pack.shape[1]
    extra = -(-small.shape[0] // (16 * pack_width)) * 16
    small = jnp.pad(small, (0, extra * pack_width - small.shape[0])).reshape(extra, pack_width)
    first_pack = gather(jnp.concatenate([first_pack, small], axis=0))
    small = first_pack[:, :, shard:].reshape(owners, groups, extra * pack_width)
    first_pack = first_pack[:, :, :shard]
    second_pack = gather(jnp.stack([w_up, w_down.T]))
    vectors = small[:, 0, : 6 * shard].reshape(owners, 6, shard).transpose(1, 0, 2)
    vectors = vectors.reshape(6, model).astype(jnp.float32)
    gain_one, shift_one, bias_out, gain_two, shift_two, bias_down = (
        vectors[index] for index in range(6)
    )

    def heads_bias(first, columns):
        part = small[:, :, first : first + heads * columns]
        part = part.reshape(owners, groups, heads, columns).transpose(1, 2, 0, 3)
        return part.reshape(groups, heads * columns * owners).astype(jnp.float32)

    bias_first = 6 * shard
    bias_query = heads_bias(bias_first, shared)
    bias_value = heads_bias(bias_first + heads * shared, shared)
    bias_up = heads_bias(bias_first + 2 * heads * shared, shared_up).reshape(-1)
    bias_qkv = jnp.stack([bias_query, jnp.zeros_like(bias_query), bias_value], axis=1).reshape(-1)

    full_qkv = first_pack[..., : 3 * width].transpose(0, 2, 1, 3)
    full_qkv = full_qkv.reshape(model, groups * 3 * width)
    turned_out = first_pack[..., 3 * width :].transpose(0, 2, 1, 3).reshape(model, groups * width)
    full_up = second_pack[:, :, 0].transpose(0, 2, 1, 3).reshape(model, groups * hidden)
    turned_down = second_pack[:, :, 1].transpose(0, 2, 1, 3).reshape(model, groups * hidden)

    inputs_low = to_sequences(tokens)
    segs = to_sequences(segment_ids)
    cotangent = to_sequences(out_grad).reshape(rows, model)
    seg_row = segs.reshape(seqs, 1, length)
    seg_col = segs.reshape(seqs, length, 1)
    slopes = jnp.exp2(-8.0 * jnp.arange(1, HEADS + 1).astype(jnp.float32) / HEADS)

    inputs = inputs_low.reshape(rows, model).astype(jnp.float32)
    normed_one = layer_norm(inputs, gain_one, shift_one).astype(jnp.bfloat16)
    qkv = (matmul(normed_one, full_qkv) + bias_qkv).astype(jnp.bfloat16)
    qkv = qkv.reshape(seqs, length, groups * 3 * width)
    mixed, log_total = attend(slopes, seg_row, seg_col, qkv, groups, heads)
    mixed = mixed.reshape(rows, groups * width)
    residual = inputs + matmul_right(mixed, turned_out) + bias_out
    normed_two = layer_norm(residual, gain_two, shift_two).astype(jnp.bfloat16)
    pre_act = matmul(normed_two, full_up) + bias_up
    activated = gelu_tanh(pre_act).astype(jnp.bfloat16)
    result = (residual + matmul_right(activated, turned_down) + bias_down).astype(jnp.bfloat16)
    outputs = to_spans(result.reshape(seqs, length, model))

    act_grad = matmul(cotangent, turned_down)
    unused, gelu_pull = jax.vjp(gelu_tanh, pre_act)
    pre_grad = gelu_pull(act_grad)[0].astype(jnp.bfloat16)
    grad_down = matmul_left(cotangent, activated).astype(jnp.bfloat16)
    grad_ubias = jnp.sum(pre_grad.astype(jnp.float32), axis=0)
    grad_up = matmul_left(normed_two, pre_grad).astype(jnp.bfloat16)
    grad_ff = jnp.stack([by_owner(grad_up, hidden), by_owner(grad_down, hidden)], axis=2)
    grad_ff, outputs = lax.optimization_barrier((grad_ff, outputs))
    sum_ff = scatter(grad_ff.reshape(-1, hidden)).astype(jnp.float32)
    sum_up = sum_ff[:shard]
    sum_down = sum_ff[shard:].T
    normed_two_back = matmul_right(pre_grad, full_up)
    unused, norm_pull = jax.vjp(layer_norm, residual, gain_two, shift_two)
    resid_grad, gain_two_grad, shift_two_grad = norm_pull(normed_two_back)
    cot_rows = cotangent.astype(jnp.float32)
    resid_grad = resid_grad + cot_rows
    attn_grad = resid_grad.astype(jnp.bfloat16)
    mixed_grad = matmul(attn_grad, turned_out).astype(jnp.bfloat16)
    grad_wout = matmul_left(attn_grad, mixed).astype(jnp.bfloat16)
    qkv_grad = attend_back(
        slopes,
        seg_row,
        seg_col,
        qkv,
        mixed_grad.reshape(seqs, length, groups * width),
        log_total,
        groups,
        heads,
    ).reshape(rows, groups * 3 * width)
    normed_one_back = matmul_right(qkv_grad, full_qkv)
    unused, first_pull = jax.vjp(layer_norm, inputs, gain_one, shift_one)
    input_grad, gain_one_grad, shift_one_grad = first_pull(normed_one_back)
    input_grad = (input_grad + resid_grad).astype(jnp.bfloat16)
    tokens_grad = to_spans(input_grad.reshape(seqs, length, model))
    grad_qkv = matmul_left(normed_one, qkv_grad).astype(jnp.bfloat16)
    grad_pack = jnp.concatenate(
        [by_owner(grad_qkv, 3 * width), by_owner(grad_wout, width)], axis=3
    )
    grad_bias = jnp.sum(qkv_grad.astype(jnp.float32), axis=0).reshape(groups, 3, heads, HEAD_DIM)

    grad_vectors = jnp.stack(
        [
            gain_one_grad,
            shift_one_grad,
            jnp.sum(resid_grad, axis=0),
            gain_two_grad,
            shift_two_grad,
            jnp.sum(cot_rows, axis=0),
        ]
    )
    grad_vectors = grad_vectors.reshape(6, owners, shard).transpose(1, 0, 2)
    grad_vectors = jnp.broadcast_to(
        grad_vectors.reshape(owners, 1, 6 * shard), (owners, groups, 6 * shard)
    )

    def owner_bias(value, columns):
        value = value.reshape(groups, heads, owners, columns).transpose(2, 0, 1, 3)
        return value.reshape(owners, groups, heads * columns)

    grad_small = jnp.concatenate(
        [
            grad_vectors,
            owner_bias(grad_bias[:, 0], shared),
            owner_bias(grad_bias[:, 2], shared),
            owner_bias(grad_ubias, shared_up),
        ],
        axis=2,
    )
    grad_small = grad_small.astype(jnp.bfloat16)
    padding = extra * pack_width - grad_small.shape[2]
    grad_small = jnp.pad(grad_small, ((0, 0), (0, 0), (0, padding)))
    grad_small = grad_small.reshape(owners, groups, extra, pack_width)
    grad_pack = jnp.concatenate([grad_pack, grad_small], axis=2)
    sum_pack = scatter(grad_pack.reshape(-1, pack_width)).astype(jnp.float32)
    sum_small = sum_pack[shard:].reshape(-1)
    sum_qkv = sum_pack[:shard, : 3 * width]
    sum_wout = sum_pack[:shard, 3 * width :].T
    sums = sum_small[: 6 * shard].reshape(6, shard)
    sum_biases = sum_small[6 * shard :]
    count = heads * shared
    return (
        outputs,
        tokens_grad,
        sums[0],
        sums[1],
        sum_qkv[:, :width],
        sum_qkv[:, width : 2 * width],
        sum_qkv[:, 2 * width :],
        sum_biases[:count].reshape(heads, shared),
        sum_biases[count : 2 * count].reshape(heads, shared),
        sum_wout,
        sums[2],
        sums[3],
        sums[4],
        sum_up,
        sum_biases[2 * count : 2 * count + heads * shared_up].reshape(heads, shared_up),
        sum_down,
        sums[5],
    )


def choose_plan(tokens, *others):
    if tokens.shape[0] % (lax.axis_size("ctx") * lax.axis_size("tensor")) == 0:
        return whole_sequences(tokens, *others)
    return shards(tokens, *others)


def solution(mesh):
    return jax.shard_map(
        choose_plan,
        mesh=mesh,
        in_specs=(
            P("dp", "ctx", None),
            P("dp", "ctx"),
            P(("dp", "ctx")),
            P(("dp", "ctx")),
            P(("dp", "ctx"), "tensor"),
            P(("dp", "ctx"), "tensor"),
            P(("dp", "ctx"), "tensor"),
            P("tensor", ("dp", "ctx")),
            P("tensor", ("dp", "ctx")),
            P("tensor", ("dp", "ctx")),
            P(("dp", "ctx")),
            P(("dp", "ctx")),
            P(("dp", "ctx")),
            P(("dp", "ctx"), "tensor"),
            P("tensor", ("dp", "ctx")),
            P("tensor", ("dp", "ctx")),
            P(("dp", "ctx")),
            P("dp", "ctx", None),
        ),
        out_specs=(
            P("dp", "ctx", None),
            P("dp", "ctx", None),
            P(("dp", "ctx")),
            P(("dp", "ctx")),
            P(("dp", "ctx"), "tensor"),
            P(("dp", "ctx"), "tensor"),
            P(("dp", "ctx"), "tensor"),
            P("tensor", ("dp", "ctx")),
            P("tensor", ("dp", "ctx")),
            P("tensor", ("dp", "ctx")),
            P(("dp", "ctx")),
            P(("dp", "ctx")),
            P(("dp", "ctx")),
            P(("dp", "ctx"), "tensor"),
            P("tensor", ("dp", "ctx")),
            P("tensor", ("dp", "ctx")),
            P(("dp", "ctx")),
        ),
        check_vma=False,
    )
```

profile of v0, /device:TPU:0, one launch (start us, length us, event | category | flops | bytes accessed | tf_op | source)
XLA Modules:
  0.0 1173.3 jit_solution(5401483107789454571)
XLA Ops:
  34.6 26.8 %all-to-all-done = bf16[4,1,256,1024]{3,2,1,0:T(8,128)(2,1)S(1)} async-done(((bf16[4,1,256,1024]{3,2,1,0:T(8,128)(2,1)}), bf16[4,1,256,1024]{3,2,1,0:T(8,128)(2,1)S(1)}, u32[]{:S(2)}, u32[]{:S(2)}) %all-to-all-start) | async-done | bytes 2097184 | tf_op jit(solution)/shard_map/all_to_all | solution.py:555
  68.5 40.0 %all-to-all-done.2 = bf16[4,1,256,1024]{3,2,1,0:T(8,128)(2,1)} async-done(((bf16[4,1,256,1024]{3,2,1,0:T(8,128)(2,1)}), bf16[4,1,256,1024]{3,2,1,0:T(8,128)(2,1)}, u32[]{:S(2)}, u32[]{:S(2)}) %all-to-all-start.2) | async-done | bytes 2097184 | tf_op jit(solution)/shard_map/all_to_all | solution.py:555
  162.7 33.8 %attend.1 = (bf16[1,1024,1024]{2,1,0:T(8,128)(2,1)S(1)}, f32[1,4,4,1024]{3,2,1,0:T(4,128)S(1)}) custom-call(f32[16]{0:T(128)S(1)} %multiply_exponential_fusion.slope_ref, s32[1,1,1024]{2,1,0:T(1,128)S(1)} %bitcast.234, s32[1,1024,1]{2,1,0:T(8,128)S(1)} %copy.94.col_ref, bf16[1,1024,3072]{2,1,0:T(8,128)(2,1)S(1)} %fusion.20.qkv_ref), custom_call_target="tpu_custom_call" | custom-call | tf_op jit(solution)/shard_map/attend/pallas_call | solution.py:480
  201.7 35.1 %all-gather.11.cloned.1.call-done = bf16[64,128,1024]{2,1,0:T(8,128)(2,1)} async-done(((bf16[2,128,1024]{2,1,0:T(8,128)(2,1)}), bf16[64,128,1024]{2,1,0:T(8,128)(2,1)}) %all-gather.11.cloned.1.call-update) | async-done | bytes 16777232 | tf_op jit(solution)/shard_map/all_gather | solution.py:549
  236.9 12.0 %fusion.85 = (bf16[8,4,1,128,1024]{4,3,2,1,0:T(8,128)(2,1)}, bf16[8,4,1,128,1024]{4,3,2,1,0:T(8,128)(2,1)}) fusion(bf16[8,4,2,128,1024]{4,3,2,1,0:T(8,128)(2,1)} %bitcast.240), kind=kLoop, calls=%fused_computation.138 | loop fusion | bytes 33554432 | tf_op jit(solution)/shard_map/slice | solution.py:612
  248.9 12.4 %copy.126 = bf16[8,4,1,128,1024]{3,0,4,1,2:T(8,128)(2,1)} copy(bf16[8,4,1,128,1024]{4,3,2,1,0:T(8,128)(2,1)} %get-tuple-element.104) | data formatting | bytes 16777216
  261.3 12.4 %copy.124 = bf16[8,4,1,128,1024]{3,0,4,1,2:T(8,128)(2,1)} copy(bf16[8,4,1,128,1024]{4,3,2,1,0:T(8,128)(2,1)} %get-tuple-element.105) | data formatting | bytes 16777216
  273.7 17.2 %fusion.12 = f32[1024,4096]{1,0:T(8,128)} fusion(bf16[512,8,8,128]{3,2,1,0:T(8,128)(2,1)} %bitcast.247, f32[1024,1024]{1,0:T(8,128)} %copy-done.7, f32[1024]{0:T(1024)S(1)} %get-tuple-element.120, f32[1024]{0:T(1024)S(1)} %get-tuple-element.121, f32[1024]{0:T(1024)S(1)} %fusion.77, f32[1024]{0:T(1024)S(1)} %broadcast_multiply_fusion), kind=kOutput, calls=%fused_computation.20 | convolution fusion | flops 8595177472 | bytes 29376512 | tf_op jit(solution)/shard_map/dot_general | solution.py:34
  290.9 18.1 %add_convert_fusion.2 = bf16[1024,1024]{1,0:T(8,128)(2,1)} fusion(f32[1024,1024]{1,0:T(8,128)S(1)} %copy-done.8, bf16[512,8,8,128]{3,2,1,0:T(8,128)(2,1)} %bitcast.249, f32[1024]{0:T(1024)S(1)} %get-tuple-element.119, f32[1024,4096]{1,0:T(8,128)} %fusion.12, f32[4096]{0:T(1024)S(1)} %reshape.407), kind=kOutput, calls=%fused_computation.65 | convolution fusion | flops 8635023360 | bytes 31477760 | tf_op jit(solution)/shard_map/dot_general | solution.py:44
  313.6 28.6 %fusion.92 = (bf16[4096]{0:T(1024)(128)(2,1)S(1)}, bf16[1024,4096]{1,0:T(8,128)(2,1)}) fusion(bf16[1024,1024]{1,0:T(8,128)(2,1)} %bitcast.29, bf16[512,8,8,128]{3,2,1,0:T(8,128)(2,1)} %bitcast.250, f32[1024,4096]{1,0:T(8,128)} %fusion.12, f32[4096]{0:T(1024)S(1)} %reshape.407), kind=kOutput, calls=%fused_computation.145 | convolution fusion | flops 8698982400 | bytes 35676160 | tf_op jit(solution)/shard_map/dot_general | solution.py:34
  342.3 15.5 %multiply_reduce_fusion = (bf16[1024]{0:T(1024)(128)(2,1)S(1)}, f32[1024]{0:T(1024)S(1)}, bf16[1024]{0:T(1024)(128)(2,1)S(1)}, f32[1024,1024]{1,0:T(8,128)S(1)}) fusion(f32[1024,1024]{1,0:T(8,128)} %copy-done.7, f32[1024]{0:T(1024)S(1)} %fusion.77, f32[1024]{0:T(1024)S(1)} %broadcast_multiply_fusion, f32[1024]{0:T(1024)S(1)} %get-tuple-element.121, ...), kind=kOutput, calls=%fused_computation.61 | convolution fusion | flops 8598320128 | bytes 25186304 | tf_op jit(solution)/shard_map/dot_general | solution.py:44
  377.9 50.3 %attend_back.1 = bf16[1,1024,3072]{2,1,0:T(8,128)(2,1)S(1)} custom-call(f32[16]{0:T(128)S(1)} %multiply_exponential_fusion.slope_ref, s32[1,1,1024]{2,1,0:T(1,128)S(1)} %bitcast.235, s32[1,1024,1]{2,1,0:T(8,128)S(1)} %copy.94.col_ref, bf16[1,1024,3072]{2,1,0:T(8,128)(2,1)} %copy-done.2, bf16[1,1024,1024]{2,1,0:T(8,128)(2,1)S(1)} %convert_bitcast_fusion.do_ref, ...), custom_call_target="tpu_custom_call" | custom-call | tf_op jit(solution)/shard_map/attend_back/pallas_call | solution.py:498
  434.8 11.5 fusion.28
  446.3 12.3 %reshape.393 = bf16[8,128,4,768]{3,2,1,0:T(4,128)(2,1)} reshape(bf16[1024,3072]{1,0:T(8,128)(2,1)} %fusion.28) | data formatting | bytes 12582912 | tf_op jit(solution)/shard_map/reshape | solution.py:565
  496.7 29.0 %all_to_all.25 = bf16[4,1,256,1024]{3,2,1,0:T(8,128)(2,1)} all-to-all(bf16[4,1,256,1024]{3,2,1,0:T(8,128)(2,1)S(1)} %bitcast.251), channel_id=1, replica_groups=mesh['dp'=2,'ctx'=4,'tensor'=4] {'ctx'}, dimensions={0} | all-to-all | bytes 4194304 | tf_op jit(solution)/shard_map/all_to_all | solution.py:560
  525.8 16.2 %convolution_convert_fusion = bf16[1024,4096]{1,0:T(8,128)(2,1)} fusion(bf16[1024,1024]{1,0:T(8,128)(2,1)} %bitcast.29, f32[1024,4096]{1,0:T(8,128)} %fusion.12, f32[4096]{0:T(1024)S(1)} %reshape.407), kind=kOutput, calls=%fused_computation.22 | convolution fusion | flops 8636071936 | bytes 27279360 | tf_op jit(solution)/shard_map/dot_general | solution.py:38
  542.0 14.6 %reshape.388 = bf16[8,128,4,1024]{3,2,1,0:T(4,128)(2,1)} reshape(bf16[1024,4096]{1,0:T(8,128)(2,1)} %convolution_convert_fusion) | data formatting | bytes 16777216 | tf_op jit(solution)/shard_map/reshape | solution.py:565
  556.6 15.6 %convolution_convert_fusion.1 = bf16[1024,4096]{1,0:T(8,128)(2,1)} fusion(bf16[1024,4096]{1,0:T(8,128)(2,1)} %get-tuple-element.138, f32[1024,1024]{1,0:T(8,128)} %copy-done.7, f32[1024]{0:T(1024)S(1)} %copy-done.22, f32[1024]{0:T(1024)S(1)} %get-tuple-element.121, f32[1024]{0:T(1024)S(1)} %fusion.77, f32[1024]{0:T(1024)S(1)} %broadcast_multiply_fusion), kind=kOutput, calls=%fused_computation.23 | convolution fusion | flops 8599371776 | bytes 20987904 | tf_op jit(solution)/shard_map/dot_general | solution.py:38
  572.2 14.6 %reshape.387 = bf16[8,128,4,1024]{3,2,1,0:T(4,128)(2,1)} reshape(bf16[1024,4096]{1,0:T(8,128)(2,1)} %convolution_convert_fusion.1) | data formatting | bytes 16777216 | tf_op jit(solution)/shard_map/reshape | solution.py:565
  586.9 15.2 %pad_maximum_fusion = bf16[8,4,2,128,1024]{4,1,3,0,2:T(4,128)(2,1)} fusion(bf16[8,4,1,128,1024]{4,1,3,0,2:T(4,128)(2,1)} %bitcast.237, bf16[8,4,1,128,1024]{4,1,3,0,2:T(4,128)(2,1)} %bitcast.238), kind=kLoop, calls=%fused_computation.10 | loop fusion | flops 8388608 | bytes 33554432 | tf_op jit(solution)/shard_map/stack | solution.py:640
  602.1 44.8 %copy.111 = bf16[8,4,2,128,1024]{3,2,1,0,4:T(2,128)(2,1)} copy(bf16[8,4,2,128,1024]{4,1,3,0,2:T(4,128)(2,1)} %pad_maximum_fusion) | data formatting | bytes 33554432 | tf_op jit(solution)/shard_map/optimization_barrier | solution.py:641
  646.9 28.0 %reshape.403 = bf16[8192,1024]{0,1:T(8,128)(2,1)} reshape(bf16[8,4,2,128,1024]{3,2,1,0,4:T(2,128)(2,1)} %copy.111) | data formatting | bytes 33554432 | tf_op jit(solution)/shard_map/reshape | solution.py:642
  681.6 99.5 %all-gather.15.cloned.1.call-done = bf16[16,1,256,1024]{3,2,1,0:T(8,128)(2,1)} async-done(((bf16[4,1,256,1024]{3,2,1,0:T(8,128)(2,1)}), bf16[16,1,256,1024]{3,2,1,0:T(8,128)(2,1)}) %all-gather.15.cloned.1.call-update) | async-done | bytes 8388624 | tf_op jit(solution)/shard_map/all_gather | solution.py:562
  781.1 364.7 %reduce-scatter.5.cloned.1.call-done = bf16[256,1024]{0,1:T(8,128)(2,1)} async-done(((bf16[8192,1024]{0,1:T(8,128)(2,1)}), bf16[256,1024]{0,1:T(8,128)(2,1)}) %reduce-scatter.5.cloned.1.call-update) | async-done | bytes 524304 | tf_op jit(solution)/shard_map/reduce_scatter | solution.py:568
  (176 shorter events, 189.7 us)
Async XLA Ops:
  7.2 12.1 %copy-start = (s32[16,256]{1,0:T(8,128)S(1)}, s32[16,256]{1,0:T(8,128)}, u32[]{:S(2)}) copy-start(s32[16,256]{1,0:T(8,128)} %param.19) | copy-start | bytes 49156
  7.2 112.8 %all-gather.9.cloned.1.call-start = ((), (), s32[]{:S(2)}) async-start(), calls=%async_computation.9 | async-start | bytes 9732096 | tf_op jit(solution)/shard_map/all_gather | solution.py:549
  16.3 220.6 %all-gather.11.cloned.1.call-start = ((), (), s32[]{:S(2)}) async-start(), calls=%async_computation.10 | async-start | bytes 17301504 | tf_op jit(solution)/shard_map/all_gather | solution.py:549
  19.9 8.0 all-to-all-start.1
  27.9 33.5 %all-to-all-start = ((bf16[4,1,256,1024]{3,2,1,0:T(8,128)(2,1)}), bf16[4,1,256,1024]{3,2,1,0:T(8,128)(2,1)S(1)}, u32[]{:S(2)}, u32[]{:S(2)}) async-start(bf16[4,1,256,1024]{3,2,1,0:T(8,128)(2,1)} %dynamic-slice_bitcast_fusion.1), calls=%async_computation | async-start | bytes 4194304 | tf_op jit(solution)/shard_map/all_to_all | solution.py:555
  61.4 89.9 %copy-start.4 = (bf16[4,1,256,1024]{3,2,1,0:T(8,128)(2,1)}, bf16[4,1,256,1024]{3,2,1,0:T(8,128)(2,1)S(1)}, u32[]{:S(2)}) copy-start(bf16[4,1,256,1024]{3,2,1,0:T(8,128)(2,1)S(1)} %all-to-all-done) | copy-start | bytes 6291460
  61.4 47.1 %all-to-all-start.2 = ((bf16[4,1,256,1024]{3,2,1,0:T(8,128)(2,1)}), bf16[4,1,256,1024]{3,2,1,0:T(8,128)(2,1)}, u32[]{:S(2)}, u32[]{:S(2)}) async-start(bf16[4,1,256,1024]{3,2,1,0:T(8,128)(2,1)} %dynamic-slice_bitcast_fusion), calls=%async_computation.2 | async-start | bytes 4194304 | tf_op jit(solution)/shard_map/all_to_all | solution.py:555
  151.3 11.4 copy-start.16
  151.3 122.4 %copy-start.21 = (f32[1024]{0:T(1024)}, f32[1024]{0:T(1024)S(1)}, u32[]{:S(2)}) copy-start(f32[1024]{0:T(1024)S(1)} %get-tuple-element.120) | copy-start | bytes 12292
  152.2 10.5 copy-start.14
  162.7 36.4 %copy-start.2 = (bf16[1,1024,3072]{2,1,0:T(8,128)(2,1)}, bf16[1,1024,3072]{2,1,0:T(8,128)(2,1)S(1)}, u32[]{:S(2)}) copy-start(bf16[1,1024,3072]{2,1,0:T(8,128)(2,1)S(1)} %fusion.20.qkv_ref) | copy-start | bytes 18874372
  162.7 33.9 %copy-start.5 = (bf16[4,1,256,1024]{3,2,1,0:T(8,128)(2,1)S(1)}, bf16[4,1,256,1024]{3,2,1,0:T(8,128)(2,1)}, u32[]{:S(2)}) copy-start(bf16[4,1,256,1024]{3,2,1,0:T(8,128)(2,1)} %copy-done.4) | copy-start | bytes 6291460
  162.7 33.9 %copy-start.13 = (bf16[8,128,4,256]{1,0,3,2:T(8,128)(2,1)S(1)}, bf16[8,128,4,256]{1,0,3,2:T(8,128)(2,1)}, u32[]{:S(2)}) copy-start(bf16[8,128,4,256]{1,0,3,2:T(8,128)(2,1)} %copy.95) | copy-start | bytes 6291460
  273.7 17.2 %copy-start.8 = (f32[1024,1024]{1,0:T(8,128)S(1)}, f32[1024,1024]{1,0:T(8,128)}, u32[]{:S(2)}) copy-start(f32[1024,1024]{1,0:T(8,128)} %copy-done.7) | copy-start | bytes 12582916
  309.0 33.2 %all-to-all-start.3 = ((bf16[4,1,256,1024]{3,2,1,0:T(8,128)(2,1)}), bf16[4,1,256,1024]{3,2,1,0:T(8,128)(2,1)}, u32[]{:S(2)}, u32[]{:S(2)}) async-start(bf16[4,1,256,1024]{3,2,1,0:T(8,128)(2,1)} %bitcast.258), calls=%async_computation.3 | async-start | bytes 4194304 | tf_op jit(solution)/shard_map/all_to_all | solution.py:560
  313.5 288.5 %all-gather.13.cloned.1.call-start = ((), (), s32[]{:S(2)}) async-start(), calls=%async_computation.11 | async-start | bytes 10485760 | tf_op jit(solution)/shard_map/all_gather | solution.py:562
  342.2 332.7 %reduce-scatter.3.cloned.1.call-start = ((), (), s32[]{:S(2)}) async-start(), calls=%async_computation.7 | async-start | bytes 9732096 | tf_op jit(solution)/shard_map/reduce_scatter | solution.py:568
  342.3 15.5 %copy-start.9 = (f32[1024,1024]{1,0:T(8,128)S(1)}, f32[1024,1024]{1,0:T(8,128)}, u32[]{:S(2)}) copy-start(f32[1024,1024]{1,0:T(8,128)} %copy-done.7) | copy-start | bytes 12582916
  458.6 7.5 copy-start.18
  466.2 11.1 copy-start.19
  492.3 288.8 %all-gather.15.cloned.1.call-start = ((), (), s32[]{:S(2)}) async-start(), calls=%async_computation.12 | async-start | bytes 10485760 | tf_op jit(solution)/shard_map/all_gather | solution.py:562
  525.7 620.1 %reduce-scatter.5.cloned.1.call-start = ((), (), s32[]{:S(2)}) async-start(), calls=%async_computation.8 | async-start | bytes 17301504 | tf_op jit(solution)/shard_map/reduce_scatter | solution.py:568
  542.0 14.6 %copy-start.22 = (f32[1024]{0:T(1024)S(1)}, f32[1024]{0:T(1024)}, u32[]{:S(2)}) copy-start(f32[1024]{0:T(1024)} %copy-done.21) | copy-start | bytes 12292
  1157.9 8.1 copy-start.1
  (9 other events, 35.2 us)
Sparse Core Ops, SparseCore 0:
  16.4 103.5 all-gather.8
  123.6 113.2 all-gather.10
  342.3 148.9 all-gather.12
  497.0 133.8 reduce-scatter.2
  632.5 148.6 all-gather.14
  783.4 362.4 reduce-scatter.4
where the time goes:
time: 1190 us; the launch traced here: 1170 us
  waiting for transfers between devices  576 us (48%)
  local copies, waits for them, and re-layouts  248 us (21%)
  matrix products  155 us (13%)
  Pallas kernels  84.1 us (7%)
  other arithmetic  49.2 us (4%)
  blocking collectives  29 us (2%)
  starting transfers between devices  17.1 us (1%)
  between operations  15.2 us (1%)
    reduce_scatter x2, waiting for transfers between devices, scatter(): return lax.psum_scatter(value, ALL, scatter_dimension=0, tiled=True)  365 us
    all_gather x2, waiting for transfers between devices, to_spans(): return lax.all_gather(mine, 'tensor', axis=0, tiled=True)  99.5 us
    all_to_all x3, waiting for transfers between devices, to_sequences(): mine = lax.all_to_all(mine, 'ctx', split_axis=0, concat_axis=0, tiled=True)  67.5 us
    dot_general x4, matrix products, matmul(): return jnp.dot(left, right, preferred_element_type=jnp.float32)  60.3 us
    unnamed x63, local copies, waits for them, and re-layouts  56.2 us
    reshape x6, local copies, waits for them, and re-layouts, by_owner(): return value.reshape(owners, shard, groups, columns).transpose(0, 2, 1, 3)  53.5 us
    pallas_call x1, Pallas kernels, attend_back(): pl.pallas_call(functools.partial(attend_back_kernel, heads, block), grid=...  50.3 us
    dot_general x4, matrix products, matmul_right(): lax.dot_general(left, right, (((1,), (1,)), ((), ())), preferred_element_...  47.1 us
  transfers between devices with their start and end apart: 10, of which 7 were waited for; matrix products, arithmetic and copies ran while one was open for 29% of the time, Pallas kernels for 7%

commit v1 on v0

--- a/solution.py
+++ b/solution.py
@@ -510,7 +510,634 @@
     )(slopes, seg_row, seg_col, qkv, mixed_grad, log_total)
 
 
-def whole_sequences(
+def core_params(mib=56):
+    return pltpu.CompilerParams(vmem_limit_bytes=mib * 2**20)
+
+
+def cost(flops, moved):
+    return pl.CostEstimate(flops=int(flops), bytes_accessed=int(moved), transcendentals=0)
+
+
+TILE = 256
+WEIGHT_ROWS = 128
+WIDE = 128
+
+
+def norm_parts(values):
+    centre = values - jnp.mean(values, axis=-1, keepdims=True)
+    spread = jnp.mean(centre * centre, axis=-1, keepdims=True)
+    scale = lax.rsqrt(spread + EPSILON)
+    return centre * scale, scale
+
+
+def norm_back(grad, normed, scale, gain):
+    scaled = grad * gain
+    mean_one = jnp.mean(scaled, axis=-1, keepdims=True)
+    mean_two = jnp.mean(scaled * normed, axis=-1, keepdims=True)
+    return scale * (scaled - mean_one - normed * mean_two)
+
+
+def column_sum(values):
+    return jnp.sum(values, axis=0, keepdims=True)
+
+
+def flat(ref):
+    block = ref[...]
+    return block.reshape(-1, block.shape[-1])
+
+
+def joined(refs):
+    blocks = [ref[...] for ref in refs]
+    return jnp.concatenate(blocks[:4], axis=0), jnp.concatenate(blocks[4:], axis=0)
+
+
+def ff_blocks(which, depth, hidden):
+    def spec(block):
+        def index(z, order):
+            return (order[block] * 4 + lax.bitwise_xor(z, order[12]), which, 0, 0)
+
+        return pl.BlockSpec((None, None, depth, hidden), index)
+
+    return [spec(block) for block in range(8)]
+
+
+def prefetched(grid, in_specs, out_specs, scratch=()):
+    return pltpu.PrefetchScalarGridSpec(
+        num_scalar_prefetch=1,
+        grid=grid,
+        in_specs=in_specs,
+        out_specs=out_specs,
+        scratch_shapes=list(scratch),
+    )
+
+
+def into_hidden(rows, near, far):
+    half = rows.shape[1] // 2
+    return dot(rows[:, :half], near, NORMAL) + dot(rows[:, half:], far, NORMAL)
+
+
+def order_kernel(order_ref, pieces_ref, out_ref):
+    columns = out_ref.shape[1] // WIDE
+    for block in range(columns):
+        place = pl.multiple_of(order_ref[block] * WIDE, WIDE)
+        out_ref[:, block * WIDE : (block + 1) * WIDE] = pieces_ref[:, pl.ds(place, WIDE)]
+
+
+def order_pieces(order, pieces):
+    count, span, model = pieces.shape
+    return pl.pallas_call(
+        order_kernel,
+        grid_spec=pltpu.PrefetchScalarGridSpec(
+            num_scalar_prefetch=1,
+            grid=(count,),
+            in_specs=[pl.BlockSpec((None, span, model), lambda p, order: (order[8 + p], 0, 0))],
+            out_specs=pl.BlockSpec((span, model), lambda p, order: (p, 0)),
+        ),
+        out_shape=jax.ShapeDtypeStruct((count * span, model), pieces.dtype),
+        compiler_params=core_params(32),
+        cost_estimate=cost(0, 4 * pieces.size),
+        name="order_pieces",
+    )(order, pieces)
+
+
+def place_kernel(order_ref, pieces_ref, out_ref):
+    out_ref[...] = pieces_ref[...]
+
+
+def place_slots(order, pieces):
+    count, span, model = pieces.shape
+
+    def index(z, j, order):
+        return (z * 4 + order[8 + j], 0, 0)
+
+    return pl.pallas_call(
+        place_kernel,
+        grid_spec=prefetched(
+            (count // 4, 4),
+            [pl.BlockSpec((None, span, model), index)],
+            pl.BlockSpec((None, span, model), lambda z, j, order: (z * 4 + j, 0, 0)),
+        ),
+        out_shape=jax.ShapeDtypeStruct(pieces.shape, pieces.dtype),
+        compiler_params=core_params(32),
+        cost_estimate=cost(0, 4 * pieces.size),
+        name="place_slots",
+    )(order, pieces)
+
+
+MESH = pl.DeviceIdType.MESH
+
+
+def partner(place, bits):
+    if bits == 3:
+        return 3 - place
+    return place + bits - 2 * bits * lax.rem(lax.div(place, bits), 2)
+
+
+def gather_kernel(
+    cut,
+    pack_ref,
+    tokens_ref,
+    seg_ref,
+    out_ref,
+    far_ref,
+    pieces_ref,
+    segs_ref,
+    local_sems,
+    ctx_send,
+    ctx_recv,
+    z_send,
+    z_recv,
+    hop_send,
+    hop_recv,
+):
+    at_x = lax.axis_index("dp")
+    at_ctx = lax.axis_index("ctx")
+    at_z = lax.axis_index("tensor")
+    ctx_of = [{"ctx": partner(at_ctx, bits)} for bits in (1, 2, 3)]
+    z_of = [{"tensor": partner(at_z, bits)} for bits in (1, 2, 3)]
+    x_of, y_of, core_of = {"dp": 1 - at_x}, ctx_of[1], ctx_of[0]
+
+    barrier = pltpu.get_barrier_semaphore()
+    for device in ctx_of + z_of + [x_of]:
+        pl.semaphore_signal(barrier, inc=1, device_id=device, device_id_type=MESH)
+    pl.semaphore_wait(barrier, 7)
+
+    def remote(source, target, send, recv, device):
+        copy = pltpu.make_async_remote_copy(
+            src_ref=source,
+            dst_ref=target,
+            send_sem=send,
+            recv_sem=recv,
+            device_id=device,
+            device_id_type=MESH,
+        )
+        copy.start()
+        return copy
+
+    def hop(stage, z, source, target, device):
+        return remote(source, target, hop_send.at[stage, z], hop_recv.at[stage, z], device)
+
+    def slot(bits):
+        place = at_ctx if bits == 0 else partner(at_ctx, bits)
+        return at_z * 4 + place
+
+    local = [
+        pltpu.make_async_copy(pack_ref, out_ref.at[0, 0, 0], local_sems.at[0]),
+        pltpu.make_async_copy(tokens_ref.at[slot(0)], pieces_ref.at[0], local_sems.at[1]),
+        pltpu.make_async_copy(seg_ref.at[slot(0)], segs_ref.at[0], local_sems.at[2]),
+    ]
+    for copy in local:
+        copy.start()
+    across = [
+        remote(pack_ref, out_ref.at[0, 0, bits], z_send.at[bits], z_recv.at[bits], z_of[bits - 1])
+        for bits in (1, 2, 3)
+    ]
+
+    def first_hops(z, source):
+        return (
+            hop(0, z, source.at[:cut], out_ref.at[0, 1, z, :cut], x_of),
+            hop(1, z, source.at[cut:], out_ref.at[1, 0, z, cut:], y_of),
+        )
+
+    first = [first_hops(0, pack_ref)]
+    others = []
+    for bits in (1, 2, 3):
+        device = ctx_of[bits - 1]
+        for kind, (source, target) in enumerate(((tokens_ref, pieces_ref), (seg_ref, segs_ref))):
+            send, recv = ctx_send.at[kind, bits], ctx_recv.at[kind, bits]
+            others.append(remote(source.at[slot(bits)], target.at[bits], send, recv, device))
+    for z in (1, 2, 3):
+        across[z - 1].wait_recv()
+        first.append(first_hops(z, out_ref.at[0, 0, z]))
+    local[0].wait()
+    second = []
+    for z in range(4):
+        first[z][0].wait_recv()
+        source = out_ref.at[0, :, z, :cut]
+        to_y = hop(2, z, source, out_ref.at[1, :, z, :cut], y_of)
+        first[z][1].wait_recv()
+        source = out_ref.at[:, 0, z, cut:]
+        second.append((to_y, hop(3, z, source, out_ref.at[:, 1, z, cut:], x_of)))
+    third = []
+    for z in range(4):
+        for copy in second[z]:
+            copy.wait_recv()
+        third.append(hop(4, z, out_ref.at[:, :, z], far_ref.at[:, :, z], core_of))
+    for copy in third + others:
+        copy.wait_recv()
+    for copy in across + others + third:
+        copy.wait_send()
+    for pair in first + second:
+        for copy in pair:
+            copy.wait_send()
+    local[1].wait()
+    local[2].wait()
+
+
+def gather_first(pack, tokens, segs, cut):
+    rows, columns = pack.shape
+    span, model = tokens.shape[1:]
+    anywhere = pl.BlockSpec(memory_space=pl.ANY)
+    sems = pltpu.SemaphoreType.DMA
+    return pl.pallas_call(
+        functools.partial(gather_kernel, cut),
+        in_specs=[anywhere] * 3,
+        out_specs=[anywhere] * 4,
+        out_shape=[
+            jax.ShapeDtypeStruct((2, 2, 4, rows, columns), pack.dtype),
+            jax.ShapeDtypeStruct((2, 2, 4, rows, columns), pack.dtype),
+            jax.ShapeDtypeStruct((4, span, model), tokens.dtype),
+            jax.ShapeDtypeStruct((4,) + segs.shape[1:], segs.dtype),
+        ],
+        scratch_shapes=[
+            sems((3,)),
+            sems((2, 4)),
+            sems((2, 4)),
+            sems((4,)),
+            sems((4,)),
+            sems((5, 4)),
+            sems((5, 4)),
+        ],
+        compiler_params=pltpu.CompilerParams(collective_id=0, has_side_effects=True),
+        cost_estimate=cost(0, 128 * 2**20),
+        name="gather_first",
+    )(pack, tokens, segs)
+
+
+def whole(*shape):
+    zeros = (0,) * len(shape)
+    return pl.BlockSpec(shape, lambda *_: zeros)
+
+
+def weight_block(rows, columns, index):
+    return pl.BlockSpec((4, None, rows, columns), lambda z: (0, z, 0, index))
+
+
+def project_kernel(x_ref, gain_ref, shift_ref, bias_ref, near_ref, far_ref, h_ref, out_ref):
+    rows = x_ref.shape[0]
+
+    @pl.when(pl.program_id(0) == 0)
+    def _():
+        for first in range(0, rows, TILE):
+            normed, _ = norm_parts(x_ref[first : first + TILE].astype(jnp.float32))
+            h_ref[first : first + TILE] = (normed * gain_ref[...] + shift_ref[...]).astype(
+                jnp.bfloat16
+            )
+
+    near, far = flat(near_ref), flat(far_ref)
+    for first in range(0, rows, TILE):
+        sums = into_hidden(h_ref[first : first + TILE], near, far) + bias_ref[...]
+        out_ref[first : first + TILE] = sums.astype(jnp.bfloat16)
+
+
+def project(x, gain, shift, bias, near, far, width):
+    rows, model = x.shape
+    groups = near.shape[1]
+    return pl.pallas_call(
+        project_kernel,
+        grid=(groups,),
+        in_specs=[
+            whole(rows, model),
+            whole(1, model),
+            whole(1, model),
+            pl.BlockSpec((None, 1, width), lambda z: (z, 0, 0)),
+            weight_block(WEIGHT_ROWS, width, 0),
+            weight_block(WEIGHT_ROWS, width, 0),
+        ],
+        out_specs=[whole(rows, model), pl.BlockSpec((rows, width), lambda z: (0, z))],
+        out_shape=[
+            jax.ShapeDtypeStruct((rows, model), jnp.bfloat16),
+            jax.ShapeDtypeStruct((rows, groups * width), jnp.bfloat16),
+        ],
+        compiler_params=core_params(),
+        cost_estimate=cost(2 * rows * model * groups * width, 2 * model * groups * width),
+        name="project",
+    )(x, gain, shift, bias, near, far)
+
+
+def mix_out_kernel(
+    o_ref, x_ref, bias_ref, gain_ref, shift_ref, near_ref, far_ref, x1_ref, h_ref
+):
+    groups, width = near_ref.shape[1], near_ref.shape[3]
+    halves = []
+    for weights in (near_ref, far_ref):
+        total = None
+        for z in range(groups):
+            block = weights[:, z].reshape(-1, width)
+            part = dot(o_ref[:, z * width : (z + 1) * width], block, ROWS)
+            total = part if total is None else total + part
+        halves.append(total)
+    residual = x_ref[...].astype(jnp.float32) + jnp.concatenate(halves, axis=1) + bias_ref[...]
+    x1_ref[...] = residual
+    normed, _ = norm_parts(residual)
+    h_ref[...] = (normed * gain_ref[...] + shift_ref[...]).astype(jnp.bfloat16)
+
+
+def mix_out(o, x, bias, gain, shift, near, far, width):
+    rows, model = x.shape
+    groups = near.shape[1]
+    rowed = pl.BlockSpec((TILE, model), lambda r: (r, 0))
+    weights = pl.BlockSpec((4, groups, WEIGHT_ROWS, width), lambda r: (0, 0, 0, 3))
+    return pl.pallas_call(
+        mix_out_kernel,
+        grid=(rows // TILE,),
+        in_specs=[rowed, rowed, whole(1, model), whole(1, model), whole(1, model)] + [weights] * 2,
+        out_specs=[rowed, rowed],
+        out_shape=[
+            jax.ShapeDtypeStruct((rows, model), jnp.float32),
+            jax.ShapeDtypeStruct((rows, model), jnp.bfloat16),
+        ],
+        compiler_params=core_params(),
+        cost_estimate=cost(2 * rows * model * model, 12 * rows * model),
+        name="mix_out",
+    )(o, x, bias, gain, shift, near, far)
+
+
+def expand_kernel(order_ref, h_ref, bias_ref, *refs):
+    near, far = joined(refs[:8])
+    g_ref, slope_ref = refs[8:]
+    root = 0.7978845608028654
+    for first in range(0, h_ref.shape[0], TILE):
+        a = into_hidden(h_ref[first : first + TILE], near, far) + bias_ref[...]
+        square = a * a
+        bent = jnp.tanh(a * (root + (root * 0.044715) * square))
+        half = 0.5 * a
+        g_ref[first : first + TILE] = (half + half * bent).astype(jnp.bfloat16)
+        inner = root + (3.0 * root * 0.044715) * square
+        slope_ref[first : first + TILE] = (
+            0.5 + 0.5 * bent + half * (1.0 - bent * bent) * inner
+        ).astype(jnp.bfloat16)
+
+
+def expand(order, h, bias, weights):
+    rows, model = h.shape
+    depth, hidden = weights.shape[2:]
+    groups = bias.shape[0]
+    out = pl.BlockSpec((rows, hidden), lambda z, order: (0, z))
+    return pl.pallas_call(
+        expand_kernel,
+        grid_spec=prefetched(
+            (groups,),
+            [whole(rows, model), pl.BlockSpec((None, 1, hidden), lambda z, order: (z, 0, 0))]
+            + ff_blocks(0, depth, hidden),
+            [out, out],
+        ),
+        out_shape=[jax.ShapeDtypeStruct((rows, groups * hidden), jnp.bfloat16)] * 2,
+        compiler_params=core_params(),
+        cost_estimate=cost(2 * rows * model * groups * hidden, 8 * rows * groups * hidden),
+        name="expand",
+    )(order, h, bias, *[weights] * 8)
+
+
+def contract_kernel(order_ref, g_ref, x1_ref, bias_ref, *refs):
+    step = pl.program_id(0)
+    near, far = joined(refs[:8])
+    out_ref, total_ref = refs[8:]
+    rows, model = total_ref.shape
+    half = model // 2
+
+    @pl.when(step == 0)
+    def _():
+        total_ref[...] = x1_ref[...] + bias_ref[...]
+
+    for first in range(0, rows, TILE):
+        part = g_ref[first : first + TILE]
+        total_ref[first : first + TILE, :half] += dot(part, near, ROWS)
+        total_ref[first : first + TILE, half:] += dot(part, far, ROWS)
+
+    @pl.when(step == pl.num_programs(0) - 1)
+    def _():
+        store_absolute(order_ref, total_ref, out_ref)
+
+
+def store_absolute(order_ref, value_ref, out_ref):
+    span = out_ref.shape[1]
+    for piece in range(out_ref.shape[0]):
+        for block in range(out_ref.shape[2] // WIDE):
+            place = pl.multiple_of(order_ref[block] * WIDE, WIDE)
+            out_ref[order_ref[8 + piece], :, pl.ds(place, WIDE)] = value_ref[
+                piece * span : (piece + 1) * span, block * WIDE : (block + 1) * WIDE
+            ].astype(out_ref.dtype)
+
+
+def contract(order, g, x1, bias, weights, groups):
+    rows, model = x1.shape
+    depth, hidden = weights.shape[2:]
+    return pl.pallas_call(
+        contract_kernel,
+        grid_spec=prefetched(
+            (groups,),
+            [
+                pl.BlockSpec((rows, hidden), lambda z, order: (0, z)),
+                whole(rows, model),
+                whole(1, model),
+            ]
+            + ff_blocks(1, depth, hidden),
+            whole(4, rows // 4, model),
+            [pltpu.VMEM((rows, model), jnp.float32)],
+        ),
+        out_shape=jax.ShapeDtypeStruct((4, rows // 4, model), jnp.bfloat16),
+        compiler_params=core_params(),
+        cost_estimate=cost(2 * rows * model * groups * hidden, 4 * rows * groups * hidden),
+        name="contract",
+    )(order, g, x1, bias, *[weights] * 8)
+
+
+def ff_back_kernel(order_ref, dy_ref, slope_ref, x1_ref, gain_ref, *refs):
+    step = pl.program_id(0)
+    near, far = joined(refs[:8])
+    up_one, up_two = joined(refs[8:16])
+    da_ref, ubias_ref, dx1_ref, dattn_ref, sums_ref, total_ref = refs[16:]
+    rows, model = total_ref.shape
+    half = model // 2
+
+    @pl.when(step == 0)
+    def _():
+        total_ref[...] = jnp.zeros_like(total_ref)
+
+    sums = None
+    for first in range(0, rows, TILE):
+        span = slice(first, first + TILE)
+        da = into_hidden(dy_ref[span], near, far) * slope_ref[span].astype(jnp.float32)
+        da = da.astype(jnp.bfloat16)
+        da_ref[span] = da
+        part = column_sum(da.astype(jnp.float32))
+        sums = part if sums is None else sums + part
+        total_ref[span, :half] += dot(da, up_one, ROWS)
+        total_ref[span, half:] += dot(da, up_two, ROWS)
+    ubias_ref[...] = sums
+
+    @pl.when(step == pl.num_programs(0) - 1)
+    def _():
+        gains = shifts = outs = downs = jnp.zeros((1, model), jnp.float32)
+        for first in range(0, rows, TILE):
+            span = slice(first, first + TILE)
+            normed, scale = norm_parts(x1_ref[span])
+            grad = total_ref[span]
+            dy = dy_ref[span].astype(jnp.float32)
+            gains = gains + column_sum(grad * normed)
+            shifts = shifts + column_sum(grad)
+            downs = downs + column_sum(dy)
+            dx1 = dy + norm_back(grad, normed, scale, gain_ref[...])
+            outs = outs + column_sum(dx1)
+            dx1_ref[span] = dx1
+            dattn_ref[span] = dx1.astype(jnp.bfloat16)
+        sums_ref[...] = jnp.concatenate([outs, gains, shifts, downs], axis=0)
+
+
+def ff_back(order, dy, slope, x1, gain, weights, groups):
+    rows, model = x1.shape
+    depth, hidden = weights.shape[2:]
+    column = pl.BlockSpec((rows, hidden), lambda z, order: (0, z))
+    return pl.pallas_call(
+        ff_back_kernel,
+        grid_spec=prefetched(
+            (groups,),
+            [whole(rows, model), column, whole(rows, model), whole(1, model)]
+            + ff_blocks(1, depth, hidden)
+            + ff_blocks(0, depth, hidden),
+            [
+                column,
+                pl.BlockSpec((None, 1, hidden), lambda z, order: (z, 0, 0)),
+                whole(rows, model),
+                whole(rows, model),
+                whole(4, model),
+            ],
+            [pltpu.VMEM((rows, model), jnp.float32)],
+        ),
+        out_shape=[
+            jax.ShapeDtypeStruct((rows, groups * hidden), jnp.bfloat16),
+            jax.ShapeDtypeStruct((groups, 1, hidden), jnp.float32),
+            jax.ShapeDtypeStruct((rows, model), jnp.float32),
+            jax.ShapeDtypeStruct((rows, model), jnp.bfloat16),
+            jax.ShapeDtypeStruct((4, model), jnp.float32),
+        ],
+        compiler_params=core_params(60),
+        cost_estimate=cost(4 * rows * model * groups * hidden, 8 * rows * groups * hidden),
+        name="ff_back",
+    )(order, dy, slope, x1, gain, *[weights] * 16)
+
+
+def mix_back_kernel(dattn_ref, near_ref, far_ref, out_ref):
+    near, far = flat(near_ref), flat(far_ref)
+    out_ref[...] = into_hidden(dattn_ref[...], near, far).astype(jnp.bfloat16)
+
+
+def mix_back(dattn, near, far, width):
+    rows, model = dattn.shape
+    groups = near.shape[1]
+    return pl.pallas_call(
+        mix_back_kernel,
+        grid=(groups,),
+        in_specs=[whole(rows, model)] + [weight_block(WEIGHT_ROWS, width, 3)] * 2,
+        out_specs=pl.BlockSpec((rows, width), lambda z: (0, z)),
+        out_shape=jax.ShapeDtypeStruct((rows, groups * width), jnp.bfloat16),
+        compiler_params=core_params(),
+        cost_estimate=cost(2 * rows * model * groups * width, 6 * rows * model),
+        name="mix_back",
+    )(dattn, near, far)
+
+
+def project_back_kernel(
+    order_ref,
+    grad_ref,
+    x_ref,
+    dx1_ref,
+    gain_ref,
+    near_ref,
+    far_ref,
+    out_ref,
+    bias_ref,
+    sums_ref,
+    total_ref,
+):
+    step = pl.program_id(0)
+    rows, model = total_ref.shape
+    half = model // 2
+    near, far = flat(near_ref), flat(far_ref)
+
+    @pl.when(step == 0)
+    def _():
+        total_ref[...] = jnp.zeros_like(total_ref)
+
+    sums = None
+    for first in range(0, rows, TILE):
+        span = slice(first, first + TILE)
+        grad = grad_ref[span]
+        part = column_sum(grad.astype(jnp.float32))
+        sums = part if sums is None else sums + part
+        total_ref[span, :half] += dot(grad, near, ROWS)
+        total_ref[span, half:] += dot(grad, far, ROWS)
+    bias_ref[...] = sums
+
+    @pl.when(step == pl.num_programs(0) - 1)
+    def _():
+        gains = shifts = jnp.zeros((1, model), jnp.float32)
+        for first in range(0, rows, TILE):
+            span = slice(first, first + TILE)
+            normed, scale = norm_parts(x_ref[span].astype(jnp.float32))
+            grad = total_ref[span]
+            gains = gains + column_sum(grad * normed)
+            shifts = shifts + column_sum(grad)
+            total_ref[span] = dx1_ref[span] + norm_back(grad, normed, scale, gain_ref[...])
+        sums_ref[...] = jnp.concatenate([gains, shifts], axis=0)
+        store_absolute(order_ref, total_ref, out_ref)
+
+
+def project_back(order, grad, x, dx1, gain, near, far, width):
+    rows, model = x.shape
+    groups = near.shape[1]
+    return pl.pallas_call(
+        project_back_kernel,
+        grid=(groups,),
+        in_specs=[
+            pl.BlockSpec(memory_space=pltpu.SMEM),
+            pl.BlockSpec((rows, width), lambda z: (0, z)),
+            whole(rows, model),
+            whole(rows, model),
+            whole(1, model),
+            weight_block(WEIGHT_ROWS, width, 0),
+            weight_block(WEIGHT_ROWS, width, 0),
+        ],
+        out_specs=[
+            whole(4, rows // 4, model),
+            pl.BlockSpec((None, 1, width), lambda z: (z, 0, 0)),
+            whole(2, model),
+        ],
+        out_shape=[
+            jax.ShapeDtypeStruct((4, rows // 4, model), jnp.bfloat16),
+            jax.ShapeDtypeStruct((groups, 1, width), jnp.float32),
+            jax.ShapeDtypeStruct((2, model), jnp.float32),
+        ],
+        scratch_shapes=[pltpu.VMEM((rows, model), jnp.float32)],
+        compiler_params=core_params(),
+        cost_estimate=cost(2 * rows * model * groups * width, 8 * rows * model),
+        name="project_back",
+    )(order, grad, x, dx1, gain, near, far)
+
+
+def swap(value, axis, bits):
+    count = lax.axis_size(axis)
+    return lax.ppermute(value, axis, [(index, index ^ bits) for index in range(count)])
+
+
+def across_x(value):
+    return swap(value, "dp", 1)
+
+
+def across_y(value):
+    return swap(value, "ctx", 2)
+
+
+def across_core(value):
+    return swap(value, "ctx", 1)
+
+
+def turned(value, axis, flag):
+    return jnp.where(flag == 1, jnp.flip(value, axis), value)
+
+
+def one_sequence(
     tokens,
     segment_ids,
     norm1_gain,
@@ -532,40 +1159,35 @@
 ):
     dps, ctxs, groups = (lax.axis_size(name) for name in ALL)
     owners = dps * ctxs
-    place = lax.axis_index("tensor")
-    seqs_local, span, model = tokens.shape
-    per_group = seqs_local // groups
-    seqs = per_group // ctxs
+    at_x = lax.axis_index("dp")
+    at_ctx = lax.axis_index("ctx")
+    at_z = lax.axis_index("tensor")
+    at_y, at_core = at_ctx // 2, at_ctx % 2
+    span, model = tokens.shape[1:]
     length = span * ctxs
-    rows = seqs * length
     heads = query_bias.shape[0]
     width = heads * HEAD_DIM
     shard = w_query.shape[0]
     hidden = w_up.shape[1]
-    shared = query_bias.shape[1]
-    shared_up = up_bias.shape[1]
-
-    def gather(value):
-        whole = lax.all_gather(value, ALL, axis=0, tiled=False)
-        return whole.reshape((owners, groups) + value.shape)
-
-    def to_sequences(value):
-        mine = lax.dynamic_slice_in_dim(value, place * per_group, per_group, axis=0)
-        mine = mine.reshape((ctxs, seqs) + value.shape[1:])
-        mine = lax.all_to_all(mine, "ctx", split_axis=0, concat_axis=0, tiled=True)
-        return jnp.swapaxes(mine, 0, 1)
-
-    def to_spans(value):
-        mine = jnp.swapaxes(value.reshape(seqs, ctxs, span, model), 0, 1)
-        mine = lax.all_to_all(mine, "ctx", split_axis=0, concat_axis=0, tiled=True)
-        mine = mine.reshape(per_group, span, model)
-        return lax.all_gather(mine, "tensor", axis=0, tiled=True)
-
-    def by_owner(value, columns):
-        return value.reshape(owners, shard, groups, columns).transpose(0, 2, 1, 3)
-
-    def scatter(value):
-        return lax.psum_scatter(value, ALL, scatter_dimension=0, tiled=True)
+    shared, shared_up = query_bias.shape[1], up_bias.shape[1]
+
+    away = jnp.array([0, 4, 2, 6, 1, 5, 3, 7], jnp.int32)
+    order = jnp.concatenate(
+        [away ^ (at_x * ctxs + at_ctx), jnp.arange(4, dtype=jnp.int32) ^ at_ctx, at_z[None]]
+    ).astype(jnp.int32)
+
+    def to_slots(value):
+        mine = lax.dynamic_slice_in_dim(value, at_z * ctxs, ctxs, axis=0)
+        return [
+            lax.dynamic_index_in_dim(mine, at_ctx ^ bits, 0, keepdims=False)
+            for bits in range(ctxs)
+        ]
+
+    def exchanged(slots):
+        return jnp.stack([slots[0]] + [swap(slots[bits], "ctx", bits) for bits in (1, 2, 3)])
+
+    def to_spans(pieces):
+        return place_slots(order, lax.all_gather(pieces, "tensor", axis=0, tiled=True))
 
     small = jnp.concatenate(
         [
@@ -580,134 +1202,160 @@
             up_bias.reshape(-1),
         ]
     )
-    first_pack = jnp.concatenate([w_query, w_key, w_value, w_out.T], axis=1)
-    pack_width = first_pack.shape[1]
-    extra = -(-small.shape[0] // (16 * pack_width)) * 16
-    small = jnp.pad(small, (0, extra * pack_width - small.shape[0])).reshape(extra, pack_width)
-    first_pack = gather(jnp.concatenate([first_pack, small], axis=0))
-    small = first_pack[:, :, shard:].reshape(owners, groups, extra * pack_width)
-    first_pack = first_pack[:, :, :shard]
-    second_pack = gather(jnp.stack([w_up, w_down.T]))
-    vectors = small[:, 0, : 6 * shard].reshape(owners, 6, shard).transpose(1, 0, 2)
-    vectors = vectors.reshape(6, model).astype(jnp.float32)
+    used = small.shape[0]
+    lanes = -(-used // (16 * 1024)) * 16 * 1024
+    kept = -(-used // WIDE) * WIDE
+    small = jnp.pad(small, (0, lanes - used)).reshape(-1, 1024)
+    pack = jnp.concatenate([w_query, w_key, w_value, w_out.T], axis=1)
+    cut = shard // 2
+    pack = jnp.concatenate([pack, small], axis=0)
+    lines = -(-span // 1024) * 8
+    segs = jnp.pad(segment_ids, ((0, 0), (0, lines * WIDE - span))).reshape(-1, lines, WIDE)
+    near, far, pieces, segs = gather_first(pack, tokens, segs, cut)
+    small = jnp.stack([near[..., shard : shard + 16, :], far[..., shard : shard + 16, :]])
+    small = small.reshape(2, 2, 2, groups, lanes)[..., :kept]
+    pack_near, pack_far = (part.reshape((4,) + part.shape[2:]) for part in (near, far))
+    segs = segs.reshape(2, 2, -1)[:, :, :span]
+    segs = turned(turned(segs, 0, at_y), 1, at_core)
+    weights = lax.all_gather(jnp.stack([w_up, w_down.T]), ALL, axis=0, tiled=False)
+
+    vectors = small[:, :, :, 0, : 6 * shard].reshape(owners, 6, shard)
+    vectors = vectors.transpose(1, 0, 2).reshape(6, 1, model).astype(jnp.float32)
+    biases = turned(turned(turned(small, 0, at_core), 1, at_y), 2, at_x)
+    biases = biases.transpose(2, 1, 0, 3, 4).reshape(owners, groups, kept)
     gain_one, shift_one, bias_out, gain_two, shift_two, bias_down = (
         vectors[index] for index in range(6)
     )
 
     def heads_bias(first, columns):
-        part = small[:, :, first : first + heads * columns]
+        part = biases[:, :, first : first + heads * columns]
         part = part.reshape(owners, groups, heads, columns).transpose(1, 2, 0, 3)
-        return part.reshape(groups, heads * columns * owners).astype(jnp.float32)
-
-    bias_first = 6 * shard
-    bias_query = heads_bias(bias_first, shared)
-    bias_value = heads_bias(bias_first + heads * shared, shared)
-    bias_up = heads_bias(bias_first + 2 * heads * shared, shared_up).reshape(-1)
-    bias_qkv = jnp.stack([bias_query, jnp.zeros_like(bias_query), bias_value], axis=1).reshape(-1)
-
-    full_qkv = first_pack[..., : 3 * width].transpose(0, 2, 1, 3)
-    full_qkv = full_qkv.reshape(model, groups * 3 * width)
-    turned_out = first_pack[..., 3 * width :].transpose(0, 2, 1, 3).reshape(model, groups * width)
-    full_up = second_pack[:, :, 0].transpose(0, 2, 1, 3).reshape(model, groups * hidden)
-    turned_down = second_pack[:, :, 1].transpose(0, 2, 1, 3).reshape(model, groups * hidden)
-
-    inputs_low = to_sequences(tokens)
-    segs = to_sequences(segment_ids)
-    cotangent = to_sequences(out_grad).reshape(rows, model)
-    seg_row = segs.reshape(seqs, 1, length)
-    seg_col = segs.reshape(seqs, length, 1)
-    slopes = jnp.exp2(-8.0 * jnp.arange(1, HEADS + 1).astype(jnp.float32) / HEADS)
-
-    inputs = inputs_low.reshape(rows, model).astype(jnp.float32)
-    normed_one = layer_norm(inputs, gain_one, shift_one).astype(jnp.bfloat16)
-    qkv = (matmul(normed_one, full_qkv) + bias_qkv).astype(jnp.bfloat16)
-    qkv = qkv.reshape(seqs, length, groups * 3 * width)
+        return part.reshape(groups, 1, heads * columns * owners).astype(jnp.float32)
+
+    first = 6 * shard
+    bias_query = heads_bias(first, shared)
+    bias_value = heads_bias(first + heads * shared, shared)
+    bias_up = heads_bias(first + 2 * heads * shared, shared_up)
+    bias_qkv = jnp.concatenate([bias_query, jnp.zeros_like(bias_query), bias_value], axis=2)
+
+    seg_row = segs.reshape(1, 1, length)
+    seg_col = segs.reshape(1, length, 1)
+    head_place = (jnp.arange(groups)[:, None] ^ at_z) * heads + jnp.arange(heads)[None]
+    slopes = jnp.exp2(-8.0 * (head_place.reshape(-1) + 1).astype(jnp.float32) / HEADS)
+
+    x = order_pieces(order, pieces)
+    h1, qkv = project(x, gain_one, shift_one, bias_qkv, pack_near, pack_far, 3 * width)
+    grad_slots, qkv = lax.optimization_barrier((to_slots(out_grad), qkv))
+    qkv = qkv.reshape(1, length, groups * 3 * width)
     mixed, log_total = attend(slopes, seg_row, seg_col, qkv, groups, heads)
-    mixed = mixed.reshape(rows, groups * width)
-    residual = inputs + matmul_right(mixed, turned_out) + bias_out
-    normed_two = layer_norm(residual, gain_two, shift_two).astype(jnp.bfloat16)
-    pre_act = matmul(normed_two, full_up) + bias_up
-    activated = gelu_tanh(pre_act).astype(jnp.bfloat16)
-    result = (residual + matmul_right(activated, turned_down) + bias_down).astype(jnp.bfloat16)
-    outputs = to_spans(result.reshape(seqs, length, model))
-
-    act_grad = matmul(cotangent, turned_down)
-    unused, gelu_pull = jax.vjp(gelu_tanh, pre_act)
-    pre_grad = gelu_pull(act_grad)[0].astype(jnp.bfloat16)
-    grad_down = matmul_left(cotangent, activated).astype(jnp.bfloat16)
-    grad_ubias = jnp.sum(pre_grad.astype(jnp.float32), axis=0)
-    grad_up = matmul_left(normed_two, pre_grad).astype(jnp.bfloat16)
-    grad_ff = jnp.stack([by_owner(grad_up, hidden), by_owner(grad_down, hidden)], axis=2)
-    grad_ff, outputs = lax.optimization_barrier((grad_ff, outputs))
-    sum_ff = scatter(grad_ff.reshape(-1, hidden)).astype(jnp.float32)
-    sum_up = sum_ff[:shard]
-    sum_down = sum_ff[shard:].T
-    normed_two_back = matmul_right(pre_grad, full_up)
-    unused, norm_pull = jax.vjp(layer_norm, residual, gain_two, shift_two)
-    resid_grad, gain_two_grad, shift_two_grad = norm_pull(normed_two_back)
-    cot_rows = cotangent.astype(jnp.float32)
-    resid_grad = resid_grad + cot_rows
-    attn_grad = resid_grad.astype(jnp.bfloat16)
-    mixed_grad = matmul(attn_grad, turned_out).astype(jnp.bfloat16)
-    grad_wout = matmul_left(attn_grad, mixed).astype(jnp.bfloat16)
-    qkv_grad = attend_back(
+    mixed = mixed.reshape(length, groups * width)
+    x1, h2 = mix_out(mixed, x, bias_out, gain_two, shift_two, pack_near, pack_far, width)
+    activated, gelu_slope = expand(order, h2, bias_up, weights)
+    result = contract(order, activated, x1, bias_down, weights, groups)
+
+    def away(left, right):
+        return matmul_left(left[:, left.shape[1] // 2 :], right).astype(jnp.bfloat16)
+
+    def home(left, right):
+        return matmul_left(left[:, : left.shape[1] // 2], right)
+
+    def add(here, there):
+        total = here.astype(jnp.float32) + there.astype(jnp.float32)
+        return total.astype(there.dtype)
+
+    def over_xy(total, x_first, depth):
+        total = total.reshape(2, 2, depth, -1)
+        if x_first:
+            total = add(total[:, 0], across_x(total[:, 1]))
+            return add(total[0], across_y(total[1]))
+        total = add(total[0], across_y(total[1]))
+        return add(total[0], across_x(total[1]))
+
+    def over_z(total):
+        columns = total.shape[1] // groups
+        result = total[:, :columns].astype(jnp.float32)
+        for bits in (1, 2, 3):
+            part = total[:, bits * columns : (bits + 1) * columns]
+            result = result + swap(part, "tensor", bits).astype(jnp.float32)
+        return result
+
+    dy = order_pieces(order, exchanged(grad_slots))
+    dy, result, activated = lax.optimization_barrier((dy, result, activated))
+    result = exchanged(list(result))
+    away_down = away(dy, activated)
+    home_down = home(dy, activated).astype(jnp.bfloat16)
+    dy, result, away_down, home_down = lax.optimization_barrier(
+        (dy, result, away_down, home_down)
+    )
+    outputs = to_spans(result)
+    da, grad_ubias, dx1, dattn, sums_two = ff_back(
+        order, dy, gelu_slope, x1, gain_two, weights, groups
+    )
+
+    from_core = across_core(away_down)
+    dattn, da, from_core = lax.optimization_barrier((dattn, da, from_core))
+    down = add(home_down, from_core).reshape(2, 2, shard, -1)
+    away_up = away(h2, da)
+    from_core = across_core(away_up)
+    do = mix_back(dattn, pack_near, pack_far, width)
+    up = add(home(h2, da), from_core).reshape(2, 2, shard, -1)
+    do, down, up = lax.optimization_barrier((do, down, up))
+    down_part, up_part = across_y(down[1]), across_x(up[:, 1])
+    dqkv = attend_back(
         slopes,
         seg_row,
         seg_col,
         qkv,
-        mixed_grad.reshape(seqs, length, groups * width),
+        do.reshape(1, length, groups * width),
         log_total,
         groups,
         heads,
-    ).reshape(rows, groups * 3 * width)
-    normed_one_back = matmul_right(qkv_grad, full_qkv)
-    unused, first_pull = jax.vjp(layer_norm, inputs, gain_one, shift_one)
-    input_grad, gain_one_grad, shift_one_grad = first_pull(normed_one_back)
-    input_grad = (input_grad + resid_grad).astype(jnp.bfloat16)
-    tokens_grad = to_spans(input_grad.reshape(seqs, length, model))
-    grad_qkv = matmul_left(normed_one, qkv_grad).astype(jnp.bfloat16)
-    grad_pack = jnp.concatenate(
-        [by_owner(grad_qkv, 3 * width), by_owner(grad_wout, width)], axis=3
-    )
-    grad_bias = jnp.sum(qkv_grad.astype(jnp.float32), axis=0).reshape(groups, 3, heads, HEAD_DIM)
-
-    grad_vectors = jnp.stack(
-        [
-            gain_one_grad,
-            shift_one_grad,
-            jnp.sum(resid_grad, axis=0),
-            gain_two_grad,
-            shift_two_grad,
-            jnp.sum(cot_rows, axis=0),
-        ]
-    )
+    ).reshape(length, groups * 3 * width)
+    dqkv, down_part, up_part = lax.optimization_barrier((dqkv, down_part, up_part))
+    down, up = add(down[0], down_part), add(up[:, 0], up_part)
+    down_part, up_part = across_x(down[1]), across_y(up[1])
+    pieces_grad, grad_bias, sums_one = project_back(
+        order, dqkv, x, dx1, gain_one, pack_near, pack_far, 3 * width
+    )
+    pieces_grad, down_part, up_part = lax.optimization_barrier((pieces_grad, down_part, up_part))
+    sum_down = over_z(add(down[0], down_part)).T
+    sum_up = over_z(add(up[0], up_part))
+    pieces_grad = exchanged(list(pieces_grad))
+    away_qkv = away(h1, dqkv)
+    away_wout = away(dattn, mixed)
+    pieces_grad, away_qkv, away_wout = lax.optimization_barrier(
+        (pieces_grad, away_qkv, away_wout)
+    )
+    tokens_grad = to_spans(pieces_grad)
+    qkv_sum = add(home(h1, dqkv), across_core(away_qkv))
+    sum_qkv = over_z(over_xy(qkv_sum, True, shard))
+    wout_sum = add(home(dattn, mixed), across_core(away_wout))
+    sum_wout = over_z(over_xy(wout_sum, False, shard)).T
+
+    grad_vectors = jnp.concatenate([sums_one, sums_two], axis=0)
     grad_vectors = grad_vectors.reshape(6, owners, shard).transpose(1, 0, 2)
-    grad_vectors = jnp.broadcast_to(
-        grad_vectors.reshape(owners, 1, 6 * shard), (owners, groups, 6 * shard)
-    )
+    grad_vectors = grad_vectors.reshape(owners, 1, 6 * shard)
+    grad_vectors = jnp.broadcast_to(grad_vectors, (owners, groups, 6 * shard))
 
     def owner_bias(value, columns):
-        value = value.reshape(groups, heads, owners, columns).transpose(2, 0, 1, 3)
+        value = value.reshape(groups, heads, 2, 2, 2, columns).transpose(4, 3, 2, 0, 1, 5)
+        value = turned(turned(turned(value, 0, at_core), 1, at_y), 2, at_x)
         return value.reshape(owners, groups, heads * columns)
 
+    grad_bias = grad_bias.reshape(groups, 3, heads, HEAD_DIM)
     grad_small = jnp.concatenate(
         [
             grad_vectors,
             owner_bias(grad_bias[:, 0], shared),
             owner_bias(grad_bias[:, 2], shared),
             owner_bias(grad_ubias, shared_up),
+            jnp.zeros((owners, groups, kept - used), jnp.float32),
         ],
         axis=2,
     )
-    grad_small = grad_small.astype(jnp.bfloat16)
-    padding = extra * pack_width - grad_small.shape[2]
-    grad_small = jnp.pad(grad_small, ((0, 0), (0, 0), (0, padding)))
-    grad_small = grad_small.reshape(owners, groups, extra, pack_width)
-    grad_pack = jnp.concatenate([grad_pack, grad_small], axis=2)
-    sum_pack = scatter(grad_pack.reshape(-1, pack_width)).astype(jnp.float32)
-    sum_small = sum_pack[shard:].reshape(-1)
-    sum_qkv = sum_pack[:shard, : 3 * width]
-    sum_wout = sum_pack[:shard, 3 * width :].T
+    grad_small = grad_small.reshape(owners, groups * kept)
+    small_sum = add(grad_small[:4], across_core(grad_small[4:]))
+    sum_small = over_z(over_xy(small_sum, True, 1)).reshape(-1)
     sums = sum_small[: 6 * shard].reshape(6, shard)
     sum_biases = sum_small[6 * shard :]
     count = heads * shared
@@ -733,8 +1381,9 @@
 
 
 def choose_plan(tokens, *others):
-    if tokens.shape[0] % (lax.axis_size("ctx") * lax.axis_size("tensor")) == 0:
-        return whole_sequences(tokens, *others)
+    sizes = tuple(lax.axis_size(name) for name in ALL)
+    if sizes == (2, 4, 4) and tokens.shape[0] == 16 and tokens.shape[1] % TILE == 0:
+        return one_sequence(tokens, *others)
     return shards(tokens, *others)
 
 

time: 1190 us -> 693 us (0.58)
  waiting for transfers between devices: 576 us -> 156 us
  Pallas kernels: 84.1 us -> 303 us
  local copies, waits for them, and re-layouts: 248 us -> 54.5 us
  matrix products: 155 us -> 55.1 us
  starting transfers between devices: 17.1 us -> 65.2 us
  blocking collectives: 29 us -> 0 us
  other arithmetic: 49.2 us -> 35.7 us
    reduce_scatter x2 -> x0, waiting for transfers between devices: 365 us -> none  [scatter(): return lax.psum_scatter(value, ALL, scatter_dimension=0, tiled=True)]
    pallas_call x0 -> x12, Pallas kernels: none -> 219 us  [the longest x1 85.2 us: gather_first(): pl.pallas_call(functools.partial(gather_kernel, cut), in_specs=[anywhere]...]
    ppermute x0 -> x39, waiting for transfers between devices: none -> 115 us  [swap(): lax.ppermute(value, axis, [(index, index ^ bits) for index in range(count)])]
    dot_general x8 -> x0, matrix products: 107 us -> none  [the longest x4 60.3 us: matmul(): return jnp.dot(left, right, preferred_element_type=jnp.float32)]
    all_gather x4 -> x3, waiting for transfers between devices: 144 us -> 40.7 us  [the longest x2 40.7 us: to_spans(): lax.all_gather(pieces, 'tensor', axis=0, tiled=True)]
    reshape x17 -> x14, local copies, waits for them, and re-layouts: 95.1 us -> 2.91 us  [the longest x1 0.66 us: one_sequence(): sum_biases[2 * count:2 * count + heads * shared_up]]
    all_to_all x4 -> x0, waiting for transfers between devices: 67.5 us -> none  [the longest x3 67.5 us: to_sequences(): mine = lax.all_to_all(mine, 'ctx', split_axis=0, concat_axis=0, tiled=True)]
    ppermute x0 -> x39, starting transfers between devices: none -> 65.1 us  [swap(): lax.ppermute(value, axis, [(index, index ^ bits) for index in range(count)])]
  transfers between devices with their start and end apart: 10 -> 42, of which waited for: 7 -> 15; matrix products, arithmetic and copies ran while one was open for 29% -> 17% of each run, Pallas kernels for 7% -> 37%
where the time goes in v1:
time: 693 us; the launch traced here: 685 us
  Pallas kernels  303 us (44%)
  waiting for transfers between devices  156 us (23%)
  starting transfers between devices  65.2 us (9%)
  matrix products  55.1 us (8%)
  local copies, waits for them, and re-layouts  54.5 us (8%)
  other arithmetic  35.7 us (5%)
  between operations  15.3 us (2%)
    ppermute x39, waiting for transfers between devices, swap(): lax.ppermute(value, axis, [(index, index ^ bits) for index in range(count)])  115 us
    pallas_call x1, Pallas kernels, gather_first(): pl.pallas_call(functools.partial(gather_kernel, cut), in_specs=[anywhere]...  85.2 us
    ppermute x39, starting transfers between devices, swap(): lax.ppermute(value, axis, [(index, index ^ bits) for index in range(count)])  65.1 us
    dot_general x8, matrix products, matmul_left(): lax.dot_general(left, right, (((0,), (0,)), ((), ())), preferred_element_...  55.1 us
    pallas_call x1, Pallas kernels, attend_back(): pl.pallas_call(functools.partial(attend_back_kernel, heads, block), grid=...  50.5 us
    all_gather x2, waiting for transfers between devices, to_spans(): lax.all_gather(pieces, 'tensor', axis=0, tiled=True)  40.7 us
    pallas_call x1, Pallas kernels, attend(): pl.pallas_call(functools.partial(attend_kernel, heads, block), grid=(seqs...  33.8 us
    pallas_call x1, Pallas kernels, ff_back(): pl.pallas_call(ff_back_kernel, grid_spec=prefetched((groups,), [whole(row...  33.2 us
  transfers between devices with their start and end apart: 42, of which 15 were waited for; matrix products, arithmetic and copies ran while one was open for 17% of the time, Pallas kernels for 37%

profile of v1, /device:TPU:0, one launch (start us, length us, event | category | flops | bytes accessed | tf_op | source)
XLA Modules:
  0.0 685.4 jit_solution(8194600207966576925)
XLA Ops:
  12.5 85.2 %gather_first.1 = (bf16[2,2,4,144,1024]{4,3,2,1,0:T(8,128)(2,1)}, bf16[2,2,4,144,1024]{4,3,2,1,0:T(8,128)(2,1)}, bf16[4,256,1024]{2,1,0:T(8,128)(2,1)}, s32[4,8,128]{2,1,0:T(8,128)}) custom-call(bf16[144,1024]{1,0:T(8,128)(2,1)} %pad_maximum_fusion.4.pack_ref, bf16[16,256,1024]{2,1,0:T(8,128)(2,1)} %tokens_ref.1, s32[16,8,128]{2,1,0:T(8,128)} %bitcast.280), custom_call_target="tpu_custom_call" | custom-call | bytes 134217728 | tf_op jit(solution)/shard_map/gather_first/pallas_call | solution.py:742
  111.2 12.4 %project.1 = (bf16[1024,1024]{1,0:T(8,128)(2,1)}, bf16[1024,3072]{1,0:T(8,128)(2,1)}) custom-call(bf16[1024,1024]{1,0:T(8,128)(2,1)} %copy-done.7, f32[1,1024]{1,0:T(1,128)} %get-tuple-element.151.gain_ref, f32[1,1024]{1,0:T(1,128)} %get-tuple-element.150.shift_ref, f32[4,1,768]{2,1,0:T(1,128)} %pad_maximum_fusion.5.bias_ref, ...), custom_call_target="tpu_custom_call" | custom-call | flops 6442450944 | bytes 6291456 | tf_op jit(solution)/shard_map/project/pallas_call | solution.py:796
  129.9 33.8 %attend.1 = (bf16[1,1024,1024]{2,1,0:T(8,128)(2,1)S(1)}, f32[1,4,4,1024]{3,2,1,0:T(4,128)S(1)}) custom-call(f32[16]{0:T(128)S(1)} %reshape.300.slope_ref, s32[1,1,1024]{2,1,0:T(1,128)S(1)} %reshape.279.row_ref, s32[1,1024,1]{2,1,0:T(8,128)S(1)} %reshape.317.col_ref, bf16[1,1024,3072]{2,1,0:T(8,128)(2,1)S(1)} %bitcast.215), custom_call_target="tpu_custom_call" | custom-call | tf_op jit(solution)/shard_map/attend/pallas_call | solution.py:480
  165.1 7.5 %mix_out.1 = (f32[1024,1024]{1,0:T(8,128)}, bf16[1024,1024]{1,0:T(8,128)(2,1)}) custom-call(bf16[1024,1024]{1,0:T(8,128)(2,1)} %bitcast.217, bf16[1024,1024]{1,0:T(8,128)(2,1)} %copy-done.7, f32[1,1024]{1,0:T(1,128)} %get-tuple-element.149.bias_ref, f32[1,1024]{1,0:T(1,128)} %get-tuple-element.148.gain_ref, f32[1,1024]{1,0:T(1,128)} %get-tuple-element.147.shift_ref, ...), custom_call_target="tpu_custom_call" | custom-call | flops 2147483648 | bytes 12582912 | tf_op jit(solution)/shard_map/mix_out/pallas_call | solution.py:841
  175.5 23.4 %expand.1 = (bf16[1024,4096]{1,0:T(8,128)(2,1)}, bf16[1024,4096]{1,0:T(8,128)(2,1)}) custom-call(s32[13]{0:T(128)} %copy-done.10, bf16[1024,1024]{1,0:T(8,128)(2,1)} %get-tuple-element.75.h_ref, f32[4,1,1024]{2,1,0:T(1,128)} %reshape.301.bias_ref, bf16[32,2,128,1024]{3,2,1,0:T(8,128)(2,1)} %bitcast.221, bf16[32,2,128,1024]{3,2,1,0:T(8,128)(2,1)} %bitcast.222, ...), custom_call_target="tpu_custom_call" | custom-call | flops 8589934592 | bytes 33554432 | tf_op jit(solution)/shard_map/expand/pallas_call | solution.py:877
  198.9 16.9 %contract.1 = bf16[4,256,1024]{2,1,0:T(8,128)(2,1)} custom-call(s32[13]{0:T(128)} %copy-done.10, bf16[1024,4096]{1,0:T(8,128)(2,1)} %get-tuple-element.80.g_ref, f32[1024,1024]{1,0:T(8,128)} %get-tuple-element.77.x1_ref, f32[1,1024]{1,0:T(1,128)} %get-tuple-element.146.bias_ref, bf16[32,2,128,1024]{3,2,1,0:T(8,128)(2,1)} %bitcast.236, ...), custom_call_target="tpu_custom_call" | custom-call | flops 8589934592 | bytes 16777216 | tf_op jit(solution)/shard_map/contract/pallas_call | solution.py:926
  219.6 10.2 %convolution_convert_fusion.1 = bf16[512,4096]{1,0:T(8,128)(2,1)} fusion(bf16[1024,4096]{1,0:T(8,128)(2,1)} %get-tuple-element.80.g_ref, bf16[1024,1024]{1,0:T(8,128)(2,1)S(1)} %order_pieces.3.dy_ref), kind=kOutput, calls=%fused_computation.4 | convolution fusion | flops 4297064448 | bytes 13631488 | tf_op jit(solution)/shard_map/dot_general | solution.py:38
  244.7 33.2 %ff_back.1 = (bf16[1024,4096]{1,0:T(8,128)(2,1)}, f32[4,1,1024]{2,1,0:T(1,128)}, f32[1024,1024]{1,0:T(8,128)}, bf16[1024,1024]{1,0:T(8,128)(2,1)}, f32[4,1024]{1,0:T(4,128)}) custom-call(s32[13]{0:T(128)} %copy-done.10, bf16[1024,1024]{1,0:T(8,128)(2,1)} %copy-done.1, bf16[1024,4096]{1,0:T(8,128)(2,1)} %get-tuple-element.83.slope_ref, ...), custom_call_target="tpu_custom_call" | custom-call | flops 17179869184 | bytes 33554432 | tf_op jit(solution)/shard_map/ff_back/pallas_call | solution.py:992
  278.0 9.5 %convolution_convert_fusion = bf16[512,4096]{1,0:T(8,128)(2,1)} fusion(bf16[1024,4096]{1,0:T(8,128)(2,1)} %get-tuple-element.90, bf16[1024,1024]{1,0:T(8,128)(2,1)S(1)} %copy-done.22), kind=kOutput, calls=%fused_computation.3 | convolution fusion | flops 4297064448 | bytes 13631488 | tf_op jit(solution)/shard_map/dot_general | solution.py:38
  299.9 8.2 %add_convert_fusion = bf16[512,4096]{1,0:T(8,128)(2,1)} fusion(bf16[512,4096]{1,0:T(8,128)(2,1)} %collective-permute-done.7, bf16[1024,4096]{1,0:T(8,128)(2,1)S(1)} %copy-done.40, bf16[1024,1024]{1,0:T(8,128)(2,1)S(1)} %copy-done.22), kind=kOutput, calls=%fused_computation | convolution fusion | flops 4301258752 | bytes 17825792 | tf_op jit(solution)/shard_map/dot_general | solution.py:38
  324.0 50.5 %attend_back.1 = bf16[1,1024,3072]{2,1,0:T(8,128)(2,1)S(1)} custom-call(f32[16]{0:T(128)S(1)} %reshape.300.slope_ref, s32[1,1,1024]{2,1,0:T(1,128)S(1)} %reshape.279.row_ref, s32[1,1024,1]{2,1,0:T(8,128)S(1)} %reshape.317.col_ref, bf16[1,1024,3072]{2,1,0:T(8,128)(2,1)} %bitcast.214, bf16[1,1024,1024]{2,1,0:T(8,128)(2,1)S(1)} %bitcast.216, ...), custom_call_target="tpu_custom_call" | custom-call | tf_op jit(solution)/shard_map/attend_back/pallas_call | solution.py:498
  386.8 17.2 %project_back.1 = (bf16[4,256,1024]{2,1,0:T(8,128)(2,1)}, f32[4,1,768]{2,1,0:T(1,128)}, f32[2,1024]{1,0:T(2,128)}) custom-call(s32[13]{0:T(128)} %copy-done.10, bf16[1024,3072]{1,0:T(8,128)(2,1)} %bitcast.218, bf16[1024,1024]{1,0:T(8,128)(2,1)} %copy-done.7, f32[1024,1024]{1,0:T(8,128)} %get-tuple-element.96.dx1_ref, f32[1,1024]{1,0:T(1,128)} %get-tuple-element.151.gain_ref, ...), custom_call_target="tpu_custom_call" | custom-call | flops 6442450944 | bytes 8388608 | tf_op jit(solution)/shard_map/project_back/pallas_call | solution.py:1090
  407.0 8.3 %convolution_convert_fusion.3 = bf16[512,3072]{1,0:T(8,128)(2,1)} fusion(bf16[1024,3072]{1,0:T(8,128)(2,1)} %bitcast.219, bf16[1024,1024]{1,0:T(8,128)(2,1)} %get-tuple-element.101), kind=kOutput, calls=%fused_computation.6 | convolution fusion | flops 3222798336 | bytes 10485760 | tf_op jit(solution)/shard_map/dot_general | solution.py:38
  419.7 13.1 %collective-permute-done.13 = bf16[256,1024]{1,0:T(8,128)(2,1)S(1)} collective-permute-done((bf16[256,1024]{1,0:T(8,128)(2,1)S(1)}, bf16[256,1024]{1,0:T(8,128)(2,1)S(1)}, u32[]{:S(2)}, u32[]{:S(2)}) %collective-permute-start.13) | collective-permute-done | bytes 524320 | tf_op jit(solution)/shard_map/ppermute | solution.py:1121
  432.9 9.5 %collective-permute-done.14 = bf16[256,1024]{1,0:T(8,128)(2,1)S(1)} collective-permute-done((bf16[256,1024]{1,0:T(8,128)(2,1)S(1)}, bf16[256,1024]{1,0:T(8,128)(2,1)S(1)}, u32[]{:S(2)}, u32[]{:S(2)}) %collective-permute-start.14) | collective-permute-done | bytes 524320 | tf_op jit(solution)/shard_map/ppermute | solution.py:1121
  448.1 9.3 %collective-permute-start.18 = (f32[1,1024]{1,0:T(1,128)S(1)}, f32[1,1024]{1,0:T(1,128)S(1)}, u32[]{:S(2)}, u32[]{:S(2)}) collective-permute-start(f32[1,1024]{1,0:T(1,128)S(1)} %get-tuple-element.154), channel_id=1, source_target_pairs={{0,1},{1,0},{2,3},{3,2},{4,5},{5,4},{6,7},{7,6},{8,9},{9,8},{10,11... | collective-permute-start | bytes 12296 | tf_op jit(solution)/shard_map/ppermute | solution.py:1121
  477.2 7.5 %add_convert_fusion.2 = bf16[512,3072]{1,0:T(8,128)(2,1)S(1)} fusion(bf16[512,3072]{1,0:T(8,128)(2,1)} %collective-permute-done.21, bf16[1024,3072]{1,0:T(8,128)(2,1)} %bitcast.220, bf16[1024,1024]{1,0:T(8,128)(2,1)} %get-tuple-element.101), kind=kOutput, calls=%fused_computation.2 | convolution fusion | flops 3225944064 | bytes 13631488 | tf_op jit(solution)/shard_map/dot_general | solution.py:38
  497.2 9.3 %collective-permute-done.38 = bf16[128,1024]{0,1:T(8,128)(2,1)} collective-permute-done((bf16[128,1024]{0,1:T(8,128)(2,1)}, bf16[128,1024]{0,1:T(8,128)(2,1)}, u32[]{:S(2)}, u32[]{:S(2)}) %collective-permute-start.38) | collective-permute-done | bytes 262176 | tf_op jit(solution)/shard_map/ppermute | solution.py:1121
  511.2 10.6 %collective-permute-done.22 = bf16[2,128,3072]{2,1,0:T(8,128)(2,1)} collective-permute-done((bf16[2,128,3072]{2,1,0:T(8,128)(2,1)}, bf16[2,128,3072]{2,1,0:T(8,128)(2,1)}, u32[]{:S(2)}, u32[]{:S(2)}) %collective-permute-start.22) | collective-permute-done | bytes 1572896 | tf_op jit(solution)/shard_map/ppermute | solution.py:1121
  526.5 25.4 %collective-permute-done.34 = bf16[128,1024]{1,0:T(8,128)(2,1)} collective-permute-done((bf16[128,1024]{1,0:T(8,128)(2,1)}, bf16[128,1024]{1,0:T(8,128)(2,1)}, u32[]{:S(2)}, u32[]{:S(2)}) %collective-permute-start.34) | collective-permute-done | bytes 262176 | tf_op jit(solution)/shard_map/ppermute | solution.py:1121
  565.8 22.9 %collective-permute-start.30 = (bf16[128,256]{0,1:T(8,128)(2,1)S(1)}, bf16[128,256]{0,1:T(8,128)(2,1)S(1)}, u32[]{:S(2)}, u32[]{:S(2)}) collective-permute-start(bf16[128,256]{0,1:T(8,128)(2,1)S(1)} %get-tuple-element.139), channel_id=1, source_target_pairs={{0,1},{1,0},{2,3},{3,2},{4,5},{5,4},{6,7},{7,6},{8,9},{9,8},{10,11... | collective-permute-start | bytes 196616 | tf_op jit(solution)/shard_map/ppermute | solution.py:1121
  601.8 12.0 %collective-permute-done.24 = bf16[128,768]{1,0:T(8,128)(2,1)S(1)} collective-permute-done((bf16[128,768]{1,0:T(8,128)(2,1)S(1)}, bf16[128,768]{1,0:T(8,128)(2,1)S(1)}, u32[]{:S(2)}, u32[]{:S(2)}) %collective-permute-start.24) | collective-permute-done | bytes 196640 | tf_op jit(solution)/shard_map/ppermute | solution.py:1121
  613.9 12.5 %collective-permute-done.25 = bf16[128,768]{1,0:T(8,128)(2,1)S(1)} collective-permute-done((bf16[128,768]{1,0:T(8,128)(2,1)S(1)}, bf16[128,768]{1,0:T(8,128)(2,1)S(1)}, u32[]{:S(2)}, u32[]{:S(2)}) %collective-permute-start.25) | collective-permute-done | bytes 196640 | tf_op jit(solution)/shard_map/ppermute | solution.py:1121
  627.3 40.7 %all-gather.7.cloned.1.call-done.pieces_ref = bf16[16,256,1024]{2,1,0:T(8,128)(2,1)} async-done(((bf16[4,256,1024]{2,1,0:T(8,128)(2,1)}), bf16[16,256,1024]{2,1,0:T(8,128)(2,1)}) %all-gather.7.cloned.1.call-update) | async-done | bytes 8388624 | tf_op jit(solution)/shard_map/all_gather | solution.py:1190
  (317 shorter events, 180.7 us)
Async XLA Ops:
  7.3 168.1 %all-gather.9.cloned.1.call-start = ((), (), s32[]{:S(2)}) async-start(), calls=%async_computation.2 | async-start | bytes 17301504 | tf_op jit(solution)/shard_map/all_gather | solution.py:1220
  10.4 543.6 %all-gather.5.cloned.1.call-start = ((), (), s32[]{:S(2)}) async-start(), calls=%async_computation | async-start | bytes 10485760 | tf_op jit(solution)/shard_map/all_gather | solution.py:1190
  123.7 48.9 %collective-permute-start = (bf16[256,1024]{1,0:T(8,128)(2,1)}, bf16[256,1024]{1,0:T(8,128)(2,1)}, u32[]{:S(2)}, u32[]{:S(2)}) collective-permute-start(bf16[256,1024]{1,0:T(8,128)(2,1)} %get-tuple-element.69), channel_id=1, source_target_pairs={{0,4},{4,0},{8,12},{12,8},{1,5},{5,1},{9,13},{13,9},{2,6},{6,2},{1... | collective-permute-start | bytes 1572872 | tf_op jit(solution)/shard_map/ppermute | solution.py:1121
  124.0 48.6 %collective-permute-start.1 = (bf16[256,1024]{1,0:T(8,128)(2,1)}, bf16[256,1024]{1,0:T(8,128)(2,1)}, u32[]{:S(2)}, u32[]{:S(2)}) collective-permute-start(bf16[256,1024]{1,0:T(8,128)(2,1)} %get-tuple-element.70), channel_id=1, source_target_pairs={{0,8},{4,12},{8,0},{12,4},{1,9},{5,13},{9,1},{13,5},{2,10},{6,14},... | collective-permute-start | bytes 1572872 | tf_op jit(solution)/shard_map/ppermute | solution.py:1121
  124.0 48.6 %collective-permute-start.2 = (bf16[256,1024]{1,0:T(8,128)(2,1)}, bf16[256,1024]{1,0:T(8,128)(2,1)}, u32[]{:S(2)}, u32[]{:S(2)}) collective-permute-start(bf16[256,1024]{1,0:T(8,128)(2,1)} %get-tuple-element.71), channel_id=1, source_target_pairs={{0,12},{4,8},{8,4},{12,0},{1,13},{5,9},{9,5},{13,1},{2,14},{6,10},... | collective-permute-start | bytes 1572872 | tf_op jit(solution)/shard_map/ppermute | solution.py:1121
  244.0 33.9 %collective-permute-start.6 = (bf16[512,4096]{1,0:T(8,128)(2,1)}, bf16[512,4096]{1,0:T(8,128)(2,1)}, u32[]{:S(2)}, u32[]{:S(2)}) collective-permute-start(bf16[512,4096]{1,0:T(8,128)(2,1)} %convolution_convert_fusion.2), channel_id=1, source_target_pairs={{0,4},{4,0},{8,12},{12,8},{1,5},{5,1},{9,13},{13,9},{2,6},{6,2},{1... | collective-permute-start | bytes 12582920 | tf_op jit(solution)/shard_map/ppermute | solution.py:1121
  287.6 380.4 %all-gather.7.cloned.1.call-start = ((), (), s32[]{:S(2)}) async-start(), calls=%async_computation.1 | async-start | bytes 10485760 | tf_op jit(solution)/shard_map/all_gather | solution.py:1190
  317.7 56.8 %collective-permute-start.8 = (bf16[2,128,4096]{1,2,0:T(8,128)(2,1)}, bf16[2,128,4096]{1,2,0:T(8,128)(2,1)}, u32[]{:S(2)}, u32[]{:S(2)}) collective-permute-start(bf16[2,128,4096]{1,2,0:T(8,128)(2,1)} %slice_bitcast_fusion.3), channel_id=1, source_target_pairs={{0,8},{4,12},{8,0},{12,4},{1,9},{5,13},{9,1},{13,5},{2,10},{6,14},... | collective-permute-start | bytes 6291464 | tf_op jit(solution)/shard_map/ppermute | solution.py:1121
  319.6 54.9 %collective-permute-start.9 = (bf16[2,128,4096]{2,1,0:T(8,128)(2,1)}, bf16[2,128,4096]{2,1,0:T(8,128)(2,1)}, u32[]{:S(2)}, u32[]{:S(2)}) collective-permute-start(bf16[2,128,4096]{2,1,0:T(8,128)(2,1)} %slice_bitcast_fusion.2), channel_id=1, source_target_pairs={{0,16},{16,0},{1,17},{17,1},{2,18},{18,2},{3,19},{19,3},{4,20},{20... | collective-permute-start | bytes 6291464 | tf_op jit(solution)/shard_map/ppermute | solution.py:1121
  379.8 35.7 %collective-permute-start.11 = (bf16[128,4096]{1,0:T(8,128)(2,1)}, bf16[128,4096]{1,0:T(8,128)(2,1)S(1)}, u32[]{:S(2)}, u32[]{:S(2)}) collective-permute-start(bf16[128,4096]{1,0:T(8,128)(2,1)} %slice_bitcast_fusion.8), channel_id=1, source_target_pairs={{0,8},{4,12},{8,0},{12,4},{1,9},{5,13},{9,1},{13,5},{2,10},{6,14},... | collective-permute-start | bytes 3145736 | tf_op jit(solution)/shard_map/ppermute | solution.py:1121
  384.9 30.5 %collective-permute-start.10 = (bf16[128,4096]{0,1:T(8,128)(2,1)}, bf16[128,4096]{0,1:T(8,128)(2,1)}, u32[]{:S(2)}, u32[]{:S(2)}) collective-permute-start(bf16[128,4096]{0,1:T(8,128)(2,1)} %slice_bitcast_fusion.9), channel_id=1, source_target_pairs={{0,16},{16,0},{1,17},{17,1},{2,18},{18,2},{3,19},{19,3},{4,20},{20... | collective-permute-start | bytes 3145736 | tf_op jit(solution)/shard_map/ppermute | solution.py:1121
  444.6 32.7 %collective-permute-start.21 = (bf16[512,3072]{1,0:T(8,128)(2,1)}, bf16[512,3072]{1,0:T(8,128)(2,1)}, u32[]{:S(2)}, u32[]{:S(2)}) collective-permute-start(bf16[512,3072]{1,0:T(8,128)(2,1)} %convolution_convert_fusion.3), channel_id=1, source_target_pairs={{0,4},{4,0},{8,12},{12,8},{1,5},{5,1},{9,13},{13,9},{2,6},{6,2},{1... | collective-permute-start | bytes 9437192 | tf_op jit(solution)/shard_map/ppermute | solution.py:1121
  468.5 28.0 %collective-permute-start.37 = (bf16[128,1024]{0,1:T(8,128)(2,1)}, bf16[128,1024]{0,1:T(8,128)(2,1)}, u32[]{:S(2)}, u32[]{:S(2)}) collective-permute-start(bf16[128,1024]{0,1:T(8,128)(2,1)} %get-tuple-element.127), channel_id=1, source_target_pairs={{0,2},{1,3},{2,0},{3,1},{4,6},{5,7},{6,4},{7,5},{8,10},{9,11},{10,... | collective-permute-start | bytes 786440 | tf_op jit(solution)/shard_map/ppermute | solution.py:1121
  471.3 35.2 %collective-permute-start.38 = (bf16[128,1024]{0,1:T(8,128)(2,1)}, bf16[128,1024]{0,1:T(8,128)(2,1)}, u32[]{:S(2)}, u32[]{:S(2)}) collective-permute-start(bf16[128,1024]{0,1:T(8,128)(2,1)} %get-tuple-element.126), channel_id=1, source_target_pairs={{0,3},{1,2},{2,1},{3,0},{4,7},{5,6},{6,5},{7,4},{8,11},{9,10},{10,... | collective-permute-start | bytes 786440 | tf_op jit(solution)/shard_map/ppermute | solution.py:1121
  475.8 34.3 %collective-permute-start.28 = (bf16[2,128,1024]{1,2,0:T(8,128)(2,1)}, bf16[2,128,1024]{1,2,0:T(8,128)(2,1)}, u32[]{:S(2)}, u32[]{:S(2)}) collective-permute-start(bf16[2,128,1024]{1,2,0:T(8,128)(2,1)} %copy.164), channel_id=1, source_target_pairs={{0,8},{4,12},{8,0},{12,4},{1,9},{5,13},{9,1},{13,5},{2,10},{6,14},... | collective-permute-start | bytes 1572872 | tf_op jit(solution)/shard_map/ppermute | solution.py:1121
  486.0 35.8 %collective-permute-start.22 = (bf16[2,128,3072]{2,1,0:T(8,128)(2,1)}, bf16[2,128,3072]{2,1,0:T(8,128)(2,1)}, u32[]{:S(2)}, u32[]{:S(2)}) collective-permute-start(bf16[2,128,3072]{2,1,0:T(8,128)(2,1)} %slice_bitcast_fusion.4), channel_id=1, source_target_pairs={{0,16},{16,0},{1,17},{17,1},{2,18},{18,2},{3,19},{19,3},{4,20},{20... | collective-permute-start | bytes 4718600 | tf_op jit(solution)/shard_map/ppermute | solution.py:1121
  494.9 31.5 %collective-permute-start.33 = (bf16[128,1024]{1,0:T(8,128)(2,1)}, bf16[128,1024]{1,0:T(8,128)(2,1)}, u32[]{:S(2)}, u32[]{:S(2)}) collective-permute-start(bf16[128,1024]{1,0:T(8,128)(2,1)} %get-tuple-element.128), channel_id=1, source_target_pairs={{0,1},{1,0},{2,3},{3,2},{4,5},{5,4},{6,7},{7,6},{8,9},{9,8},{10,11... | collective-permute-start | bytes 786440 | tf_op jit(solution)/shard_map/ppermute | solution.py:1121
  496.5 55.4 %collective-permute-start.34 = (bf16[128,1024]{1,0:T(8,128)(2,1)}, bf16[128,1024]{1,0:T(8,128)(2,1)}, u32[]{:S(2)}, u32[]{:S(2)}) collective-permute-start(bf16[128,1024]{1,0:T(8,128)(2,1)} %get-tuple-element.130), channel_id=1, source_target_pairs={{0,2},{1,3},{2,0},{3,1},{4,6},{5,7},{6,4},{7,5},{8,10},{9,11},{10,... | collective-permute-start | bytes 786440 | tf_op jit(solution)/shard_map/ppermute | solution.py:1121
  506.5 45.4 %collective-permute-start.35 = (bf16[128,1024]{1,0:T(8,128)(2,1)}, bf16[128,1024]{1,0:T(8,128)(2,1)}, u32[]{:S(2)}, u32[]{:S(2)}) collective-permute-start(bf16[128,1024]{1,0:T(8,128)(2,1)} %get-tuple-element.129), channel_id=1, source_target_pairs={{0,3},{1,2},{2,1},{3,0},{4,7},{5,6},{6,5},{7,4},{8,11},{9,10},{10,... | collective-permute-start | bytes 786440 | tf_op jit(solution)/shard_map/ppermute | solution.py:1121
  524.4 66.8 %collective-permute-start.23 = (bf16[128,3072]{1,0:T(8,128)(2,1)S(1)}, bf16[128,3072]{1,0:T(8,128)(2,1)}, u32[]{:S(2)}, u32[]{:S(2)}) collective-permute-start(bf16[128,3072]{1,0:T(8,128)(2,1)S(1)} %slice_bitcast_fusion.10), channel_id=1, source_target_pairs={{0,8},{4,12},{8,0},{12,4},{1,9},{5,13},{9,1},{13,5},{2,10},{6,14},... | collective-permute-start | bytes 2359304 | tf_op jit(solution)/shard_map/ppermute | solution.py:1121
  525.1 39.7 %collective-permute-start.29 = (bf16[128,1024]{0,1:T(8,128)(2,1)S(1)}, bf16[128,1024]{0,1:T(8,128)(2,1)}, u32[]{:S(2)}, u32[]{:S(2)}) collective-permute-start(bf16[128,1024]{0,1:T(8,128)(2,1)S(1)} %slice_bitcast_fusion.18), channel_id=1, source_target_pairs={{0,16},{16,0},{1,17},{17,1},{2,18},{18,2},{3,19},{19,3},{4,20},{20... | collective-permute-start | bytes 786440 | tf_op jit(solution)/shard_map/ppermute | solution.py:1121
  565.8 29.8 %collective-permute-start.30 = (bf16[128,256]{0,1:T(8,128)(2,1)S(1)}, bf16[128,256]{0,1:T(8,128)(2,1)S(1)}, u32[]{:S(2)}, u32[]{:S(2)}) collective-permute-start(bf16[128,256]{0,1:T(8,128)(2,1)S(1)} %get-tuple-element.139), channel_id=1, source_target_pairs={{0,1},{1,0},{2,3},{3,2},{4,5},{5,4},{6,7},{7,6},{8,9},{9,8},{10,11... | collective-permute-start | bytes 196616 | tf_op jit(solution)/shard_map/ppermute | solution.py:1121
  593.7 32.7 %collective-permute-start.25 = (bf16[128,768]{1,0:T(8,128)(2,1)S(1)}, bf16[128,768]{1,0:T(8,128)(2,1)S(1)}, u32[]{:S(2)}, u32[]{:S(2)}) collective-permute-start(bf16[128,768]{1,0:T(8,128)(2,1)S(1)} %get-tuple-element.135), channel_id=1, source_target_pairs={{0,2},{1,3},{2,0},{3,1},{4,6},{5,7},{6,4},{7,5},{8,10},{9,11},{10,... | collective-permute-start | bytes 589832 | tf_op jit(solution)/shard_map/ppermute | solution.py:1121
  595.6 30.8 %collective-permute-start.26 = (bf16[128,768]{1,0:T(8,128)(2,1)S(1)}, bf16[128,768]{1,0:T(8,128)(2,1)S(1)}, u32[]{:S(2)}, u32[]{:S(2)}) collective-permute-start(bf16[128,768]{1,0:T(8,128)(2,1)S(1)} %get-tuple-element.134), channel_id=1, source_target_pairs={{0,3},{1,2},{2,1},{3,0},{4,7},{5,6},{6,5},{7,4},{8,11},{9,10},{10,... | collective-permute-start | bytes 589832 | tf_op jit(solution)/shard_map/ppermute | solution.py:1121
  (65 other events, 721.7 us)
Sparse Core Ops, SparseCore 0:
  11.7 156.4 all-gather.8
  287.7 155.7 all-gather.4
  445.0 222.8 all-gather.6

commit v2 on v1

--- a/solution.py
+++ b/solution.py
@@ -389,31 +389,36 @@
     return lax.dot_general(left, right, dims, preferred_element_type=jnp.float32)
 
 
-def scores_turned(query, key, slope, first, seg_query, seg_key, causal_from):
-    count, block = key.shape[0], query.shape[0]
-    raw = dot(key, query, ROWS) * (1.0 / math.sqrt(HEAD_DIM))
-    key_place = lax.broadcasted_iota(jnp.int32, (count, 1), 0)
-    query_place = first + lax.broadcasted_iota(jnp.int32, (1, block), 1)
-    scores = raw + slope * (key_place - query_place).astype(jnp.float32)
-    allowed = (key_place <= query_place) & (seg_key == seg_query)
-    return jnp.where(allowed, scores, -1e30)
-
-
-def attend_kernel(heads, block, slope_ref, row_ref, col_ref, qkv_ref, o_ref, lse_ref):
+def fill_distances(block, row_ref, col_ref, far_ref):
+    @pl.when(pl.program_id(1) == 0)
+    def _():
+        for index in range(far_ref.shape[0]):
+            first, last = index * block, (index + 1) * block
+            key_place = lax.broadcasted_iota(jnp.int32, (last, 1), 0)
+            query_place = first + lax.broadcasted_iota(jnp.int32, (1, block), 1)
+            allowed = (key_place <= query_place) & (col_ref[0:last, :] == row_ref[:, first:last])
+            distance = (key_place - query_place).astype(jnp.float32)
+            far_ref[index, 0:last, :] = jnp.where(allowed, distance, -1e35)
+
+
+def scaled(query):
+    return (query.astype(jnp.float32) * (1.0 / math.sqrt(HEAD_DIM))).astype(jnp.bfloat16)
+
+
+def attend_kernel(heads, block, slope_ref, row_ref, col_ref, qkv_ref, o_ref, lse_ref, far_ref):
     step = pl.program_id(1)
     length = qkv_ref.shape[0]
     width = heads * HEAD_DIM
+    fill_distances(block, row_ref, col_ref, far_ref)
     for head in range(heads):
         lo = head * HEAD_DIM
         slope = slope_ref[step * heads + head]
         for first in range(0, length, block):
             last = first + block
-            query = qkv_ref[first:last, lo : lo + HEAD_DIM]
+            query = scaled(qkv_ref[first:last, lo : lo + HEAD_DIM])
             key = qkv_ref[0:last, width + lo : width + lo + HEAD_DIM]
             value = qkv_ref[0:last, 2 * width + lo : 2 * width + lo + HEAD_DIM]
-            scores = scores_turned(
-                query, key, slope, first, row_ref[:, first:last], col_ref[0:last, :], first
-            )
+            scores = dot(key, query, ROWS) + slope * far_ref[first // block, 0:last, :]
             highest = jnp.max(scores, axis=0, keepdims=True)
             exponent = jnp.exp(scores - highest)
             totals = jnp.sum(exponent, axis=0, keepdims=True)
@@ -424,24 +429,34 @@
 
 
 def attend_back_kernel(
-    heads, block, slope_ref, row_ref, col_ref, qkv_ref, do_ref, lse_ref, grad_ref, dk_ref, dv_ref
+    heads,
+    block,
+    slope_ref,
+    row_ref,
+    col_ref,
+    qkv_ref,
+    do_ref,
+    lse_ref,
+    grad_ref,
+    dk_ref,
+    dv_ref,
+    far_ref,
 ):
     step = pl.program_id(1)
     length = qkv_ref.shape[0]
     width = heads * HEAD_DIM
     scale = 1.0 / math.sqrt(HEAD_DIM)
+    fill_distances(block, row_ref, col_ref, far_ref)
     for head in range(heads):
         lo = head * HEAD_DIM
         slope = slope_ref[step * heads + head]
         for first in reversed(range(0, length, block)):
             last = first + block
-            query = qkv_ref[first:last, lo : lo + HEAD_DIM]
+            query = scaled(qkv_ref[first:last, lo : lo + HEAD_DIM])
             key = qkv_ref[0:last, width + lo : width + lo + HEAD_DIM]
             value = qkv_ref[0:last, 2 * width + lo : 2 * width + lo + HEAD_DIM]
             mixed_grad = do_ref[first:last, lo : lo + HEAD_DIM]
-            scores = scores_turned(
-                query, key, slope, first, row_ref[:, first:last], col_ref[0:last, :], first
-            )
+            scores = dot(key, query, ROWS) + slope * far_ref[first // block, 0:last, :]
             softmaxed = jnp.exp(scores - lse_ref[head : head + 1, first:last])
             prob_grad = dot(value, mixed_grad, ROWS)
             delta = jnp.sum(softmaxed * prob_grad, axis=0, keepdims=True)
@@ -457,7 +472,7 @@
             else:
                 dk_ref[0:last, :] += key_grad
                 dv_ref[0:last, :] += value_grad
-        grad_ref[:, width + lo : width + lo + HEAD_DIM] = (dk_ref[...] * scale).astype(jnp.bfloat16)
+        grad_ref[:, width + lo : width + lo + HEAD_DIM] = dk_ref[...].astype(jnp.bfloat16)
         grad_ref[:, 2 * width + lo : 2 * width + lo + HEAD_DIM] = dv_ref[...].astype(jnp.bfloat16)
 
 
@@ -486,7 +501,9 @@
             jax.ShapeDtypeStruct((seqs, length, groups * heads * HEAD_DIM), jnp.bfloat16),
             jax.ShapeDtypeStruct((seqs, groups, heads, length), jnp.float32),
         ],
+        scratch_shapes=[pltpu.VMEM((length // block, length, block), jnp.float32)],
         compiler_params=pltpu.CompilerParams(vmem_limit_bytes=40 * 2**20),
+        cost_estimate=cost(4 * qkv.size * length, 4 * qkv.size),
         name="attend",
     )(slopes, seg_row, seg_col, qkv)
 
@@ -504,8 +521,10 @@
         scratch_shapes=[
             pltpu.VMEM((length, HEAD_DIM), jnp.float32),
             pltpu.VMEM((length, HEAD_DIM), jnp.float32),
+            pltpu.VMEM((length // block, length, block), jnp.float32),
         ],
         compiler_params=pltpu.CompilerParams(vmem_limit_bytes=40 * 2**20),
+        cost_estimate=cost(4 * qkv.size * length, 4 * qkv.size),
         name="attend_back",
     )(slopes, seg_row, seg_col, qkv, mixed_grad, log_total)
 
@@ -515,7 +534,9 @@
 
 
 def cost(flops, moved):
-    return pl.CostEstimate(flops=int(flops), bytes_accessed=int(moved), transcendentals=0)
+    return pl.CostEstimate(
+        flops=int(flops) // 64, bytes_accessed=int(moved) // 64, transcendentals=0
+    )
 
 
 TILE = 256
@@ -600,28 +621,40 @@
     )(order, pieces)
 
 
-def place_kernel(order_ref, pieces_ref, out_ref):
-    out_ref[...] = pieces_ref[...]
-
-
-def place_slots(order, pieces):
-    count, span, model = pieces.shape
-
-    def index(z, j, order):
-        return (z * 4 + order[8 + j], 0, 0)
-
+def place_kernel(order_ref, one_ref, two_ref, out_ref):
+    first = order_ref[8 + pl.program_id(1)] < 2
+
+    @pl.when(first)
+    def _():
+        out_ref[...] = one_ref[...]
+
+    @pl.when(jnp.logical_not(first))
+    def _():
+        out_ref[...] = two_ref[...]
+
+
+def place_slots(order, one, two):
+    count, span, model = one.shape
+
+    def index_one(z, j, order):
+        return (z * 2 + jnp.minimum(order[8 + j], 1), 0, 0)
+
+    def index_two(z, j, order):
+        return (z * 2 + jnp.maximum(order[8 + j] - 2, 0), 0, 0)
+
+    block = (None, span, model)
     return pl.pallas_call(
         place_kernel,
         grid_spec=prefetched(
-            (count // 4, 4),
-            [pl.BlockSpec((None, span, model), index)],
-            pl.BlockSpec((None, span, model), lambda z, j, order: (z * 4 + j, 0, 0)),
+            (count // 2, 4),
+            [pl.BlockSpec(block, index_one), pl.BlockSpec(block, index_two)],
+            pl.BlockSpec(block, lambda z, j, order: (z * 4 + j, 0, 0)),
         ),
-        out_shape=jax.ShapeDtypeStruct(pieces.shape, pieces.dtype),
+        out_shape=jax.ShapeDtypeStruct((2 * count, span, model), one.dtype),
         compiler_params=core_params(32),
-        cost_estimate=cost(0, 4 * pieces.size),
+        cost_estimate=cost(0, 8 * one.size),
         name="place_slots",
-    )(order, pieces)
+    )(order, one, two)
 
 
 MESH = pl.DeviceIdType.MESH
@@ -1186,8 +1219,8 @@
     def exchanged(slots):
         return jnp.stack([slots[0]] + [swap(slots[bits], "ctx", bits) for bits in (1, 2, 3)])
 
-    def to_spans(pieces):
-        return place_slots(order, lax.all_gather(pieces, "tensor", axis=0, tiled=True))
+    def over_groups(pieces):
+        return lax.all_gather(pieces, "tensor", axis=0, tiled=True)
 
     small = jnp.concatenate(
         [
@@ -1271,13 +1304,30 @@
         total = add(total[0], across_y(total[1]))
         return add(total[0], across_x(total[1]))
 
-    def over_z(total):
-        columns = total.shape[1] // groups
-        result = total[:, :columns].astype(jnp.float32)
-        for bits in (1, 2, 3):
-            part = total[:, bits * columns : (bits + 1) * columns]
-            result = result + swap(part, "tensor", bits).astype(jnp.float32)
-        return result
+    def over_z(*totals):
+        widths = [total.shape[1] // groups for total in totals]
+        arrived = {}
+        for step in range(1, groups):
+            for sign in (1, -1):
+                place = at_z if sign == 1 else groups - 1 - at_z
+                target = jnp.minimum(groups - step + place, groups - 1)
+                target = target if sign == 1 else groups - 1 - target
+                pairs = [(index, index + 1) for index in range(step)]
+                if sign == -1:
+                    pairs = [(groups - 1 - here, groups - 1 - there) for here, there in pairs]
+                for index, (total, columns) in enumerate(zip(totals, widths)):
+                    part = lax.dynamic_slice_in_dim(
+                        total, (target ^ at_z) * columns, columns, axis=1
+                    )
+                    if step > 1:
+                        part = add(arrived[index, sign], part)
+                    arrived[index, sign] = lax.ppermute(part, "tensor", pairs)
+        return [
+            total[:, :columns].astype(jnp.float32)
+            + arrived[index, 1].astype(jnp.float32)
+            + arrived[index, -1].astype(jnp.float32)
+            for index, (total, columns) in enumerate(zip(totals, widths))
+        ]
 
     dy = order_pieces(order, exchanged(grad_slots))
     dy, result, activated = lax.optimization_barrier((dy, result, activated))
@@ -1287,7 +1337,7 @@
     dy, result, away_down, home_down = lax.optimization_barrier(
         (dy, result, away_down, home_down)
     )
-    outputs = to_spans(result)
+    result_one, result_two = over_groups(result[:2]), over_groups(result[2:])
     da, grad_ubias, dx1, dattn, sums_two = ff_back(
         order, dy, gelu_slope, x1, gain_two, weights, groups
     )
@@ -1295,12 +1345,9 @@
     from_core = across_core(away_down)
     dattn, da, from_core = lax.optimization_barrier((dattn, da, from_core))
     down = add(home_down, from_core).reshape(2, 2, shard, -1)
-    away_up = away(h2, da)
-    from_core = across_core(away_up)
     do = mix_back(dattn, pack_near, pack_far, width)
-    up = add(home(h2, da), from_core).reshape(2, 2, shard, -1)
-    do, down, up = lax.optimization_barrier((do, down, up))
-    down_part, up_part = across_y(down[1]), across_x(up[:, 1])
+    do, down = lax.optimization_barrier((do, down))
+    down_part = across_y(down[1])
     dqkv = attend_back(
         slopes,
         seg_row,
@@ -1311,26 +1358,43 @@
         groups,
         heads,
     ).reshape(length, groups * 3 * width)
-    dqkv, down_part, up_part = lax.optimization_barrier((dqkv, down_part, up_part))
-    down, up = add(down[0], down_part), add(up[:, 0], up_part)
-    down_part, up_part = across_x(down[1]), across_y(up[1])
+    dqkv, down_part, result_one = lax.optimization_barrier((dqkv, down_part, result_one))
+    down = add(down[0], down_part)
+    down_part = across_x(down[1])
     pieces_grad, grad_bias, sums_one = project_back(
         order, dqkv, x, dx1, gain_one, pack_near, pack_far, 3 * width
     )
-    pieces_grad, down_part, up_part = lax.optimization_barrier((pieces_grad, down_part, up_part))
-    sum_down = over_z(add(down[0], down_part)).T
-    sum_up = over_z(add(up[0], up_part))
+    pieces_grad, h2, h1, dattn = lax.optimization_barrier((pieces_grad, h2, h1, dattn))
     pieces_grad = exchanged(list(pieces_grad))
+    away_up = away(h2, da)
     away_qkv = away(h1, dqkv)
     away_wout = away(dattn, mixed)
-    pieces_grad, away_qkv, away_wout = lax.optimization_barrier(
-        (pieces_grad, away_qkv, away_wout)
-    )
-    tokens_grad = to_spans(pieces_grad)
-    qkv_sum = add(home(h1, dqkv), across_core(away_qkv))
-    sum_qkv = over_z(over_xy(qkv_sum, True, shard))
-    wout_sum = add(home(dattn, mixed), across_core(away_wout))
-    sum_wout = over_z(over_xy(wout_sum, False, shard)).T
+    aways = away_up, away_qkv, away_wout
+    pieces_grad, result_two, aways, down_part = lax.optimization_barrier(
+        (pieces_grad, result_two, aways, down_part)
+    )
+    tokens_one, tokens_two = over_groups(pieces_grad[:2]), over_groups(pieces_grad[2:])
+    outputs = place_slots(order, result_one, result_two)
+    from_core = [across_core(part) for part in aways]
+    up = add(home(h2, da), from_core[0]).reshape(2, 2, shard, -1)
+    qkv_sum = add(home(h1, dqkv), from_core[1]).reshape(2, 2, shard, -1)
+    wout_sum = add(home(dattn, mixed), from_core[2]).reshape(2, 2, shard, -1)
+    down = add(down[0], down_part)
+    up, qkv_sum, wout_sum, down = lax.optimization_barrier((up, qkv_sum, wout_sum, down))
+    moved = across_x(up[:, 1]), across_y(qkv_sum[1]), across_y(wout_sum[1])
+    (sum_down,) = over_z(down)
+    sum_down = sum_down.T
+    moved, sum_down = lax.optimization_barrier((moved, sum_down))
+    up, qkv_sum, wout_sum = (
+        add(up[:, 0], moved[0]),
+        add(qkv_sum[0], moved[1]),
+        add(wout_sum[0], moved[2]),
+    )
+    moved = across_y(up[1]), across_x(qkv_sum[1]), across_x(wout_sum[1])
+    sum_up, sum_qkv, sum_wout = over_z(
+        add(up[0], moved[0]), add(qkv_sum[0], moved[1]), add(wout_sum[0], moved[2])
+    )
+    sum_wout = sum_wout.T
 
     grad_vectors = jnp.concatenate([sums_one, sums_two], axis=0)
     grad_vectors = grad_vectors.reshape(6, owners, shard).transpose(1, 0, 2)
@@ -1354,8 +1418,13 @@
         axis=2,
     )
     grad_small = grad_small.reshape(owners, groups * kept)
+    grad_small, sum_down = lax.optimization_barrier((grad_small, sum_down))
     small_sum = add(grad_small[:4], across_core(grad_small[4:]))
-    sum_small = over_z(over_xy(small_sum, True, 1)).reshape(-1)
+    sum_small = over_z(over_xy(small_sum, True, 1))[0].reshape(-1)
+    tokens_one, tokens_two, sum_up, sum_qkv, sum_wout, sum_small = lax.optimization_barrier(
+        (tokens_one, tokens_two, sum_up, sum_qkv, sum_wout, sum_small)
+    )
+    tokens_grad = place_slots(order, tokens_one, tokens_two)
     sums = sum_small[: 6 * shard].reshape(6, shard)
     sum_biases = sum_small[6 * shard :]
     count = heads * shared

time: 693 us -> 647 us (0.934)
  waiting for transfers between devices: 156 us -> 85.4 us
  starting transfers between devices: 65.2 us -> 103 us
  Pallas kernels: 303 us -> 289 us
    ppermute x39 -> x24, waiting for transfers between devices: 115 us -> 29.9 us  [swap(): lax.ppermute(value, axis, [(index, index ^ bits) for index in range(count)])]
    ppermute x0 -> x30, starting transfers between devices: none -> 81.6 us  [over_z(): arrived[index, sign] = lax.ppermute(part, 'tensor', pairs)]
    ppermute x39 -> x24, starting transfers between devices: 65.1 us -> 20.8 us  [swap(): lax.ppermute(value, axis, [(index, index ^ bits) for index in range(count)])]
    ppermute x0 -> x30, waiting for transfers between devices: none -> 38.1 us  [over_z(): arrived[index, sign] = lax.ppermute(part, 'tensor', pairs)]
    all_gather x2 -> x4, waiting for transfers between devices: 40.7 us -> 15.6 us  [over_groups(): return lax.all_gather(pieces, 'tensor', axis=0, tiled=True)]
    pallas_call x1, Pallas kernels: 33.8 us -> 23.6 us  [attend(): pl.pallas_call(functools.partial(attend_kernel, heads, block), grid=(seqs...]
    unnamed x104 -> x132, local copies, waits for them, and re-layouts: 16.7 us -> 23.4 us
    convert_element_type x9 -> x18, other arithmetic: 20.5 us -> 23.3 us  [add(): return total.astype(there.dtype)]
  transfers between devices with their start and end apart: 42 -> 59, of which waited for: 15 -> 16; matrix products, arithmetic and copies ran while one was open for 17% -> 19% of each run, Pallas kernels for 37% -> 38%
where the time goes in v2:
time: 647 us; the launch traced here: 642 us
  Pallas kernels  289 us (45%)
  starting transfers between devices  103 us (16%)
  waiting for transfers between devices  85.4 us (13%)
  local copies, waits for them, and re-layouts  60.7 us (9%)
  matrix products  52.9 us (8%)
  other arithmetic  34.8 us (5%)
  between operations  16 us (2%)
    pallas_call x1, Pallas kernels, gather_first(): pl.pallas_call(functools.partial(gather_kernel, cut), in_specs=[anywhere]...  85.2 us
    ppermute x30, starting transfers between devices, over_z(): arrived[index, sign] = lax.ppermute(part, 'tensor', pairs)  81.6 us
    dot_general x8, matrix products, matmul_left(): lax.dot_general(left, right, (((0,), (0,)), ((), ())), preferred_element_...  52.9 us
    pallas_call x1, Pallas kernels, attend_back(): pl.pallas_call(functools.partial(attend_back_kernel, heads, block), grid=...  46.4 us
    ppermute x30, waiting for transfers between devices, over_z(): arrived[index, sign] = lax.ppermute(part, 'tensor', pairs)  38.1 us
    pallas_call x1, Pallas kernels, ff_back(): pl.pallas_call(ff_back_kernel, grid_spec=prefetched((groups,), [whole(row...  32.9 us
    ppermute x24, waiting for transfers between devices, swap(): lax.ppermute(value, axis, [(index, index ^ bits) for index in range(count)])  29.9 us
    pallas_call x1, Pallas kernels, attend(): pl.pallas_call(functools.partial(attend_kernel, heads, block), grid=(seqs...  23.6 us
  transfers between devices with their start and end apart: 59, of which 16 were waited for; matrix products, arithmetic and copies ran while one was open for 19% of the time, Pallas kernels for 38%

profile of v2, /device:TPU:0, one launch (start us, length us, event | category | flops | bytes accessed | tf_op | source)
XLA Modules:
  0.0 641.7 jit_solution(17146402743684486304)
XLA Ops:
  12.5 85.2 %gather_first.1 = (bf16[2,2,4,144,1024]{4,3,2,1,0:T(8,128)(2,1)}, bf16[2,2,4,144,1024]{4,3,2,1,0:T(8,128)(2,1)}, bf16[4,256,1024]{2,1,0:T(8,128)(2,1)}, s32[4,8,128]{2,1,0:T(8,128)}) custom-call(bf16[144,1024]{1,0:T(8,128)(2,1)} %pad_maximum_fusion.4.pack_ref, bf16[16,256,1024]{2,1,0:T(8,128)(2,1)} %tokens_ref.1, s32[16,8,128]{2,1,0:T(8,128)} %bitcast.269), custom_call_target="tpu_custom_call" | custom-call | bytes 2097152 | tf_op jit(solution)/shard_map/gather_first/pallas_call | solution.py:775
  109.0 12.8 %project.1 = (bf16[1024,1024]{1,0:T(8,128)(2,1)}, bf16[1024,3072]{1,0:T(8,128)(2,1)}) custom-call(bf16[1024,1024]{1,0:T(8,128)(2,1)} %copy-done, f32[1,1024]{1,0:T(1,128)} %get-tuple-element.199.gain_ref, f32[1,1024]{1,0:T(1,128)} %get-tuple-element.198.shift_ref, f32[4,1,768]{2,1,0:T(1,128)} %pad_maximum_fusion.5.bias_ref, ...), custom_call_target="tpu_custom_call" | custom-call | flops 100663296 | bytes 98304 | tf_op jit(solution)/shard_map/project/pallas_call | solution.py:829
  130.5 23.6 %attend.1 = (bf16[1,1024,1024]{2,1,0:T(8,128)(2,1)S(1)}, f32[1,4,4,1024]{3,2,1,0:T(4,128)S(1)}) custom-call(f32[16]{0:T(128)S(1)} %reshape.310.slope_ref, s32[1,1,1024]{2,1,0:T(1,128)S(1)} %reshape.287.row_ref, s32[1,1024,1]{2,1,0:T(8,128)S(1)} %reshape.329.col_ref, bf16[1,1024,3072]{2,1,0:T(8,128)(2,1)S(1)} %bitcast.199), custom_call_target="tpu_custom_call" | custom-call | flops 201326592 | bytes 196608 | tf_op jit(solution)/shard_map/attend/pallas_call | solution.py:495
  155.5 8.0 %mix_out.1 = (f32[1024,1024]{1,0:T(8,128)}, bf16[1024,1024]{1,0:T(8,128)(2,1)}) custom-call(bf16[1024,1024]{1,0:T(8,128)(2,1)} %bitcast.205, bf16[1024,1024]{1,0:T(8,128)(2,1)} %copy-done, f32[1,1024]{1,0:T(1,128)} %get-tuple-element.197.bias_ref, f32[1,1024]{1,0:T(1,128)} %get-tuple-element.196.gain_ref, f32[1,1024]{1,0:T(1,128)} %get-tuple-element.195.shift_ref, ...), custom_call_target="tpu_custom_call" | custom-call | flops 33554432 | bytes 196608 | tf_op jit(solution)/shard_map/mix_out/pallas_call | solution.py:874
  167.8 22.9 %expand.1 = (bf16[1024,4096]{1,0:T(8,128)(2,1)}, bf16[1024,4096]{1,0:T(8,128)(2,1)}) custom-call(s32[13]{0:T(128)} %copy-done.14, bf16[1024,1024]{1,0:T(8,128)(2,1)} %get-tuple-element.118.h_ref, f32[4,1,1024]{2,1,0:T(1,128)} %reshape.313.bias_ref, bf16[32,2,128,1024]{3,2,1,0:T(8,128)(2,1)} %bitcast.207, bf16[32,2,128,1024]{3,2,1,0:T(8,128)(2,1)} %bitcast.208, ...), custom_call_target="tpu_custom_call" | custom-call | flops 134217728 | bytes 524288 | tf_op jit(solution)/shard_map/expand/pallas_call | solution.py:910
  190.8 16.8 %contract.1 = bf16[4,256,1024]{2,1,0:T(8,128)(2,1)} custom-call(s32[13]{0:T(128)} %copy-done.14, bf16[1024,4096]{1,0:T(8,128)(2,1)} %get-tuple-element.99.g_ref, f32[1024,1024]{1,0:T(8,128)} %get-tuple-element.96.x1_ref, f32[1,1024]{1,0:T(1,128)} %get-tuple-element.194.bias_ref, bf16[32,2,128,1024]{3,2,1,0:T(8,128)(2,1)} %bitcast.222, ...), custom_call_target="tpu_custom_call" | custom-call | flops 134217728 | bytes 262144 | tf_op jit(solution)/shard_map/contract/pallas_call | solution.py:959
  211.2 10.0 %convolution_convert_fusion.1 = bf16[512,4096]{1,0:T(8,128)(2,1)} fusion(bf16[1024,4096]{1,0:T(8,128)(2,1)} %get-tuple-element.99.g_ref, bf16[1024,1024]{1,0:T(8,128)(2,1)S(1)} %order_pieces.3.dy_ref), kind=kOutput, calls=%fused_computation.4 | convolution fusion | flops 4297064448 | bytes 13631488 | tf_op jit(solution)/shard_map/dot_general | solution.py:38
  221.3 6.7 %convolution_convert_fusion.2 = bf16[512,4096]{1,0:T(8,128)(2,1)} fusion(bf16[1024,4096]{1,0:T(8,128)(2,1)S(1)} %bitcast.249, bf16[1024,1024]{1,0:T(8,128)(2,1)S(1)} %order_pieces.3.dy_ref), kind=kOutput, calls=%fused_computation.5 | convolution fusion | flops 4297064448 | bytes 13631488 | tf_op jit(solution)/shard_map/dot_general | solution.py:38
  228.0 6.5 %collective-permute-done.5 = bf16[256,1024]{1,0:T(8,128)(2,1)S(1)} collective-permute-done((bf16[256,1024]{1,0:T(8,128)(2,1)S(1)}, bf16[256,1024]{1,0:T(8,128)(2,1)S(1)}, u32[]{:S(2)}, u32[]{:S(2)}) %collective-permute-start.5) | collective-permute-done | bytes 524320 | tf_op jit(solution)/shard_map/ppermute | solution.py:1154
  236.7 32.9 %ff_back.1 = (bf16[1024,4096]{1,0:T(8,128)(2,1)}, f32[4,1,1024]{2,1,0:T(1,128)}, f32[1024,1024]{1,0:T(8,128)}, bf16[1024,1024]{1,0:T(8,128)(2,1)}, f32[4,1024]{1,0:T(4,128)}) custom-call(s32[13]{0:T(128)} %copy-done.14, bf16[1024,1024]{1,0:T(8,128)(2,1)} %copy-done.5, bf16[1024,4096]{1,0:T(8,128)(2,1)} %get-tuple-element.101.slope_ref, ...), custom_call_target="tpu_custom_call" | custom-call | flops 268435456 | bytes 524288 | tf_op jit(solution)/shard_map/ff_back/pallas_call | solution.py:1025
  281.8 6.4 copy.141
  292.5 46.4 %attend_back.1 = bf16[1,1024,3072]{2,1,0:T(8,128)(2,1)S(1)} custom-call(f32[16]{0:T(128)S(1)} %copy-done.19, s32[1,1,1024]{2,1,0:T(1,128)S(1)} %copy-done.17, s32[1,1024,1]{2,1,0:T(8,128)S(1)} %copy-done.8, bf16[1,1024,3072]{2,1,0:T(8,128)(2,1)} %bitcast.198, bf16[1,1024,1024]{2,1,0:T(8,128)(2,1)S(1)} %bitcast.206, ...), custom_call_target="tpu_custom_call" | custom-call | flops 201326592 | bytes 196608 | tf_op jit(solution)/shard_map/attend_back/pallas_call | solution.py:515
  348.7 17.3 %project_back.1 = (bf16[4,256,1024]{2,1,0:T(8,128)(2,1)}, f32[4,1,768]{2,1,0:T(1,128)}, f32[2,1024]{1,0:T(2,128)}) custom-call(s32[13]{0:T(128)} %copy-done.14, bf16[1024,3072]{1,0:T(8,128)(2,1)} %bitcast.200, bf16[1024,1024]{1,0:T(8,128)(2,1)} %copy-done, f32[1024,1024]{1,0:T(8,128)} %get-tuple-element.114.dx1_ref, f32[1,1024]{1,0:T(1,128)} %get-tuple-element.199.gain_ref, ...), custom_call_target="tpu_custom_call" | custom-call | flops 100663296 | bytes 131072 | tf_op jit(solution)/shard_map/project_back/pallas_call | solution.py:1123
  369.8 9.9 %convolution_convert_fusion = bf16[512,4096]{1,0:T(8,128)(2,1)} fusion(bf16[1024,4096]{1,0:T(8,128)(2,1)} %get-tuple-element.119, bf16[1024,1024]{1,0:T(8,128)(2,1)S(1)} %copy-done.29), kind=kOutput, calls=%fused_computation.3 | convolution fusion | flops 4297064448 | bytes 13631488 | tf_op jit(solution)/shard_map/dot_general | solution.py:38
  394.7 11.6 %all-gather.9.cloned.1.call-done.two_ref = bf16[8,256,1024]{2,1,0:T(8,128)(2,1)} async-done(((bf16[2,256,1024]{2,1,0:T(8,128)(2,1)}), bf16[8,256,1024]{2,1,0:T(8,128)(2,1)}) %all-gather.9.cloned.1.call-update) | async-done | bytes 4194320 | tf_op jit(solution)/shard_map/all_gather | solution.py:1223
  422.6 7.2 %add_convert_fusion.2 = bf16[512,3072]{1,0:T(8,128)(2,1)S(1)} fusion(bf16[512,3072]{1,0:T(8,128)(2,1)} %collective-permute-done.13, bf16[1024,3072]{1,0:T(8,128)(2,1)} %bitcast.201, bf16[1024,1024]{1,0:T(8,128)(2,1)S(1)} %copy-done.51), kind=kOutput, calls=%fused_computation.2 | convolution fusion | flops 3225944064 | bytes 13631488 | tf_op jit(solution)/shard_map/dot_general | solution.py:38
  429.8 7.5 %add_convert_fusion = bf16[512,4096]{1,0:T(8,128)(2,1)S(1)} fusion(bf16[512,4096]{1,0:T(8,128)(2,1)} %collective-permute-done.12, bf16[1024,4096]{1,0:T(8,128)(2,1)S(1)} %bitcast.284, bf16[1024,1024]{1,0:T(8,128)(2,1)S(1)} %copy-done.30), kind=kOutput, calls=%fused_computation | convolution fusion | flops 4301258752 | bytes 17825792 | tf_op jit(solution)/shard_map/dot_general | solution.py:38
  461.7 6.5 %collective-permute-done.19 = bf16[128,1024]{0,1:T(8,128)(2,1)S(1)} collective-permute-done((bf16[128,1024]{0,1:T(8,128)(2,1)}, bf16[128,1024]{0,1:T(8,128)(2,1)S(1)}, u32[]{:S(2)}, u32[]{:S(2)}) %collective-permute-start.19) | collective-permute-done | bytes 262176 | tf_op jit(solution)/shard_map/ppermute | solution.py:1324
  470.1 14.8 %collective-permute-start.20 = (bf16[128,1024]{0,1:T(8,128)(2,1)}, bf16[128,1024]{0,1:T(8,128)(2,1)S(1)}, u32[]{:S(2)}, u32[]{:S(2)}) collective-permute-start(bf16[128,1024]{0,1:T(8,128)(2,1)} %get-tuple-element.171), channel_id=1, source_target_pairs={{0,1},{1,2},{2,3},{4,5},{5,6},{6,7},{8,9},{9,10},{10,11},{12,13},{... | collective-permute-start | bytes 786440 | tf_op jit(solution)/shard_map/ppermute | solution.py:1324
  491.1 7.4 %place_slots.2 = bf16[16,256,1024]{2,1,0:T(8,128)(2,1)} custom-call(s32[13]{0:T(128)S(1)} %copy-done.15, bf16[8,256,1024]{2,1,0:T(8,128)(2,1)S(1)} %copy-done.10, bf16[8,256,1024]{2,1,0:T(8,128)(2,1)S(1)} %copy-done.11), custom_call_target="tpu_custom_call" | custom-call | bytes 262144 | tf_op jit(solution)/shard_map/place_slots/pallas_call | solution.py:646
  542.2 11.9 %collective-permute-done.24 = bf16[128,4096]{1,0:T(8,128)(2,1)S(1)} collective-permute-done((bf16[128,4096]{1,0:T(8,128)(2,1)S(1)}, bf16[128,4096]{1,0:T(8,128)(2,1)S(1)}, u32[]{:S(2)}, u32[]{:S(2)}) %collective-permute-start.24) | collective-permute-done | bytes 1048608 | tf_op jit(solution)/shard_map/ppermute | solution.py:1154
  564.5 6.5 %collective-permute-done.25 = bf16[128,1024]{1,0:T(8,128)(2,1)S(1)} collective-permute-done((bf16[128,1024]{1,0:T(8,128)(2,1)S(1)}, bf16[128,1024]{1,0:T(8,128)(2,1)S(1)}, u32[]{:S(2)}, u32[]{:S(2)}) %collective-permute-start.25) | collective-permute-done | bytes 262176 | tf_op jit(solution)/shard_map/ppermute | solution.py:1324
  604.8 10.1 %collective-permute-done.27 = bf16[128,1024]{1,0:T(8,128)(2,1)S(1)} collective-permute-done((bf16[128,1024]{1,0:T(8,128)(2,1)S(1)}, bf16[128,1024]{1,0:T(8,128)(2,1)S(1)}, u32[]{:S(2)}, u32[]{:S(2)}) %collective-permute-start.27) | collective-permute-done | bytes 262176 | tf_op jit(solution)/shard_map/ppermute | solution.py:1324
  627.6 7.4 %place_slots.3 = bf16[16,256,1024]{2,1,0:T(8,128)(2,1)} custom-call(s32[13]{0:T(128)S(1)} %copy-done.15, bf16[8,256,1024]{2,1,0:T(8,128)(2,1)S(1)} %copy-done.9, bf16[8,256,1024]{2,1,0:T(8,128)(2,1)S(1)} %copy-done.12), custom_call_target="tpu_custom_call" | custom-call | bytes 262144 | tf_op jit(solution)/shard_map/place_slots/pallas_call | solution.py:646
  (396 shorter events, 229.4 us)
Async XLA Ops:
  7.3 160.5 %all-gather.15.cloned.1.call-start = ((), (), s32[]{:S(2)}) async-start(), calls=%async_computation.4 | async-start | bytes 17301504 | tf_op jit(solution)/shard_map/all_gather | solution.py:1253
  10.4 331.2 %all-gather.7.cloned.1.call-start = ((), (), s32[]{:S(2)}) async-start(), calls=%async_computation | async-start | bytes 5242880 | tf_op jit(solution)/shard_map/all_gather | solution.py:1223
  124.2 39.3 %collective-permute-start = (bf16[256,1024]{1,0:T(8,128)(2,1)}, bf16[256,1024]{1,0:T(8,128)(2,1)S(1)}, u32[]{:S(2)}, u32[]{:S(2)}) collective-permute-start(bf16[256,1024]{1,0:T(8,128)(2,1)} %get-tuple-element.90), channel_id=1, source_target_pairs={{0,4},{4,0},{8,12},{12,8},{1,5},{5,1},{9,13},{13,9},{2,6},{6,2},{1... | collective-permute-start | bytes 1572872 | tf_op jit(solution)/shard_map/ppermute | solution.py:1154
  124.7 38.9 %collective-permute-start.1 = (bf16[256,1024]{1,0:T(8,128)(2,1)S(1)}, bf16[256,1024]{1,0:T(8,128)(2,1)}, u32[]{:S(2)}, u32[]{:S(2)}) collective-permute-start(bf16[256,1024]{1,0:T(8,128)(2,1)S(1)} %get-tuple-element.91), channel_id=1, source_target_pairs={{0,8},{4,12},{8,0},{12,4},{1,9},{5,13},{9,1},{13,5},{2,10},{6,14},... | collective-permute-start | bytes 1572872 | tf_op jit(solution)/shard_map/ppermute | solution.py:1154
  125.1 38.5 %collective-permute-start.2 = (bf16[256,1024]{1,0:T(8,128)(2,1)S(1)}, bf16[256,1024]{1,0:T(8,128)(2,1)}, u32[]{:S(2)}, u32[]{:S(2)}) collective-permute-start(bf16[256,1024]{1,0:T(8,128)(2,1)S(1)} %get-tuple-element.92), channel_id=1, source_target_pairs={{0,12},{4,8},{8,4},{12,0},{1,13},{5,9},{9,5},{13,1},{2,14},{6,10},... | collective-permute-start | bytes 1572872 | tf_op jit(solution)/shard_map/ppermute | solution.py:1154
  210.1 24.4 %collective-permute-start.5 = (bf16[256,1024]{1,0:T(8,128)(2,1)S(1)}, bf16[256,1024]{1,0:T(8,128)(2,1)S(1)}, u32[]{:S(2)}, u32[]{:S(2)}) collective-permute-start(bf16[256,1024]{1,0:T(8,128)(2,1)S(1)} %get-tuple-element.162), channel_id=1, source_target_pairs={{0,12},{4,8},{8,4},{12,0},{1,13},{5,9},{9,5},{13,1},{2,14},{6,10},... | collective-permute-start | bytes 1572872 | tf_op jit(solution)/shard_map/ppermute | solution.py:1154
  234.8 34.8 %collective-permute-start.6 = (bf16[512,4096]{1,0:T(8,128)(2,1)}, bf16[512,4096]{1,0:T(8,128)(2,1)}, u32[]{:S(2)}, u32[]{:S(2)}) collective-permute-start(bf16[512,4096]{1,0:T(8,128)(2,1)} %convolution_convert_fusion.2), channel_id=1, source_target_pairs={{0,4},{4,0},{8,12},{12,8},{1,5},{5,1},{9,13},{13,9},{2,6},{6,2},{1... | collective-permute-start | bytes 12582920 | tf_op jit(solution)/shard_map/ppermute | solution.py:1154
  236.6 169.6 %all-gather.9.cloned.1.call-start = ((), (), s32[]{:S(2)}) async-start(), calls=%async_computation.1 | async-start | bytes 5242880 | tf_op jit(solution)/shard_map/all_gather | solution.py:1223
  291.4 50.2 %collective-permute-start.7 = (bf16[2,128,4096]{1,2,0:T(8,128)(2,1)}, bf16[2,128,4096]{1,2,0:T(8,128)(2,1)}, u32[]{:S(2)}, u32[]{:S(2)}) collective-permute-start(bf16[2,128,4096]{1,2,0:T(8,128)(2,1)} %slice_bitcast_fusion.3), channel_id=1, source_target_pairs={{0,8},{4,12},{8,0},{12,4},{1,9},{5,13},{9,1},{13,5},{2,10},{6,14},... | collective-permute-start | bytes 6291464 | tf_op jit(solution)/shard_map/ppermute | solution.py:1154
  292.1 323.7 %all-gather.11.cloned.1.call-start = ((), (), s32[]{:S(2)}) async-start(), calls=%async_computation.2 | async-start | bytes 5242880 | tf_op jit(solution)/shard_map/all_gather | solution.py:1223
  346.7 59.5 %collective-permute-start.11 = (bf16[128,4096]{0,1:T(8,128)(2,1)}, bf16[128,4096]{0,1:T(8,128)(2,1)S(1)}, u32[]{:S(2)}, u32[]{:S(2)}) collective-permute-start(bf16[128,4096]{0,1:T(8,128)(2,1)} %slice_bitcast_fusion.8), channel_id=1, source_target_pairs={{0,16},{16,0},{1,17},{17,1},{2,18},{18,2},{3,19},{19,3},{4,20},{20... | collective-permute-start | bytes 3145736 | tf_op jit(solution)/shard_map/ppermute | solution.py:1154
  369.1 24.0 %collective-permute-start.10 = (bf16[256,1024]{1,0:T(8,128)(2,1)S(1)}, bf16[256,1024]{1,0:T(8,128)(2,1)S(1)}, u32[]{:S(2)}, u32[]{:S(2)}) collective-permute-start(bf16[256,1024]{1,0:T(8,128)(2,1)S(1)} %get-tuple-element.158), channel_id=1, source_target_pairs={{0,12},{4,8},{8,4},{12,0},{1,13},{5,9},{9,5},{13,1},{2,14},{6,10},... | collective-permute-start | bytes 1572872 | tf_op jit(solution)/shard_map/ppermute | solution.py:1154
  406.2 23.5 %collective-permute-start.12 = (bf16[512,4096]{1,0:T(8,128)(2,1)}, bf16[512,4096]{1,0:T(8,128)(2,1)}, u32[]{:S(2)}, u32[]{:S(2)}) collective-permute-start(bf16[512,4096]{1,0:T(8,128)(2,1)} %convolution_convert_fusion), channel_id=1, source_target_pairs={{0,4},{4,0},{8,12},{12,8},{1,5},{5,1},{9,13},{13,9},{2,6},{6,2},{1... | collective-permute-start | bytes 12582920 | tf_op jit(solution)/shard_map/ppermute | solution.py:1154
  413.3 206.5 %all-gather.13.cloned.1.call-start = ((), (), s32[]{:S(2)}) async-start(), calls=%async_computation.3 | async-start | bytes 5242880 | tf_op jit(solution)/shard_map/all_gather | solution.py:1223
  441.0 59.4 %collective-permute-start.15 = (bf16[2,128,4096]{2,1,0:T(8,128)(2,1)}, bf16[2,128,4096]{2,1,0:T(8,128)(2,1)}, u32[]{:S(2)}, u32[]{:S(2)}) collective-permute-start(bf16[2,128,4096]{2,1,0:T(8,128)(2,1)} %slice_bitcast_fusion), channel_id=1, source_target_pairs={{0,16},{16,0},{1,17},{17,1},{2,18},{18,2},{3,19},{19,3},{4,20},{20... | collective-permute-start | bytes 6291464 | tf_op jit(solution)/shard_map/ppermute | solution.py:1154
  443.9 56.4 %collective-permute-start.16 = (bf16[2,128,3072]{2,1,0:T(8,128)(2,1)}, bf16[2,128,3072]{2,1,0:T(8,128)(2,1)}, u32[]{:S(2)}, u32[]{:S(2)}) collective-permute-start(bf16[2,128,3072]{2,1,0:T(8,128)(2,1)} %slice_bitcast_fusion.4), channel_id=1, source_target_pairs={{0,8},{4,12},{8,0},{12,4},{1,9},{5,13},{9,1},{13,5},{2,10},{6,14},... | collective-permute-start | bytes 4718600 | tf_op jit(solution)/shard_map/ppermute | solution.py:1154
  460.1 40.2 %collective-permute-start.17 = (bf16[2,128,1024]{1,2,0:T(8,128)(2,1)}, bf16[2,128,1024]{1,2,0:T(8,128)(2,1)S(1)}, u32[]{:S(2)}, u32[]{:S(2)}) collective-permute-start(bf16[2,128,1024]{1,2,0:T(8,128)(2,1)} %slice_bitcast_fusion.12), channel_id=1, source_target_pairs={{0,8},{4,12},{8,0},{12,4},{1,9},{5,13},{9,1},{13,5},{2,10},{6,14},... | collective-permute-start | bytes 1572872 | tf_op jit(solution)/shard_map/ppermute | solution.py:1154
  470.1 28.4 %collective-permute-start.20 = (bf16[128,1024]{0,1:T(8,128)(2,1)}, bf16[128,1024]{0,1:T(8,128)(2,1)S(1)}, u32[]{:S(2)}, u32[]{:S(2)}) collective-permute-start(bf16[128,1024]{0,1:T(8,128)(2,1)} %get-tuple-element.171), channel_id=1, source_target_pairs={{0,1},{1,2},{2,3},{4,5},{5,6},{6,7},{8,9},{9,10},{10,11},{12,13},{... | collective-permute-start | bytes 786440 | tf_op jit(solution)/shard_map/ppermute | solution.py:1324
  504.1 30.4 %collective-permute-start.38 = (bf16[128,1024]{0,1:T(8,128)(2,1)S(1)}, bf16[128,1024]{0,1:T(8,128)(2,1)S(1)}, u32[]{:S(2)}, u32[]{:S(2)}) collective-permute-start(bf16[128,1024]{0,1:T(8,128)(2,1)S(1)} %slice_bitcast_fusion.19), channel_id=1, source_target_pairs={{0,16},{16,0},{1,17},{17,1},{2,18},{18,2},{3,19},{19,3},{4,20},{20... | collective-permute-start | bytes 786440 | tf_op jit(solution)/shard_map/ppermute | solution.py:1154
  516.1 23.9 %collective-permute-start.31 = (bf16[128,3072]{1,0:T(8,128)(2,1)S(1)}, bf16[128,3072]{1,0:T(8,128)(2,1)S(1)}, u32[]{:S(2)}, u32[]{:S(2)}) collective-permute-start(bf16[128,3072]{1,0:T(8,128)(2,1)S(1)} %slice_bitcast_fusion.9), channel_id=1, source_target_pairs={{0,16},{16,0},{1,17},{17,1},{2,18},{18,2},{3,19},{19,3},{4,20},{20... | collective-permute-start | bytes 2359304 | tf_op jit(solution)/shard_map/ppermute | solution.py:1154
  530.2 23.9 %collective-permute-start.24 = (bf16[128,4096]{1,0:T(8,128)(2,1)S(1)}, bf16[128,4096]{1,0:T(8,128)(2,1)S(1)}, u32[]{:S(2)}, u32[]{:S(2)}) collective-permute-start(bf16[128,4096]{1,0:T(8,128)(2,1)S(1)} %slice_bitcast_fusion.5), channel_id=1, source_target_pairs={{0,8},{4,12},{8,0},{12,4},{1,9},{5,13},{9,1},{13,5},{2,10},{6,14},... | collective-permute-start | bytes 3145736 | tf_op jit(solution)/shard_map/ppermute | solution.py:1154
  534.5 24.2 %collective-permute-start.39 = (bf16[128,256]{0,1:T(8,128)(2,1)S(1)}, bf16[128,256]{0,1:T(8,128)(2,1)S(1)}, u32[]{:S(2)}, u32[]{:S(2)}) collective-permute-start(bf16[128,256]{0,1:T(8,128)(2,1)S(1)} %get-tuple-element.190), channel_id=1, source_target_pairs={{0,1},{4,5},{8,9},{12,13},{16,17},{20,21},{24,25},{28,29}} | collective-permute-start | bytes 196616 | tf_op jit(solution)/shard_map/ppermute | solution.py:1324
  571.9 21.6 %collective-permute-start.26 = (bf16[128,1024]{1,0:T(8,128)(2,1)S(1)}, bf16[128,1024]{1,0:T(8,128)(2,1)S(1)}, u32[]{:S(2)}, u32[]{:S(2)}) collective-permute-start(bf16[128,1024]{1,0:T(8,128)(2,1)S(1)} %get-tuple-element.167), channel_id=1, source_target_pairs={{0,1},{1,2},{4,5},{5,6},{8,9},{9,10},{12,13},{13,14},{16,17},{17,1... | collective-permute-start | bytes 786440 | tf_op jit(solution)/shard_map/ppermute | solution.py:1324
  577.7 22.3 %collective-permute-start.41 = (bf16[128,256]{0,1:T(8,128)(2,1)S(1)}, bf16[128,256]{0,1:T(8,128)(2,1)S(1)}, u32[]{:S(2)}, u32[]{:S(2)}) collective-permute-start(bf16[128,256]{0,1:T(8,128)(2,1)S(1)} %get-tuple-element.186), channel_id=1, source_target_pairs={{0,1},{1,2},{2,3},{4,5},{5,6},{6,7},{8,9},{9,10},{10,11},{12,13},{... | collective-permute-start | bytes 196616 | tf_op jit(solution)/shard_map/ppermute | solution.py:1324
  (97 other events, 1028.0 us)
Sparse Core Ops, SparseCore 0:
  11.7 156.0 all-gather.14
  236.7 88.5 all-gather.6
  326.9 79.2 all-gather.8
  413.5 92.1 all-gather.10
  507.1 112.7 all-gather.12

commit v3 on v2

--- a/solution.py
+++ b/solution.py
@@ -1331,13 +1331,14 @@
 
     dy = order_pieces(order, exchanged(grad_slots))
     dy, result, activated = lax.optimization_barrier((dy, result, activated))
-    result = exchanged(list(result))
+    result_one = over_groups(jnp.stack([result[0], across_core(result[1])]))
+    result = jnp.stack([swap(result[bits], "ctx", bits) for bits in (2, 3)])
     away_down = away(dy, activated)
     home_down = home(dy, activated).astype(jnp.bfloat16)
     dy, result, away_down, home_down = lax.optimization_barrier(
         (dy, result, away_down, home_down)
     )
-    result_one, result_two = over_groups(result[:2]), over_groups(result[2:])
+    result_two = over_groups(result)
     da, grad_ubias, dx1, dattn, sums_two = ff_back(
         order, dy, gelu_slope, x1, gain_two, weights, groups
     )

time: 647 us -> 657 us (1.015)
  local copies, waits for them, and re-layouts: 60.7 us -> 69.5 us
    unnamed x132 -> x110, local copies, waits for them, and re-layouts: 23.4 us -> 23.8 us
  transfers between devices with their start and end apart: 59 -> 59, of which waited for: 16 -> 15; matrix products, arithmetic and copies ran while one was open for 19% -> 20% of each run, Pallas kernels for 38% -> 38%
where the time goes in v3:
time: 657 us; the launch traced here: 651 us
  Pallas kernels  293 us (45%)
  starting transfers between devices  103 us (16%)
  waiting for transfers between devices  81 us (12%)
  local copies, waits for them, and re-layouts  69.5 us (11%)
  matrix products  52.5 us (8%)
  other arithmetic  35.8 us (5%)
  between operations  15.7 us (2%)
    pallas_call x1, Pallas kernels, gather_first(): pl.pallas_call(functools.partial(gather_kernel, cut), in_specs=[anywhere]...  89.4 us
    ppermute x30, starting transfers between devices, over_z(): arrived[index, sign] = lax.ppermute(part, 'tensor', pairs)  83.7 us
    dot_general x8, matrix products, matmul_left(): lax.dot_general(left, right, (((0,), (0,)), ((), ())), preferred_element_...  52.5 us
    pallas_call x1, Pallas kernels, attend_back(): pl.pallas_call(functools.partial(attend_back_kernel, heads, block), grid=...  46.4 us
    ppermute x30, waiting for transfers between devices, over_z(): arrived[index, sign] = lax.ppermute(part, 'tensor', pairs)  40.1 us
    pallas_call x1, Pallas kernels, ff_back(): pl.pallas_call(ff_back_kernel, grid_spec=prefetched((groups,), [whole(row...  33.3 us
    ppermute x24, waiting for transfers between devices, swap(): lax.ppermute(value, axis, [(index, index ^ bits) for index in range(count)])  27 us
    unnamed x110, local copies, waits for them, and re-layouts  23.8 us
  transfers between devices with their start and end apart: 59, of which 15 were waited for; matrix products, arithmetic and copies ran while one was open for 20% of the time, Pallas kernels for 38%

profile of v3, /device:TPU:0, one launch (start us, length us, event | category | flops | bytes accessed | tf_op | source)
XLA Modules:
  0.0 651.2 jit_solution(1961303247113945418)
XLA Ops:
  20.6 89.4 %gather_first.1 = (bf16[2,2,4,144,1024]{4,3,2,1,0:T(8,128)(2,1)}, bf16[2,2,4,144,1024]{4,3,2,1,0:T(8,128)(2,1)}, bf16[4,256,1024]{2,1,0:T(8,128)(2,1)}, s32[4,8,128]{2,1,0:T(8,128)}) custom-call(bf16[144,1024]{1,0:T(8,128)(2,1)} %pad_maximum_fusion.5.pack_ref, bf16[16,256,1024]{2,1,0:T(8,128)(2,1)} %tokens_ref.1, s32[16,8,128]{2,1,0:T(8,128)} %bitcast.269), custom_call_target="tpu_custom_call" | custom-call | bytes 2097152 | tf_op jit(solution)/shard_map/gather_first/pallas_call | solution.py:775
  121.9 12.4 %project.1 = (bf16[1024,1024]{1,0:T(8,128)(2,1)}, bf16[1024,3072]{1,0:T(8,128)(2,1)}) custom-call(bf16[1024,1024]{1,0:T(8,128)(2,1)} %copy-done, f32[1,1024]{1,0:T(1,128)} %get-tuple-element.197.gain_ref, f32[1,1024]{1,0:T(1,128)} %get-tuple-element.196.shift_ref, f32[4,1,768]{2,1,0:T(1,128)} %pad_maximum_fusion.6.bias_ref, ...), custom_call_target="tpu_custom_call" | custom-call | flops 100663296 | bytes 98304 | tf_op jit(solution)/shard_map/project/pallas_call | solution.py:829
  142.4 23.6 %attend.1 = (bf16[1,1024,1024]{2,1,0:T(8,128)(2,1)S(1)}, f32[1,4,4,1024]{3,2,1,0:T(4,128)S(1)}) custom-call(f32[16]{0:T(128)S(1)} %reshape.310.slope_ref, s32[1,1,1024]{2,1,0:T(1,128)S(1)} %reshape.287.row_ref, s32[1,1024,1]{2,1,0:T(8,128)S(1)} %reshape.329.col_ref, bf16[1,1024,3072]{2,1,0:T(8,128)(2,1)S(1)} %bitcast.199), custom_call_target="tpu_custom_call" | custom-call | flops 201326592 | bytes 196608 | tf_op jit(solution)/shard_map/attend/pallas_call | solution.py:495
  167.4 7.6 %mix_out.1 = (f32[1024,1024]{1,0:T(8,128)}, bf16[1024,1024]{1,0:T(8,128)(2,1)}) custom-call(bf16[1024,1024]{1,0:T(8,128)(2,1)} %bitcast.205, bf16[1024,1024]{1,0:T(8,128)(2,1)} %copy-done, f32[1,1024]{1,0:T(1,128)} %get-tuple-element.195.bias_ref, f32[1,1024]{1,0:T(1,128)} %get-tuple-element.194.gain_ref, f32[1,1024]{1,0:T(1,128)} %get-tuple-element.193.shift_ref, ...), custom_call_target="tpu_custom_call" | custom-call | flops 33554432 | bytes 196608 | tf_op jit(solution)/shard_map/mix_out/pallas_call | solution.py:874
  177.9 23.0 %expand.1 = (bf16[1024,4096]{1,0:T(8,128)(2,1)}, bf16[1024,4096]{1,0:T(8,128)(2,1)}) custom-call(s32[13]{0:T(128)} %copy-done.14, bf16[1024,1024]{1,0:T(8,128)(2,1)} %get-tuple-element.118.h_ref, f32[4,1,1024]{2,1,0:T(1,128)} %reshape.313.bias_ref, bf16[32,2,128,1024]{3,2,1,0:T(8,128)(2,1)} %bitcast.207, bf16[32,2,128,1024]{3,2,1,0:T(8,128)(2,1)} %bitcast.208, ...), custom_call_target="tpu_custom_call" | custom-call | flops 134217728 | bytes 524288 | tf_op jit(solution)/shard_map/expand/pallas_call | solution.py:910
  200.9 16.9 %contract.1 = bf16[4,256,1024]{2,1,0:T(8,128)(2,1)} custom-call(s32[13]{0:T(128)} %copy-done.14, bf16[1024,4096]{1,0:T(8,128)(2,1)} %get-tuple-element.99.g_ref, f32[1024,1024]{1,0:T(8,128)} %get-tuple-element.96.x1_ref, f32[1,1024]{1,0:T(1,128)} %get-tuple-element.192.bias_ref, bf16[32,2,128,1024]{3,2,1,0:T(8,128)(2,1)} %bitcast.222, ...), custom_call_target="tpu_custom_call" | custom-call | flops 134217728 | bytes 262144 | tf_op jit(solution)/shard_map/contract/pallas_call | solution.py:959
  222.4 9.7 %convolution_convert_fusion.2 = bf16[512,4096]{1,0:T(8,128)(2,1)} fusion(bf16[1024,4096]{1,0:T(8,128)(2,1)} %get-tuple-element.99.g_ref, bf16[1024,1024]{1,0:T(8,128)(2,1)S(1)} %order_pieces.3.dy_ref), kind=kOutput, calls=%fused_computation.5 | convolution fusion | flops 4297064448 | bytes 13631488 | tf_op jit(solution)/shard_map/dot_general | solution.py:38
  238.3 7.4 %collective-permute-done.3 = bf16[256,1024]{1,0:T(8,128)(2,1)S(1)} collective-permute-done((bf16[256,1024]{1,0:T(8,128)(2,1)S(1)}, bf16[256,1024]{1,0:T(8,128)(2,1)S(1)}, u32[]{:S(2)}, u32[]{:S(2)}) %collective-permute-start.3) | collective-permute-done | bytes 524320 | tf_op jit(solution)/shard_map/ppermute | solution.py:1154
  247.9 33.3 %ff_back.1 = (bf16[1024,4096]{1,0:T(8,128)(2,1)}, f32[4,1,1024]{2,1,0:T(1,128)}, f32[1024,1024]{1,0:T(8,128)}, bf16[1024,1024]{1,0:T(8,128)(2,1)}, f32[4,1024]{1,0:T(4,128)}) custom-call(s32[13]{0:T(128)} %copy-done.14, bf16[1024,1024]{1,0:T(8,128)(2,1)} %copy-done.5, bf16[1024,4096]{1,0:T(8,128)(2,1)} %get-tuple-element.101.slope_ref, ...), custom_call_target="tpu_custom_call" | custom-call | flops 268435456 | bytes 524288 | tf_op jit(solution)/shard_map/ff_back/pallas_call | solution.py:1025
  304.3 46.4 %attend_back.1 = bf16[1,1024,3072]{2,1,0:T(8,128)(2,1)S(1)} custom-call(f32[16]{0:T(128)S(1)} %copy-done.19, s32[1,1,1024]{2,1,0:T(1,128)S(1)} %copy-done.17, s32[1,1024,1]{2,1,0:T(8,128)S(1)} %copy-done.8, bf16[1,1024,3072]{2,1,0:T(8,128)(2,1)} %bitcast.198, bf16[1,1024,1024]{2,1,0:T(8,128)(2,1)S(1)} %bitcast.206, ...), custom_call_target="tpu_custom_call" | custom-call | flops 201326592 | bytes 196608 | tf_op jit(solution)/shard_map/attend_back/pallas_call | solution.py:515
  353.3 17.3 %project_back.1 = (bf16[4,256,1024]{2,1,0:T(8,128)(2,1)}, f32[4,1,768]{2,1,0:T(1,128)}, f32[2,1024]{1,0:T(2,128)}) custom-call(s32[13]{0:T(128)} %copy-done.14, bf16[1024,3072]{1,0:T(8,128)(2,1)} %bitcast.200, bf16[1024,1024]{1,0:T(8,128)(2,1)} %copy-done, f32[1024,1024]{1,0:T(8,128)} %get-tuple-element.113.dx1_ref, f32[1,1024]{1,0:T(1,128)} %get-tuple-element.197.gain_ref, ...), custom_call_target="tpu_custom_call" | custom-call | flops 100663296 | bytes 131072 | tf_op jit(solution)/shard_map/project_back/pallas_call | solution.py:1123
  380.4 10.2 %convolution_convert_fusion = bf16[512,4096]{1,0:T(8,128)(2,1)} fusion(bf16[1024,4096]{1,0:T(8,128)(2,1)} %get-tuple-element.119, bf16[1024,1024]{1,0:T(8,128)(2,1)S(1)} %copy-done.31), kind=kOutput, calls=%fused_computation.3 | convolution fusion | flops 4297064448 | bytes 13631488 | tf_op jit(solution)/shard_map/dot_general | solution.py:38
  400.0 13.8 %all-gather.9.cloned.1.call-done.two_ref = bf16[8,256,1024]{2,1,0:T(8,128)(2,1)} async-done(((bf16[2,256,1024]{2,1,0:T(8,128)(2,1)}), bf16[8,256,1024]{2,1,0:T(8,128)(2,1)}) %all-gather.9.cloned.1.call-update) | async-done | bytes 4194320 | tf_op jit(solution)/shard_map/all_gather | solution.py:1223
  430.2 7.3 %add_convert_fusion.2 = bf16[512,3072]{1,0:T(8,128)(2,1)S(1)} fusion(bf16[512,3072]{1,0:T(8,128)(2,1)} %collective-permute-done.13, bf16[1024,3072]{1,0:T(8,128)(2,1)} %bitcast.201, bf16[1024,1024]{1,0:T(8,128)(2,1)S(1)} %copy-done.43), kind=kOutput, calls=%fused_computation.2 | convolution fusion | flops 3225944064 | bytes 13631488 | tf_op jit(solution)/shard_map/dot_general | solution.py:38
  437.6 7.5 %add_convert_fusion = bf16[512,4096]{1,0:T(8,128)(2,1)S(1)} fusion(bf16[512,4096]{1,0:T(8,128)(2,1)} %collective-permute-done.12, bf16[1024,4096]{1,0:T(8,128)(2,1)S(1)} %bitcast.284, bf16[1024,1024]{1,0:T(8,128)(2,1)S(1)} %copy-done.32), kind=kOutput, calls=%fused_computation | convolution fusion | flops 4301258752 | bytes 17825792 | tf_op jit(solution)/shard_map/dot_general | solution.py:38
  453.3 8.5 %collective-permute-done.18 = bf16[128,1024]{0,1:T(8,128)(2,1)S(1)} collective-permute-done((bf16[128,1024]{0,1:T(8,128)(2,1)S(1)}, bf16[128,1024]{0,1:T(8,128)(2,1)S(1)}, u32[]{:S(2)}, u32[]{:S(2)}) %collective-permute-start.18) | collective-permute-done | bytes 262176 | tf_op jit(solution)/shard_map/ppermute | solution.py:1324
  472.6 6.6 %collective-permute-done.19 = bf16[128,1024]{0,1:T(8,128)(2,1)S(1)} collective-permute-done((bf16[128,1024]{0,1:T(8,128)(2,1)}, bf16[128,1024]{0,1:T(8,128)(2,1)S(1)}, u32[]{:S(2)}, u32[]{:S(2)}) %collective-permute-start.19) | collective-permute-done | bytes 262176 | tf_op jit(solution)/shard_map/ppermute | solution.py:1324
  482.4 17.6 %collective-permute-start.20 = (bf16[128,1024]{0,1:T(8,128)(2,1)}, bf16[128,1024]{0,1:T(8,128)(2,1)S(1)}, u32[]{:S(2)}, u32[]{:S(2)}) collective-permute-start(bf16[128,1024]{0,1:T(8,128)(2,1)} %get-tuple-element.169), channel_id=1, source_target_pairs={{0,1},{1,2},{2,3},{4,5},{5,6},{6,7},{8,9},{9,10},{10,11},{12,13},{... | collective-permute-start | bytes 786440 | tf_op jit(solution)/shard_map/ppermute | solution.py:1324
  505.7 7.6 %place_slots.2 = bf16[16,256,1024]{2,1,0:T(8,128)(2,1)} custom-call(s32[13]{0:T(128)S(1)} %copy-done.15, bf16[8,256,1024]{2,1,0:T(8,128)(2,1)S(1)} %copy-done.10, bf16[8,256,1024]{2,1,0:T(8,128)(2,1)S(1)} %copy-done.11), custom_call_target="tpu_custom_call" | custom-call | bytes 262144 | tf_op jit(solution)/shard_map/place_slots/pallas_call | solution.py:646
  538.6 7.0 %collective-permute-start.50 = (f32[1,1024]{1,0:T(1,128)S(1)}, f32[1,1024]{1,0:T(1,128)S(1)}, u32[]{:S(2)}, u32[]{:S(2)}) collective-permute-start(f32[1,1024]{1,0:T(1,128)S(1)} %get-tuple-element.200), channel_id=1, source_target_pairs={{0,1},{1,2},{2,3},{4,5},{5,6},{6,7},{8,9},{9,10},{10,11},{12,13},{... | collective-permute-start | bytes 12296 | tf_op jit(solution)/shard_map/ppermute | solution.py:1324
  555.4 13.9 %collective-permute-done.24 = bf16[128,4096]{1,0:T(8,128)(2,1)S(1)} collective-permute-done((bf16[128,4096]{1,0:T(8,128)(2,1)S(1)}, bf16[128,4096]{1,0:T(8,128)(2,1)S(1)}, u32[]{:S(2)}, u32[]{:S(2)}) %collective-permute-start.24) | collective-permute-done | bytes 1048608 | tf_op jit(solution)/shard_map/ppermute | solution.py:1154
  579.0 6.5 %collective-permute-done.25 = bf16[128,1024]{1,0:T(8,128)(2,1)S(1)} collective-permute-done((bf16[128,1024]{1,0:T(8,128)(2,1)S(1)}, bf16[128,1024]{1,0:T(8,128)(2,1)S(1)}, u32[]{:S(2)}, u32[]{:S(2)}) %collective-permute-start.25) | collective-permute-done | bytes 262176 | tf_op jit(solution)/shard_map/ppermute | solution.py:1324
  621.4 7.1 %collective-permute-done.27 = bf16[128,1024]{1,0:T(8,128)(2,1)S(1)} collective-permute-done((bf16[128,1024]{1,0:T(8,128)(2,1)S(1)}, bf16[128,1024]{1,0:T(8,128)(2,1)S(1)}, u32[]{:S(2)}, u32[]{:S(2)}) %collective-permute-start.27) | collective-permute-done | bytes 262176 | tf_op jit(solution)/shard_map/ppermute | solution.py:1324
  637.1 7.4 %place_slots.3 = bf16[16,256,1024]{2,1,0:T(8,128)(2,1)} custom-call(s32[13]{0:T(128)S(1)} %copy-done.15, bf16[8,256,1024]{2,1,0:T(8,128)(2,1)S(1)} %copy-done.9, bf16[8,256,1024]{2,1,0:T(8,128)(2,1)S(1)} %copy-done.12), custom_call_target="tpu_custom_call" | custom-call | bytes 262144 | tf_op jit(solution)/shard_map/place_slots/pallas_call | solution.py:646
  (374 shorter events, 227.8 us)
Async XLA Ops:
  7.2 170.7 %all-gather.15.cloned.1.call-start = ((), (), s32[]{:S(2)}) async-start(), calls=%async_computation.4 | async-start | bytes 17301504 | tf_op jit(solution)/shard_map/all_gather | solution.py:1253
  10.1 343.2 %all-gather.7.cloned.1.call-start = ((), (), s32[]{:S(2)}) async-start(), calls=%async_computation | async-start | bytes 5242880 | tf_op jit(solution)/shard_map/all_gather | solution.py:1223
  136.0 39.0 %collective-permute-start.2 = (bf16[256,1024]{1,0:T(8,128)(2,1)S(1)}, bf16[256,1024]{1,0:T(8,128)(2,1)S(1)}, u32[]{:S(2)}, u32[]{:S(2)}) collective-permute-start(bf16[256,1024]{1,0:T(8,128)(2,1)S(1)} %get-tuple-element.92), channel_id=1, source_target_pairs={{0,12},{4,8},{8,4},{12,0},{1,13},{5,9},{9,5},{13,1},{2,14},{6,10},... | collective-permute-start | bytes 1572872 | tf_op jit(solution)/shard_map/ppermute | solution.py:1154
  136.7 38.3 %collective-permute-start.1 = (bf16[256,1024]{1,0:T(8,128)(2,1)S(1)}, bf16[256,1024]{1,0:T(8,128)(2,1)}, u32[]{:S(2)}, u32[]{:S(2)}) collective-permute-start(bf16[256,1024]{1,0:T(8,128)(2,1)S(1)} %get-tuple-element.91), channel_id=1, source_target_pairs={{0,8},{4,12},{8,0},{12,4},{1,9},{5,13},{9,1},{13,5},{2,10},{6,14},... | collective-permute-start | bytes 1572872 | tf_op jit(solution)/shard_map/ppermute | solution.py:1154
  138.0 37.0 %collective-permute-start = (bf16[256,1024]{1,0:T(8,128)(2,1)S(1)}, bf16[256,1024]{1,0:T(8,128)(2,1)}, u32[]{:S(2)}, u32[]{:S(2)}) collective-permute-start(bf16[256,1024]{1,0:T(8,128)(2,1)S(1)} %get-tuple-element.90), channel_id=1, source_target_pairs={{0,4},{4,0},{8,12},{12,8},{1,5},{5,1},{9,13},{13,9},{2,6},{6,2},{1... | collective-permute-start | bytes 1572872 | tf_op jit(solution)/shard_map/ppermute | solution.py:1154
  221.1 24.6 %collective-permute-start.3 = (bf16[256,1024]{1,0:T(8,128)(2,1)S(1)}, bf16[256,1024]{1,0:T(8,128)(2,1)S(1)}, u32[]{:S(2)}, u32[]{:S(2)}) collective-permute-start(bf16[256,1024]{1,0:T(8,128)(2,1)S(1)} %get-tuple-element.162), channel_id=1, source_target_pairs={{0,8},{4,12},{8,0},{12,4},{1,9},{5,13},{9,1},{13,5},{2,10},{6,14},... | collective-permute-start | bytes 1572872 | tf_op jit(solution)/shard_map/ppermute | solution.py:1154
  222.4 24.4 %collective-permute-start.7 = (bf16[256,1024]{1,0:T(8,128)(2,1)}, bf16[256,1024]{1,0:T(8,128)(2,1)S(1)}, u32[]{:S(2)}, u32[]{:S(2)}) collective-permute-start(bf16[256,1024]{1,0:T(8,128)(2,1)} %get-tuple-element.160), channel_id=1, source_target_pairs={{0,4},{4,0},{8,12},{12,8},{1,5},{5,1},{9,13},{13,9},{2,6},{6,2},{1... | collective-permute-start | bytes 1572872 | tf_op jit(solution)/shard_map/ppermute | solution.py:1154
  246.7 34.4 %collective-permute-start.5 = (bf16[512,4096]{1,0:T(8,128)(2,1)}, bf16[512,4096]{1,0:T(8,128)(2,1)}, u32[]{:S(2)}, u32[]{:S(2)}) collective-permute-start(bf16[512,4096]{1,0:T(8,128)(2,1)} %convolution_convert_fusion.2), channel_id=1, source_target_pairs={{0,4},{4,0},{8,12},{12,8},{1,5},{5,1},{9,13},{13,9},{2,6},{6,2},{1... | collective-permute-start | bytes 12582920 | tf_op jit(solution)/shard_map/ppermute | solution.py:1154
  247.9 165.9 %all-gather.9.cloned.1.call-start = ((), (), s32[]{:S(2)}) async-start(), calls=%async_computation.1 | async-start | bytes 5242880 | tf_op jit(solution)/shard_map/all_gather | solution.py:1223
  303.0 50.3 %collective-permute-start.6 = (bf16[2,128,4096]{1,2,0:T(8,128)(2,1)}, bf16[2,128,4096]{1,2,0:T(8,128)(2,1)}, u32[]{:S(2)}, u32[]{:S(2)}) collective-permute-start(bf16[2,128,4096]{1,2,0:T(8,128)(2,1)} %slice_bitcast_fusion.3), channel_id=1, source_target_pairs={{0,8},{4,12},{8,0},{12,4},{1,9},{5,13},{9,1},{13,5},{2,10},{6,14},... | collective-permute-start | bytes 6291464 | tf_op jit(solution)/shard_map/ppermute | solution.py:1154
  303.8 325.6 %all-gather.11.cloned.1.call-start = ((), (), s32[]{:S(2)}) async-start(), calls=%async_computation.2 | async-start | bytes 5242880 | tf_op jit(solution)/shard_map/all_gather | solution.py:1223
  372.5 25.8 %collective-permute-start.10 = (bf16[256,1024]{1,0:T(8,128)(2,1)S(1)}, bf16[256,1024]{1,0:T(8,128)(2,1)S(1)}, u32[]{:S(2)}, u32[]{:S(2)}) collective-permute-start(bf16[256,1024]{1,0:T(8,128)(2,1)S(1)} %get-tuple-element.156), channel_id=1, source_target_pairs={{0,12},{4,8},{8,4},{12,0},{1,13},{5,9},{9,5},{13,1},{2,14},{6,10},... | collective-permute-start | bytes 1572872 | tf_op jit(solution)/shard_map/ppermute | solution.py:1154
  373.8 24.6 %collective-permute-start.9 = (bf16[256,1024]{1,0:T(8,128)(2,1)S(1)}, bf16[256,1024]{1,0:T(8,128)(2,1)S(1)}, u32[]{:S(2)}, u32[]{:S(2)}) collective-permute-start(bf16[256,1024]{1,0:T(8,128)(2,1)S(1)} %get-tuple-element.157), channel_id=1, source_target_pairs={{0,8},{4,12},{8,0},{12,4},{1,9},{5,13},{9,1},{13,5},{2,10},{6,14},... | collective-permute-start | bytes 1572872 | tf_op jit(solution)/shard_map/ppermute | solution.py:1154
  374.5 23.9 %collective-permute-start.8 = (bf16[256,1024]{1,0:T(8,128)(2,1)S(1)}, bf16[256,1024]{1,0:T(8,128)(2,1)S(1)}, u32[]{:S(2)}, u32[]{:S(2)}) collective-permute-start(bf16[256,1024]{1,0:T(8,128)(2,1)S(1)} %get-tuple-element.158), channel_id=1, source_target_pairs={{0,4},{4,0},{8,12},{12,8},{1,5},{5,1},{9,13},{13,9},{2,6},{6,2},{1... | collective-permute-start | bytes 1572872 | tf_op jit(solution)/shard_map/ppermute | solution.py:1154
  379.2 34.6 %collective-permute-start.11 = (bf16[128,4096]{0,1:T(8,128)(2,1)}, bf16[128,4096]{0,1:T(8,128)(2,1)S(1)}, u32[]{:S(2)}, u32[]{:S(2)}) collective-permute-start(bf16[128,4096]{0,1:T(8,128)(2,1)} %slice_bitcast_fusion.8), channel_id=1, source_target_pairs={{0,16},{16,0},{1,17},{17,1},{2,18},{18,2},{3,19},{19,3},{4,20},{20... | collective-permute-start | bytes 3145736 | tf_op jit(solution)/shard_map/ppermute | solution.py:1154
  413.8 23.7 %collective-permute-start.12 = (bf16[512,4096]{1,0:T(8,128)(2,1)}, bf16[512,4096]{1,0:T(8,128)(2,1)}, u32[]{:S(2)}, u32[]{:S(2)}) collective-permute-start(bf16[512,4096]{1,0:T(8,128)(2,1)} %convolution_convert_fusion), channel_id=1, source_target_pairs={{0,4},{4,0},{8,12},{12,8},{1,5},{5,1},{9,13},{13,9},{2,6},{6,2},{1... | collective-permute-start | bytes 12582920 | tf_op jit(solution)/shard_map/ppermute | solution.py:1154
  422.0 207.4 %all-gather.13.cloned.1.call-start = ((), (), s32[]{:S(2)}) async-start(), calls=%async_computation.3 | async-start | bytes 5242880 | tf_op jit(solution)/shard_map/all_gather | solution.py:1223
  446.8 67.4 %collective-permute-start.15 = (bf16[2,128,4096]{2,1,0:T(8,128)(2,1)}, bf16[2,128,4096]{2,1,0:T(8,128)(2,1)}, u32[]{:S(2)}, u32[]{:S(2)}) collective-permute-start(bf16[2,128,4096]{2,1,0:T(8,128)(2,1)} %slice_bitcast_fusion), channel_id=1, source_target_pairs={{0,16},{16,0},{1,17},{17,1},{2,18},{18,2},{3,19},{19,3},{4,20},{20... | collective-permute-start | bytes 6291464 | tf_op jit(solution)/shard_map/ppermute | solution.py:1154
  451.7 62.5 %collective-permute-start.16 = (bf16[2,128,3072]{2,1,0:T(8,128)(2,1)}, bf16[2,128,3072]{2,1,0:T(8,128)(2,1)}, u32[]{:S(2)}, u32[]{:S(2)}) collective-permute-start(bf16[2,128,3072]{2,1,0:T(8,128)(2,1)} %slice_bitcast_fusion.4), channel_id=1, source_target_pairs={{0,8},{4,12},{8,0},{12,4},{1,9},{5,13},{9,1},{13,5},{2,10},{6,14},... | collective-permute-start | bytes 4718600 | tf_op jit(solution)/shard_map/ppermute | solution.py:1154
  471.1 43.1 %collective-permute-start.17 = (bf16[2,128,1024]{1,2,0:T(8,128)(2,1)}, bf16[2,128,1024]{1,2,0:T(8,128)(2,1)S(1)}, u32[]{:S(2)}, u32[]{:S(2)}) collective-permute-start(bf16[2,128,1024]{1,2,0:T(8,128)(2,1)} %slice_bitcast_fusion.12), channel_id=1, source_target_pairs={{0,8},{4,12},{8,0},{12,4},{1,9},{5,13},{9,1},{13,5},{2,10},{6,14},... | collective-permute-start | bytes 1572872 | tf_op jit(solution)/shard_map/ppermute | solution.py:1154
  481.1 32.2 %collective-permute-start.23 = (bf16[128,1024]{0,1:T(8,128)(2,1)}, bf16[128,1024]{0,1:T(8,128)(2,1)S(1)}, u32[]{:S(2)}, u32[]{:S(2)}) collective-permute-start(bf16[128,1024]{0,1:T(8,128)(2,1)} %get-tuple-element.170), channel_id=1, source_target_pairs={{3,2},{2,1},{1,0},{7,6},{6,5},{5,4},{11,10},{10,9},{9,8},{15,14},{... | collective-permute-start | bytes 786440 | tf_op jit(solution)/shard_map/ppermute | solution.py:1324
  482.4 30.9 %collective-permute-start.20 = (bf16[128,1024]{0,1:T(8,128)(2,1)}, bf16[128,1024]{0,1:T(8,128)(2,1)S(1)}, u32[]{:S(2)}, u32[]{:S(2)}) collective-permute-start(bf16[128,1024]{0,1:T(8,128)(2,1)} %get-tuple-element.169), channel_id=1, source_target_pairs={{0,1},{1,2},{2,3},{4,5},{5,6},{6,7},{8,9},{9,10},{10,11},{12,13},{... | collective-permute-start | bytes 786440 | tf_op jit(solution)/shard_map/ppermute | solution.py:1324
  523.8 29.3 %collective-permute-start.31 = (bf16[128,3072]{1,0:T(8,128)(2,1)S(1)}, bf16[128,3072]{1,0:T(8,128)(2,1)S(1)}, u32[]{:S(2)}, u32[]{:S(2)}) collective-permute-start(bf16[128,3072]{1,0:T(8,128)(2,1)S(1)} %slice_bitcast_fusion.9), channel_id=1, source_target_pairs={{0,16},{16,0},{1,17},{17,1},{2,18},{18,2},{3,19},{19,3},{4,20},{20... | collective-permute-start | bytes 2359304 | tf_op jit(solution)/shard_map/ppermute | solution.py:1154
  548.5 24.7 %collective-permute-start.39 = (bf16[128,256]{0,1:T(8,128)(2,1)S(1)}, bf16[128,256]{0,1:T(8,128)(2,1)S(1)}, u32[]{:S(2)}, u32[]{:S(2)}) collective-permute-start(bf16[128,256]{0,1:T(8,128)(2,1)S(1)} %get-tuple-element.188), channel_id=1, source_target_pairs={{0,1},{4,5},{8,9},{12,13},{16,17},{20,21},{24,25},{28,29}} | collective-permute-start | bytes 196616 | tf_op jit(solution)/shard_map/ppermute | solution.py:1324
  (86 other events, 1150.9 us)
Sparse Core Ops, SparseCore 0:
  11.6 151.3 all-gather.14
  248.0 84.8 all-gather.6
  334.5 79.2 all-gather.8
  422.2 92.1 all-gather.10
  515.8 111.5 all-gather.12
